TPU v7x, 512 devices: a whole 4x4x16 slice. The times are simulated.
512 devices in a mesh: gx: 4 (over y), gy: 16 (over z), gz: 8 (over x, core).
Axes of the slice: x: 4, y: 4, z: 16, core: 2. Of those that a mesh axis runs over, the one named last changes fastest.
Arguments:
- state: float32 [3, 128, 640, 512], P(None, 'gz', 'gy', 'gx'), may hold values from -6 to 6
- right_side: float32 [3, 128, 640, 512], P(None, 'gz', 'gy', 'gx'), may hold values from -6 to 6
- permeability: bfloat16 [128, 640, 512], P('gz', 'gy', 'gx'), may hold values from 0.099609375 to 10
- pore_volume: bfloat16 [128, 640, 512], P('gz', 'gy', 'gx'), may hold values from 0.019897461 to 0.19921875
- facies: int32 [128], P('gz'), may hold values from 0 to 3
- storage_table: float32 [4, 3, 3], replicated, may hold values from -0.3 to 2, as said below
- coupling_table: float32 [4, 3, 3], replicated, may hold values from -0.3 to 2, as said below
Outputs:
- new_state: float32 [3, 128, 640, 512], P(None, 'gz', 'gy', 'gx')
- correction: float32 [640, 512], P('gy', 'gx')
Inputs may be any that keep to these rules, and one draw needn't show every extreme that they name: `storage_table`: each facies block has a diagonal of 1 to 2 and off-diagonal entries of magnitude at most 0.3. `coupling_table`: each facies block has a diagonal of 1 to 2 and off-diagonal entries of magnitude at most 0.3.
All inputs are finite; a program needn't handle non-finite values.
Results may differ from a plain program's by a relative error of at most 0.0003.
Values sent between devices are 32-bit elements; how exact they have to be, the bound alone decides.
No kernel may reach another device: no remote copies, remote signals or barrier semaphores. Data moves between devices by JAX's collectives and lax.ppermute only.
A program may use at most 64 MiB of HBM per device.

v0:
```python
import jax
import jax.numpy as jnp
from jax import lax
from jax.sharding import PartitionSpec as P

SWEEPS = 8


relax = 0.8


def extended(cells, sides, width):
    for axis, dim in sides:
        count = lax.axis_size(axis)
        ends = count - 1
        head = lax.slice_in_dim(cells, 0, width, axis=dim)
        tail = lax.slice_in_dim(cells, cells.shape[dim] - width, cells.shape[dim], axis=dim)
        cells = jnp.concatenate(
            [
                lax.ppermute(tail, axis, [(i, (i + 1) % count) for i in range(ends)]),
                cells,
                lax.ppermute(head, axis, [((i + 1) % count, i) for i in range(ends)]),
            ],
            axis=dim,
        )
    return cells


def layer_tables(facies, table):
    onehot = (facies[:, None] == jnp.arange(table.shape[0])[None, :]).astype(jnp.float32)
    return jnp.dot(onehot, table.reshape(table.shape[0], 9), precision=lax.Precision.HIGHEST)


def layer_coefficient(rows, row_index, column_index):
    return rows[:, 3 * row_index + column_index][:, None, None]


def neighbours(padded):
    return [
        padded[..., 2:, 1:-1, 1:-1],
        padded[..., :-2, 1:-1, 1:-1],
        padded[..., 1:-1, 2:, 1:-1],
        padded[..., 1:-1, :-2, 1:-1],
        padded[..., 1:-1, 1:-1, 2:],
        padded[..., 1:-1, 1:-1, :-2],
    ]


def face_weights(padded_perm):
    center = padded_perm[1:-1, 1:-1, 1:-1]
    return [2.0 * center * nearby / (center + nearby) for nearby in neighbours(padded_perm)]


def apply_operator(padded_state, weights, storage, storage_rows, coupling_rows):
    center = padded_state[:, 1:-1, 1:-1, 1:-1]
    fluxes = jnp.zeros_like(center)
    for weight, nearby in zip(weights, neighbours(padded_state)):
        fluxes = fluxes + weight[None] * (center - nearby)
    outputs = []
    for row_index in range(3):
        local = sum((layer_coefficient(storage_rows, row_index, k) * center[k] for k in range(3)))
        moved = sum((layer_coefficient(coupling_rows, row_index, k) * fluxes[k] for k in range(3)))
        outputs.append(storage * local + moved)
    return jnp.stack(outputs)


def coarse_planes(residual, weights, storage, storage_rows, coupling_rows):
    first_coupling = layer_coefficient(coupling_rows, 0, 0)
    first_storage = layer_coefficient(storage_rows, 0, 0)
    items = [residual[0], storage * first_storage] + [
        weights[k] * first_coupling for k in range(2, 6)
    ]
    return jnp.stack([jnp.sum(item, axis=0) for item in items])


def jacobi(field, bordered, planes):
    diagonal = planes[1] + planes[2] + planes[3] + planes[4] + planes[5]
    nearby = (
        planes[2] * bordered[2:, 1:-1]
        + planes[3] * bordered[:-2, 1:-1]
        + planes[4] * bordered[1:-1, 2:]
        + planes[5] * bordered[1:-1, :-2]
    )
    return field + relax * (planes[0] - diagonal * field + nearby) / diagonal


def block_solve(weights, storage, storage_rows, coupling_rows, residual):
    face_total = weights[0] + weights[1] + weights[2] + weights[3] + weights[4] + weights[5]
    entries = [
        [
            storage * layer_coefficient(storage_rows, r, c)
            + face_total * layer_coefficient(coupling_rows, r, c)
            for c in range(3)
        ]
        for r in range(3)
    ]

    def cofactor(r, c):
        return (
            entries[(r + 1) % 3][(c + 1) % 3] * entries[(r + 2) % 3][(c + 2) % 3]
            - entries[(r + 1) % 3][(c + 2) % 3] * entries[(r + 2) % 3][(c + 1) % 3]
        )

    factors = [[cofactor(r, c) for c in range(3)] for r in range(3)]
    determinant = (
        entries[0][0] * factors[0][0]
        + entries[0][1] * factors[0][1]
        + entries[0][2] * factors[0][2]
    )
    return jnp.stack(
        [
            (
                factors[0][r] * residual[0]
                + factors[1][r] * residual[1]
                + factors[2][r] * residual[2]
            )
            / determinant
            for r in range(3)
        ]
    )


def per_device(state, right_side, permeability, pore_volume, facies, storage_table, coupling_table):
    perm_wide = permeability.astype(jnp.float32)
    storage = pore_volume.astype(jnp.float32)
    storage_rows = layer_tables(facies, storage_table)
    coupling_rows = layer_tables(facies, coupling_table)
    stacked = jnp.concatenate([state, perm_wide[None]], axis=0)
    padded = extended(stacked, (("gz", 1), ("gy", 2), ("gx", 3)), 1)
    weights = face_weights(padded[3])
    residual = right_side - apply_operator(
        padded[:3], weights, storage, storage_rows, coupling_rows
    )
    planes = coarse_planes(residual, weights, storage, storage_rows, coupling_rows)
    totals = lax.psum(planes, "gz")
    correction = jnp.zeros(totals.shape[1:], jnp.float32)
    for repeat_index in range(SWEEPS):
        bordered = extended(correction, (("gy", 0), ("gx", 1)), 1)
        correction = jacobi(correction, bordered, totals)
    state_one = state.at[0].add(correction[None])
    padded_again = extended(state_one, (("gz", 1), ("gy", 2), ("gx", 3)), 1)
    later_residual = right_side - apply_operator(
        padded_again, weights, storage, storage_rows, coupling_rows
    )
    new_state = state_one + block_solve(
        weights, storage, storage_rows, coupling_rows, later_residual
    )
    return (new_state, correction)


def solution(mesh):
    return jax.shard_map(
        per_device,
        mesh=mesh,
        in_specs=(
            P(None, "gz", "gy", "gx"),
            P(None, "gz", "gy", "gx"),
            P("gz", "gy", "gx"),
            P("gz", "gy", "gx"),
            P("gz"),
            P(),
            P(),
        ),
        out_specs=(P(None, "gz", "gy", "gx"), P("gy", "gx")),
        check_vma=False,
    )
```

profile of v0, /device:TPU:154, one launch (start us, length us, event | category | flops | bytes accessed | tf_op | source)
XLA Modules:
  0.0 306.7 jit_solution(5272867238131126008)
XLA Ops:
  9.4 3.8 %collective-permute-start.7 = (f32[1,128]{1,0:T(1,128)S(1)}, f32[1,128]{1,0:T(1,128)S(1)}, u32[]{:S(2)}, u32[]{:S(2)}) collective-permute-start(f32[1,128]{1,0:T(1,128)S(1)} %broadcast.56), channel_id=1, source_target_pairs={{0,8},{8,16},{16,24},{24,32},{32,40},{40,48},{48,56},{56,64},{64,7... | collective-permute-start | bytes 1544 | tf_op jit(solution)/shard_map/ppermute | solution.py:20
  17.0 3.6 %collective-permute-start.1 = (f32[4,1,40,128]{3,2,1,0:T(8,128)S(1)}, f32[4,1,40,128]{3,2,1,0:T(8,128)S(1)}, u32[]{:S(2)}, u32[]{:S(2)}) collective-permute-start(f32[4,1,40,128]{3,2,1,0:T(8,128)S(1)} %get-tuple-element.39), channel_id=1, source_target_pairs={{1,0},{2,1},{3,2},{4,3},{5,4},{6,5},{7,6},{9,8},{10,9},{11,10},{12... | collective-permute-start | bytes 245768 | tf_op jit(solution)/shard_map/ppermute | solution.py:22
  22.8 3.8 %collective-permute-start.2 = (f32[4,18,1,128]{3,0,2,1:T(4,128)S(1)}, f32[4,18,1,128]{3,0,2,1:T(4,128)S(1)}, u32[]{:S(2)}, u32[]{:S(2)}) collective-permute-start(f32[4,18,1,128]{3,0,2,1:T(4,128)S(1)} %copy.276), channel_id=1, source_target_pairs={{0,8},{8,16},{16,24},{24,32},{32,40},{40,48},{48,56},{56,64},{64,7... | collective-permute-start | bytes 110600 | tf_op jit(solution)/shard_map/ppermute | solution.py:20
  26.6 3.2 %collective-permute-start.3 = (f32[4,18,1,128]{3,0,2,1:T(4,128)S(1)}, f32[4,18,1,128]{3,0,2,1:T(4,128)S(1)}, u32[]{:S(2)}, u32[]{:S(2)}) collective-permute-start(f32[4,18,1,128]{3,0,2,1:T(4,128)S(1)} %copy.277), channel_id=1, source_target_pairs={{8,0},{16,8},{24,16},{32,24},{40,32},{48,40},{56,48},{64,56},{72,6... | collective-permute-start | bytes 110600 | tf_op jit(solution)/shard_map/ppermute | solution.py:22
  38.7 4.5 %collective-permute-start.5 = (f32[4,18,42,1]{2,0,3,1:T(4,128)S(1)}, f32[4,18,42,1]{2,0,3,1:T(4,128)S(1)}, u32[]{:S(2)}, u32[]{:S(2)}) collective-permute-start(f32[4,18,42,1]{2,0,3,1:T(4,128)S(1)} %copy.247), channel_id=1, source_target_pairs={{128,0},{256,128},{384,256},{129,1},{257,129},{385,257},{130,2},{2... | collective-permute-start | bytes 36296 | tf_op jit(solution)/shard_map/ppermute | solution.py:22
  49.8 3.3 %fusion.19 = f32[3,16,40,128]{3,2,1,0:T(8,128)S(1)} fusion(f32[3,16,40,128]{3,2,1,0:T(8,128)S(1)} %copy-done, f32[4,18,42,1]{3,2,1,0:T(8,128)S(1)} %copy.248, f32[4,18,1,128]{3,2,1,0:T(1,128)S(1)} %copy.245, f32[4,18,1,128]{3,2,1,0:T(1,128)S(1)} %copy.244, f32[4,1,40,128]{3,2,1,0:T(8,128)S(1)} %collective-permute-done.1, ...), kind=kLoop, calls=%fused_computation.57 | loop fusion | flops 10076160 | bytes 4521600 | tf_op jit(solution)/shard_map/add | solution.py:58
  57.4 4.2 %collective-permute-start.8 = (f32[42,1]{1,0:T(8,128)S(1)}, f32[42,1]{1,0:T(8,128)S(1)}, u32[]{:S(2)}, u32[]{:S(2)}) collective-permute-start(f32[42,1]{1,0:T(8,128)S(1)} %get-tuple-element.70), channel_id=1, source_target_pairs={{128,0},{256,128},{384,256},{129,1},{257,129},{385,257},{130,2},{2... | collective-permute-start | bytes 512 | tf_op jit(solution)/shard_map/ppermute | solution.py:22
  63.1 4.2 %collective-permute-done.9 = f32[42,1]{1,0:T(8,128)S(1)} collective-permute-done((f32[42,1]{1,0:T(8,128)S(1)}, f32[42,1]{1,0:T(8,128)S(1)}, u32[]{:S(2)}, u32[]{:S(2)}) %collective-permute-start.9) | collective-permute-done | bytes 200 | tf_op jit(solution)/shard_map/ppermute | solution.py:20
  67.3 67.1 %all-reduce.4.cloned.1.call-done = f32[6,40,128]{2,1,0:T(8,128)} async-done(((f32[6,40,128]{2,1,0:T(8,128)}), f32[6,40,128]{2,1,0:T(8,128)}) %all-reduce.4.cloned.1.call-update) | async-done | bytes 122896 | tf_op jit(solution)/shard_map/psum | solution.py:135
  137.8 3.5 %collective-permute-start.11 = (f32[1,128]{1,0:T(1,128)S(1)}, f32[1,128]{1,0:T(1,128)S(1)}, u32[]{:S(2)}, u32[]{:S(2)}) collective-permute-start(f32[1,128]{1,0:T(1,128)S(1)} %get-tuple-element.84), channel_id=1, source_target_pairs={{0,8},{8,16},{16,24},{24,32},{32,40},{40,48},{48,56},{56,64},{64,7... | collective-permute-start | bytes 1544 | tf_op jit(solution)/shard_map/ppermute | solution.py:20
  141.3 3.2 %collective-permute-done.11 = f32[1,128]{1,0:T(1,128)S(1)} collective-permute-done((f32[1,128]{1,0:T(1,128)S(1)}, f32[1,128]{1,0:T(1,128)S(1)}, u32[]{:S(2)}, u32[]{:S(2)}) %collective-permute-start.11) | collective-permute-done | bytes 544 | tf_op jit(solution)/shard_map/ppermute | solution.py:20
  144.5 2.7 collective-permute-start.12
  148.7 4.2 %collective-permute-done.13 = f32[42,1]{1,0:T(8,128)S(1)} collective-permute-done((f32[42,1]{1,0:T(8,128)S(1)}, f32[42,1]{1,0:T(8,128)S(1)}, u32[]{:S(2)}, u32[]{:S(2)}) %collective-permute-start.13) | collective-permute-done | bytes 200 | tf_op jit(solution)/shard_map/ppermute | solution.py:20
  155.8 3.9 %collective-permute-start.15 = (f32[1,128]{1,0:T(1,128)S(1)}, f32[1,128]{1,0:T(1,128)S(1)}, u32[]{:S(2)}, u32[]{:S(2)}) collective-permute-start(f32[1,128]{1,0:T(1,128)S(1)} %get-tuple-element.82), channel_id=1, source_target_pairs={{0,8},{8,16},{16,24},{24,32},{32,40},{40,48},{48,56},{56,64},{64,7... | collective-permute-start | bytes 1544 | tf_op jit(solution)/shard_map/ppermute | solution.py:20
  159.8 2.7 collective-permute-done.15
  166.5 4.2 %collective-permute-done.17 = f32[42,1]{1,0:T(8,128)S(1)} collective-permute-done((f32[42,1]{1,0:T(8,128)S(1)}, f32[42,1]{1,0:T(8,128)S(1)}, u32[]{:S(2)}, u32[]{:S(2)}) %collective-permute-start.17) | collective-permute-done | bytes 200 | tf_op jit(solution)/shard_map/ppermute | solution.py:20
  173.6 3.9 %collective-permute-start.19 = (f32[1,128]{1,0:T(1,128)S(1)}, f32[1,128]{1,0:T(1,128)S(1)}, u32[]{:S(2)}, u32[]{:S(2)}) collective-permute-start(f32[1,128]{1,0:T(1,128)S(1)} %get-tuple-element.80), channel_id=1, source_target_pairs={{0,8},{8,16},{16,24},{24,32},{32,40},{40,48},{48,56},{56,64},{64,7... | collective-permute-start | bytes 1544 | tf_op jit(solution)/shard_map/ppermute | solution.py:20
  177.5 2.7 collective-permute-done.19
  184.2 4.2 %collective-permute-done.21 = f32[42,1]{1,0:T(8,128)S(1)} collective-permute-done((f32[42,1]{1,0:T(8,128)S(1)}, f32[42,1]{1,0:T(8,128)S(1)}, u32[]{:S(2)}, u32[]{:S(2)}) %collective-permute-start.21) | collective-permute-done | bytes 200 | tf_op jit(solution)/shard_map/ppermute | solution.py:20
  191.5 3.9 %collective-permute-start.23 = (f32[1,128]{1,0:T(1,128)S(1)}, f32[1,128]{1,0:T(1,128)S(1)}, u32[]{:S(2)}, u32[]{:S(2)}) collective-permute-start(f32[1,128]{1,0:T(1,128)S(1)} %get-tuple-element.78), channel_id=1, source_target_pairs={{0,8},{8,16},{16,24},{24,32},{32,40},{40,48},{48,56},{56,64},{64,7... | collective-permute-start | bytes 1544 | tf_op jit(solution)/shard_map/ppermute | solution.py:20
  201.6 4.2 %collective-permute-done.25 = f32[42,1]{1,0:T(8,128)S(1)} collective-permute-done((f32[42,1]{1,0:T(8,128)S(1)}, f32[42,1]{1,0:T(8,128)S(1)}, u32[]{:S(2)}, u32[]{:S(2)}) %collective-permute-start.25) | collective-permute-done | bytes 200 | tf_op jit(solution)/shard_map/ppermute | solution.py:20
  208.7 3.9 %collective-permute-start.27 = (f32[1,128]{1,0:T(1,128)S(1)}, f32[1,128]{1,0:T(1,128)S(1)}, u32[]{:S(2)}, u32[]{:S(2)}) collective-permute-start(f32[1,128]{1,0:T(1,128)S(1)} %get-tuple-element.76), channel_id=1, source_target_pairs={{0,8},{8,16},{16,24},{24,32},{32,40},{40,48},{48,56},{56,64},{64,7... | collective-permute-start | bytes 1544 | tf_op jit(solution)/shard_map/ppermute | solution.py:20
  212.6 2.7 collective-permute-done.27
  218.8 4.2 %collective-permute-done.29 = f32[42,1]{1,0:T(8,128)S(1)} collective-permute-done((f32[42,1]{1,0:T(8,128)S(1)}, f32[42,1]{1,0:T(8,128)S(1)}, u32[]{:S(2)}, u32[]{:S(2)}) %collective-permute-start.29) | collective-permute-done | bytes 200 | tf_op jit(solution)/shard_map/ppermute | solution.py:20
  225.1 3.9 %collective-permute-start.31 = (f32[1,128]{1,0:T(1,128)S(1)}, f32[1,128]{1,0:T(1,128)S(1)}, u32[]{:S(2)}, u32[]{:S(2)}) collective-permute-start(f32[1,128]{1,0:T(1,128)S(1)} %get-tuple-element.74), channel_id=1, source_target_pairs={{0,8},{8,16},{16,24},{24,32},{32,40},{40,48},{48,56},{56,64},{64,7... | collective-permute-start | bytes 1544 | tf_op jit(solution)/shard_map/ppermute | solution.py:20
  235.3 4.2 %collective-permute-done.33 = f32[42,1]{1,0:T(8,128)S(1)} collective-permute-done((f32[42,1]{1,0:T(8,128)S(1)}, f32[42,1]{1,0:T(8,128)S(1)}, u32[]{:S(2)}, u32[]{:S(2)}) %collective-permute-start.33) | collective-permute-done | bytes 200 | tf_op jit(solution)/shard_map/ppermute | solution.py:20
  241.5 3.9 %collective-permute-start.35 = (f32[1,128]{1,0:T(1,128)S(1)}, f32[1,128]{1,0:T(1,128)S(1)}, u32[]{:S(2)}, u32[]{:S(2)}) collective-permute-start(f32[1,128]{1,0:T(1,128)S(1)} %get-tuple-element.72), channel_id=1, source_target_pairs={{0,8},{8,16},{16,24},{24,32},{32,40},{40,48},{48,56},{56,64},{64,7... | collective-permute-start | bytes 1544 | tf_op jit(solution)/shard_map/ppermute | solution.py:20
  251.8 4.2 %collective-permute-done.37 = f32[42,1]{1,0:T(8,128)S(1)} collective-permute-done((f32[42,1]{1,0:T(8,128)S(1)}, f32[42,1]{1,0:T(8,128)S(1)}, u32[]{:S(2)}, u32[]{:S(2)}) %collective-permute-start.37) | collective-permute-done | bytes 200 | tf_op jit(solution)/shard_map/ppermute | solution.py:20
  260.6 4.1 %collective-permute-done.39 = f32[3,1,40,128]{3,2,1,0:T(8,128)S(1)} collective-permute-done((f32[3,1,40,128]{3,2,1,0:T(8,128)S(1)}, f32[3,1,40,128]{3,2,1,0:T(8,128)S(1)}, u32[]{:S(2)}, u32[]{:S(2)}) %collective-permute-start.39) | collective-permute-done | bytes 61472 | tf_op jit(solution)/shard_map/ppermute | solution.py:20
  266.7 3.9 %collective-permute-start.41 = (f32[3,18,1,128]{3,2,1,0:T(1,128)S(1)}, f32[3,18,1,128]{3,2,1,0:T(1,128)S(1)}, u32[]{:S(2)}, u32[]{:S(2)}) collective-permute-start(f32[3,18,1,128]{3,2,1,0:T(1,128)S(1)} %get-tuple-element.40), channel_id=1, source_target_pairs={{0,8},{8,16},{16,24},{24,32},{32,40},{40,48},{48,56},{56,64},{64,7... | collective-permute-start | bytes 82952 | tf_op jit(solution)/shard_map/ppermute | solution.py:20
  270.6 3.0 collective-permute-done.41
  288.9 4.2 %fusion.2 = f32[3,16,40,128]{3,2,1,0:T(8,128)S(1)} fusion(f32[3,16,40,128]{3,2,1,0:T(8,128)S(1)} %add_dynamic-update-slice_fusion, f32[3,18,42,1]{3,2,1,0:T(8,128)} %copy.269, f32[3,18,1,128]{3,2,1,0:T(1,128)S(1)} %collective-permute-done.40, f32[3,18,1,128]{3,2,1,0:T(1,128)S(1)} %collective-permute-done.41, ...), kind=kLoop, calls=%fused_computation.22 | loop fusion | flops 8601600 | bytes 4128480 | tf_op jit(solution)/shard_map/add | solution.py:58
  (259 shorter events, 107.6 us)
Async XLA Ops:
  7.2 127.2 %all-reduce.4.cloned.1.call-start = ((), (), s32[]{:S(2)}) async-start(), calls=%async_computation | async-start | bytes 245760 | tf_op jit(solution)/shard_map/psum | solution.py:135
  7.3 36.0 %collective-permute-start.6 = (f32[1,128]{1,0:T(1,128)S(1)}, f32[1,128]{1,0:T(1,128)S(1)}, u32[]{:S(2)}, u32[]{:S(2)}) collective-permute-start(f32[1,128]{1,0:T(1,128)S(1)} %broadcast.56), channel_id=1, source_target_pairs={{8,0},{16,8},{24,16},{32,24},{40,32},{48,40},{56,48},{64,56},{72,6... | collective-permute-start | bytes 1544 | tf_op jit(solution)/shard_map/ppermute | solution.py:22
  9.4 33.9 %collective-permute-start.7 = (f32[1,128]{1,0:T(1,128)S(1)}, f32[1,128]{1,0:T(1,128)S(1)}, u32[]{:S(2)}, u32[]{:S(2)}) collective-permute-start(f32[1,128]{1,0:T(1,128)S(1)} %broadcast.56), channel_id=1, source_target_pairs={{0,8},{8,16},{16,24},{24,32},{32,40},{40,48},{48,56},{56,64},{64,7... | collective-permute-start | bytes 1544 | tf_op jit(solution)/shard_map/ppermute | solution.py:20
  15.1 6.2 %collective-permute-start = (f32[4,1,40,128]{3,2,1,0:T(8,128)S(1)}, f32[4,1,40,128]{3,2,1,0:T(8,128)S(1)}, u32[]{:S(2)}, u32[]{:S(2)}) collective-permute-start(f32[4,1,40,128]{3,2,1,0:T(8,128)S(1)} %get-tuple-element.38), channel_id=1, source_target_pairs={{0,1},{1,2},{2,3},{3,4},{4,5},{5,6},{6,7},{8,9},{9,10},{10,11},{11... | collective-permute-start | bytes 245768 | tf_op jit(solution)/shard_map/ppermute | solution.py:20
  22.8 7.8 %collective-permute-start.2 = (f32[4,18,1,128]{3,0,2,1:T(4,128)S(1)}, f32[4,18,1,128]{3,0,2,1:T(4,128)S(1)}, u32[]{:S(2)}, u32[]{:S(2)}) collective-permute-start(f32[4,18,1,128]{3,0,2,1:T(4,128)S(1)} %copy.276), channel_id=1, source_target_pairs={{0,8},{8,16},{16,24},{24,32},{32,40},{40,48},{48,56},{56,64},{64,7... | collective-permute-start | bytes 110600 | tf_op jit(solution)/shard_map/ppermute | solution.py:20
  26.6 5.9 %collective-permute-start.3 = (f32[4,18,1,128]{3,0,2,1:T(4,128)S(1)}, f32[4,18,1,128]{3,0,2,1:T(4,128)S(1)}, u32[]{:S(2)}, u32[]{:S(2)}) collective-permute-start(f32[4,18,1,128]{3,0,2,1:T(4,128)S(1)} %copy.277), channel_id=1, source_target_pairs={{8,0},{16,8},{24,16},{32,24},{40,32},{48,40},{56,48},{64,56},{72,6... | collective-permute-start | bytes 110600 | tf_op jit(solution)/shard_map/ppermute | solution.py:22
  36.7 6.6 %collective-permute-start.4 = (f32[4,18,42,1]{2,0,3,1:T(4,128)S(1)}, f32[4,18,42,1]{2,0,3,1:T(4,128)S(1)}, u32[]{:S(2)}, u32[]{:S(2)}) collective-permute-start(f32[4,18,42,1]{2,0,3,1:T(4,128)S(1)} %copy.246), channel_id=1, source_target_pairs={{0,128},{128,256},{256,384},{1,129},{129,257},{257,385},{2,130},{1... | collective-permute-start | bytes 36296 | tf_op jit(solution)/shard_map/ppermute | solution.py:20
  38.7 6.2 %collective-permute-start.5 = (f32[4,18,42,1]{2,0,3,1:T(4,128)S(1)}, f32[4,18,42,1]{2,0,3,1:T(4,128)S(1)}, u32[]{:S(2)}, u32[]{:S(2)}) collective-permute-start(f32[4,18,42,1]{2,0,3,1:T(4,128)S(1)} %copy.247), channel_id=1, source_target_pairs={{128,0},{256,128},{384,256},{129,1},{257,129},{385,257},{130,2},{2... | collective-permute-start | bytes 36296 | tf_op jit(solution)/shard_map/ppermute | solution.py:22
  57.4 5.7 %collective-permute-start.8 = (f32[42,1]{1,0:T(8,128)S(1)}, f32[42,1]{1,0:T(8,128)S(1)}, u32[]{:S(2)}, u32[]{:S(2)}) collective-permute-start(f32[42,1]{1,0:T(8,128)S(1)} %get-tuple-element.70), channel_id=1, source_target_pairs={{128,0},{256,128},{384,256},{129,1},{257,129},{385,257},{130,2},{2... | collective-permute-start | bytes 512 | tf_op jit(solution)/shard_map/ppermute | solution.py:22
  61.6 5.7 %collective-permute-start.9 = (f32[42,1]{1,0:T(8,128)S(1)}, f32[42,1]{1,0:T(8,128)S(1)}, u32[]{:S(2)}, u32[]{:S(2)}) collective-permute-start(f32[42,1]{1,0:T(8,128)S(1)} %get-tuple-element.71), channel_id=1, source_target_pairs={{0,128},{128,256},{256,384},{1,129},{129,257},{257,385},{2,130},{1... | collective-permute-start | bytes 512 | tf_op jit(solution)/shard_map/ppermute | solution.py:20
  135.4 5.9 %collective-permute-start.10 = (f32[1,128]{1,0:T(1,128)S(1)}, f32[1,128]{1,0:T(1,128)S(1)}, u32[]{:S(2)}, u32[]{:S(2)}) collective-permute-start(f32[1,128]{1,0:T(1,128)S(1)} %get-tuple-element.85), channel_id=1, source_target_pairs={{8,0},{16,8},{24,16},{32,24},{40,32},{48,40},{56,48},{64,56},{72,6... | collective-permute-start | bytes 1544 | tf_op jit(solution)/shard_map/ppermute | solution.py:22
  137.8 6.6 %collective-permute-start.11 = (f32[1,128]{1,0:T(1,128)S(1)}, f32[1,128]{1,0:T(1,128)S(1)}, u32[]{:S(2)}, u32[]{:S(2)}) collective-permute-start(f32[1,128]{1,0:T(1,128)S(1)} %get-tuple-element.84), channel_id=1, source_target_pairs={{0,8},{8,16},{16,24},{24,32},{32,40},{40,48},{48,56},{56,64},{64,7... | collective-permute-start | bytes 1544 | tf_op jit(solution)/shard_map/ppermute | solution.py:20
  147.2 5.7 %collective-permute-start.13 = (f32[42,1]{1,0:T(8,128)S(1)}, f32[42,1]{1,0:T(8,128)S(1)}, u32[]{:S(2)}, u32[]{:S(2)}) collective-permute-start(f32[42,1]{1,0:T(8,128)S(1)} %get-tuple-element.69), channel_id=1, source_target_pairs={{0,128},{128,256},{256,384},{1,129},{129,257},{257,385},{2,130},{1... | collective-permute-start | bytes 512 | tf_op jit(solution)/shard_map/ppermute | solution.py:20
  153.9 5.9 %collective-permute-start.14 = (f32[1,128]{1,0:T(1,128)S(1)}, f32[1,128]{1,0:T(1,128)S(1)}, u32[]{:S(2)}, u32[]{:S(2)}) collective-permute-start(f32[1,128]{1,0:T(1,128)S(1)} %get-tuple-element.83), channel_id=1, source_target_pairs={{8,0},{16,8},{24,16},{32,24},{40,32},{48,40},{56,48},{64,56},{72,6... | collective-permute-start | bytes 1544 | tf_op jit(solution)/shard_map/ppermute | solution.py:22
  155.8 6.6 %collective-permute-start.15 = (f32[1,128]{1,0:T(1,128)S(1)}, f32[1,128]{1,0:T(1,128)S(1)}, u32[]{:S(2)}, u32[]{:S(2)}) collective-permute-start(f32[1,128]{1,0:T(1,128)S(1)} %get-tuple-element.82), channel_id=1, source_target_pairs={{0,8},{8,16},{16,24},{24,32},{32,40},{40,48},{48,56},{56,64},{64,7... | collective-permute-start | bytes 1544 | tf_op jit(solution)/shard_map/ppermute | solution.py:20
  171.6 5.9 %collective-permute-start.18 = (f32[1,128]{1,0:T(1,128)S(1)}, f32[1,128]{1,0:T(1,128)S(1)}, u32[]{:S(2)}, u32[]{:S(2)}) collective-permute-start(f32[1,128]{1,0:T(1,128)S(1)} %get-tuple-element.81), channel_id=1, source_target_pairs={{8,0},{16,8},{24,16},{32,24},{40,32},{48,40},{56,48},{64,56},{72,6... | collective-permute-start | bytes 1544 | tf_op jit(solution)/shard_map/ppermute | solution.py:22
  173.6 6.6 %collective-permute-start.19 = (f32[1,128]{1,0:T(1,128)S(1)}, f32[1,128]{1,0:T(1,128)S(1)}, u32[]{:S(2)}, u32[]{:S(2)}) collective-permute-start(f32[1,128]{1,0:T(1,128)S(1)} %get-tuple-element.80), channel_id=1, source_target_pairs={{0,8},{8,16},{16,24},{24,32},{32,40},{40,48},{48,56},{56,64},{64,7... | collective-permute-start | bytes 1544 | tf_op jit(solution)/shard_map/ppermute | solution.py:20
  182.7 5.7 %collective-permute-start.21 = (f32[42,1]{1,0:T(8,128)S(1)}, f32[42,1]{1,0:T(8,128)S(1)}, u32[]{:S(2)}, u32[]{:S(2)}) collective-permute-start(f32[42,1]{1,0:T(8,128)S(1)} %get-tuple-element.65), channel_id=1, source_target_pairs={{0,128},{128,256},{256,384},{1,129},{129,257},{257,385},{2,130},{1... | collective-permute-start | bytes 512 | tf_op jit(solution)/shard_map/ppermute | solution.py:20
  189.4 6.0 %collective-permute-start.22 = (f32[1,128]{1,0:T(1,128)S(1)}, f32[1,128]{1,0:T(1,128)S(1)}, u32[]{:S(2)}, u32[]{:S(2)}) collective-permute-start(f32[1,128]{1,0:T(1,128)S(1)} %get-tuple-element.79), channel_id=1, source_target_pairs={{8,0},{16,8},{24,16},{32,24},{40,32},{48,40},{56,48},{64,56},{72,6... | collective-permute-start | bytes 1544 | tf_op jit(solution)/shard_map/ppermute | solution.py:22
  191.5 6.6 %collective-permute-start.23 = (f32[1,128]{1,0:T(1,128)S(1)}, f32[1,128]{1,0:T(1,128)S(1)}, u32[]{:S(2)}, u32[]{:S(2)}) collective-permute-start(f32[1,128]{1,0:T(1,128)S(1)} %get-tuple-element.78), channel_id=1, source_target_pairs={{0,8},{8,16},{16,24},{24,32},{32,40},{40,48},{48,56},{56,64},{64,7... | collective-permute-start | bytes 1544 | tf_op jit(solution)/shard_map/ppermute | solution.py:20
  200.1 5.7 %collective-permute-start.25 = (f32[42,1]{1,0:T(8,128)S(1)}, f32[42,1]{1,0:T(8,128)S(1)}, u32[]{:S(2)}, u32[]{:S(2)}) collective-permute-start(f32[42,1]{1,0:T(8,128)S(1)} %get-tuple-element.63), channel_id=1, source_target_pairs={{0,128},{128,256},{256,384},{1,129},{129,257},{257,385},{2,130},{1... | collective-permute-start | bytes 512 | tf_op jit(solution)/shard_map/ppermute | solution.py:20
  206.8 5.9 %collective-permute-start.26 = (f32[1,128]{1,0:T(1,128)S(1)}, f32[1,128]{1,0:T(1,128)S(1)}, u32[]{:S(2)}, u32[]{:S(2)}) collective-permute-start(f32[1,128]{1,0:T(1,128)S(1)} %get-tuple-element.77), channel_id=1, source_target_pairs={{8,0},{16,8},{24,16},{32,24},{40,32},{48,40},{56,48},{64,56},{72,6... | collective-permute-start | bytes 1544 | tf_op jit(solution)/shard_map/ppermute | solution.py:22
  208.7 6.6 %collective-permute-start.27 = (f32[1,128]{1,0:T(1,128)S(1)}, f32[1,128]{1,0:T(1,128)S(1)}, u32[]{:S(2)}, u32[]{:S(2)}) collective-permute-start(f32[1,128]{1,0:T(1,128)S(1)} %get-tuple-element.76), channel_id=1, source_target_pairs={{0,8},{8,16},{16,24},{24,32},{32,40},{40,48},{48,56},{56,64},{64,7... | collective-permute-start | bytes 1544 | tf_op jit(solution)/shard_map/ppermute | solution.py:20
  223.2 5.9 %collective-permute-start.30 = (f32[1,128]{1,0:T(1,128)S(1)}, f32[1,128]{1,0:T(1,128)S(1)}, u32[]{:S(2)}, u32[]{:S(2)}) collective-permute-start(f32[1,128]{1,0:T(1,128)S(1)} %get-tuple-element.75), channel_id=1, source_target_pairs={{8,0},{16,8},{24,16},{32,24},{40,32},{48,40},{56,48},{64,56},{72,6... | collective-permute-start | bytes 1544 | tf_op jit(solution)/shard_map/ppermute | solution.py:22
  225.1 6.6 %collective-permute-start.31 = (f32[1,128]{1,0:T(1,128)S(1)}, f32[1,128]{1,0:T(1,128)S(1)}, u32[]{:S(2)}, u32[]{:S(2)}) collective-permute-start(f32[1,128]{1,0:T(1,128)S(1)} %get-tuple-element.74), channel_id=1, source_target_pairs={{0,8},{8,16},{16,24},{24,32},{32,40},{40,48},{48,56},{56,64},{64,7... | collective-permute-start | bytes 1544 | tf_op jit(solution)/shard_map/ppermute | solution.py:20
  239.6 5.9 %collective-permute-start.34 = (f32[1,128]{1,0:T(1,128)S(1)}, f32[1,128]{1,0:T(1,128)S(1)}, u32[]{:S(2)}, u32[]{:S(2)}) collective-permute-start(f32[1,128]{1,0:T(1,128)S(1)} %get-tuple-element.73), channel_id=1, source_target_pairs={{8,0},{16,8},{24,16},{32,24},{40,32},{48,40},{56,48},{64,56},{72,6... | collective-permute-start | bytes 1544 | tf_op jit(solution)/shard_map/ppermute | solution.py:22
  241.5 6.6 %collective-permute-start.35 = (f32[1,128]{1,0:T(1,128)S(1)}, f32[1,128]{1,0:T(1,128)S(1)}, u32[]{:S(2)}, u32[]{:S(2)}) collective-permute-start(f32[1,128]{1,0:T(1,128)S(1)} %get-tuple-element.72), channel_id=1, source_target_pairs={{0,8},{8,16},{16,24},{24,32},{32,40},{40,48},{48,56},{56,64},{64,7... | collective-permute-start | bytes 1544 | tf_op jit(solution)/shard_map/ppermute | solution.py:20
  250.3 5.7 %collective-permute-start.37 = (f32[42,1]{1,0:T(8,128)S(1)}, f32[42,1]{1,0:T(8,128)S(1)}, u32[]{:S(2)}, u32[]{:S(2)}) collective-permute-start(f32[42,1]{1,0:T(8,128)S(1)} %get-tuple-element.57), channel_id=1, source_target_pairs={{0,128},{128,256},{256,384},{1,129},{129,257},{257,385},{2,130},{1... | collective-permute-start | bytes 512 | tf_op jit(solution)/shard_map/ppermute | solution.py:20
  258.2 6.6 %collective-permute-start.39 = (f32[3,1,40,128]{3,2,1,0:T(8,128)S(1)}, f32[3,1,40,128]{3,2,1,0:T(8,128)S(1)}, u32[]{:S(2)}, u32[]{:S(2)}) collective-permute-start(f32[3,1,40,128]{3,2,1,0:T(8,128)S(1)} %get-tuple-element.42), channel_id=1, source_target_pairs={{0,1},{1,2},{2,3},{3,4},{4,5},{5,6},{6,7},{8,9},{9,10},{10,11},{11... | collective-permute-start | bytes 184328 | tf_op jit(solution)/shard_map/ppermute | solution.py:20
  264.8 5.9 %collective-permute-start.40 = (f32[3,18,1,128]{3,2,1,0:T(1,128)S(1)}, f32[3,18,1,128]{3,2,1,0:T(1,128)S(1)}, u32[]{:S(2)}, u32[]{:S(2)}) collective-permute-start(f32[3,18,1,128]{3,2,1,0:T(1,128)S(1)} %get-tuple-element.41), channel_id=1, source_target_pairs={{8,0},{16,8},{24,16},{32,24},{40,32},{48,40},{56,48},{64,56},{72,6... | collective-permute-start | bytes 82952 | tf_op jit(solution)/shard_map/ppermute | solution.py:22
  266.7 7.0 %collective-permute-start.41 = (f32[3,18,1,128]{3,2,1,0:T(1,128)S(1)}, f32[3,18,1,128]{3,2,1,0:T(1,128)S(1)}, u32[]{:S(2)}, u32[]{:S(2)}) collective-permute-start(f32[3,18,1,128]{3,2,1,0:T(1,128)S(1)} %get-tuple-element.40), channel_id=1, source_target_pairs={{0,8},{8,16},{16,24},{24,32},{32,40},{40,48},{48,56},{56,64},{64,7... | collective-permute-start | bytes 82952 | tf_op jit(solution)/shard_map/ppermute | solution.py:20
  281.5 5.8 %collective-permute-start.43 = (f32[3,18,42,1]{2,3,1,0:T(1,128)S(1)}, f32[3,18,42,1]{2,3,1,0:T(1,128)S(1)}, u32[]{:S(2)}, u32[]{:S(2)}) collective-permute-start(f32[3,18,42,1]{2,3,1,0:T(1,128)S(1)} %copy.279), channel_id=1, source_target_pairs={{0,128},{128,256},{256,384},{1,129},{129,257},{257,385},{2,130},{1... | collective-permute-start | bytes 27224 | tf_op jit(solution)/shard_map/ppermute | solution.py:20
  (65 other events, 579.7 us)
Sparse Core Ops, SparseCore 0:
  57.4 76.9 all-reduce.3
where the time goes:
time: 309 us; the launch traced here: 307 us
  waiting for transfers between devices  136 us (44%)
  starting transfers between devices  109 us (35%)
  other arithmetic  23.4 us (8%)
  local copies, waits for them, and re-layouts  22.7 us (7%)
  between operations  15.3 us (5%)
    psum x1, waiting for transfers between devices, per_device(): totals = lax.psum(planes, 'gz')  67.1 us
    ppermute x22, waiting for transfers between devices, extended(): lax.ppermute(tail, axis, [(i, (i + 1) % count) for i in range(ends)])  62.9 us
    ppermute x22, starting transfers between devices, extended(): lax.ppermute(tail, axis, [(i, (i + 1) % count) for i in range(ends)])  56 us
    ppermute x22, starting transfers between devices, extended(): lax.ppermute(head, axis, [((i + 1) % count, i) for i in range(ends)])  53 us
    unnamed x121, local copies, waits for them, and re-layouts  8.34 us
    add x2, other arithmetic, apply_operator(): fluxes = fluxes + weight[None] * (center - nearby)  7.53 us
  transfers between devices with their start and end apart: 45, of which 30 were waited for; matrix products, arithmetic and copies ran while one was open for 4% of the time, Pallas kernels for 0%

commit v1 on v0

v1 whole, which is shorter than its diff:
```python
import jax
import jax.numpy as jnp
from jax import lax
from jax.experimental import pallas as pl
from jax.experimental.pallas import tpu as pltpu
from jax.sharding import PartitionSpec as P

SWEEPS = 8
RELAX = 0.8
DIRECTIONS = ((-1, 0), (1, 0), (0, -1), (0, 1), (-1, -1), (1, 1), (-1, 1), (1, -1))
F32 = jnp.float32
PARAMS = pltpu.CompilerParams(vmem_limit_bytes=24 * 2**20)


def vmem(count):
    return [pl.BlockSpec(memory_space=pltpu.VMEM)] * count


def smem(count):
    return [pl.BlockSpec(memory_space=pltpu.SMEM)] * count


def lane_index(shape):
    return lax.broadcasted_iota(jnp.int32, shape, len(shape) - 1)


def row_index(shape):
    return lax.broadcasted_iota(jnp.int32, shape, len(shape) - 2)


def faces_kernel(state, perm, zlo, zhi, ylo, yhi, xlo, xhi):
    depth, height, width = perm.shape
    tiles = height // 8
    lanes = lane_index((8, 128))

    def layer(z, columns):
        columns = list(columns)
        for c in range(4):
            cells = state[c, z] if c < 3 else perm[z].astype(F32)
            ylo[c, pl.ds(z, 1), :] = cells[0:1]
            yhi[c, pl.ds(z, 1), :] = cells[height - 1 : height]
            for t in range(tiles):
                here = lanes == z * tiles + t
                block = cells[8 * t : 8 * t + 8]
                first = jnp.broadcast_to(block[:, 0:1], (8, 128))
                last = jnp.broadcast_to(block[:, width - 1 : width], (8, 128))
                columns[c] = jnp.where(here, first, columns[c])
                columns[4 + c] = jnp.where(here, last, columns[4 + c])
        return tuple(columns)

    columns = lax.fori_loop(0, depth, layer, (jnp.zeros((8, 128), F32),) * 8)
    for c in range(4):
        xlo[c] = columns[c]
        xhi[c] = columns[4 + c]
        zlo[c] = state[c, 0] if c < 3 else perm[0].astype(F32)
        zhi[c] = state[c, depth - 1] if c < 3 else perm[depth - 1].astype(F32)


def inverse(value):
    return 1.0 / value


def mean_weight(a, b):
    return 2.0 * a * b * inverse(a + b)


def cells_kernel(
    facies, storage_table, coupling_table,
    state, right, perm, pore, zlo, zhi, ylo, yhi, xlo, xhi,
    base, gain, face, message,
    sums,
):
    depth, height, width = perm.shape
    tiles = height // 8
    rows = row_index((height, width))
    lanes = lane_index((height, width))
    sums[...] = jnp.zeros_like(sums)

    def layer(z, carry):
        fid = facies[z]
        m = [[storage_table[fid, 3 * i + j] for j in range(3)] for i in range(3)]
        k = [[coupling_table[fid, 3 * i + j] for j in range(3)] for i in range(3)]
        below = jnp.minimum(z + 1, depth - 1)
        above = jnp.maximum(z - 1, 0)
        shift = lax.rem(128 - tiles * z, 128)

        def values(c):
            if c < 3:
                here, down, up = state[c, z], state[c, below], state[c, above]
            else:
                here, down, up = (perm[i].astype(F32) for i in (z, below, above))
            down = jnp.where(z == depth - 1, zhi[c], down)
            up = jnp.where(z == 0, zlo[c], up)
            south = pltpu.roll(here, height - 1, 0)
            south = jnp.where(rows == height - 1, yhi[c, pl.ds(z, 1), :], south)
            north = pltpu.roll(here, 1, 0)
            north = jnp.where(rows == 0, ylo[c, pl.ds(z, 1), :], north)

            def column(ref):
                turned = pltpu.roll(ref[c], shift, 1)
                return jnp.concatenate(
                    [jnp.broadcast_to(turned[:, t : t + 1], (8, width)) for t in range(tiles)], axis=0
                )

            east = jnp.where(lanes == width - 1, column(xhi), pltpu.roll(here, width - 1, 1))
            west = jnp.where(lanes == 0, column(xlo), pltpu.roll(here, 1, 1))
            return here, (down, up, south, north, east, west)

        q, near = values(3)
        weights = [mean_weight(q, n) for n in near]
        total = weights[0] + weights[1] + weights[2] + weights[3] + weights[4] + weights[5]
        cells, flux = [], []
        for c in range(3):
            u, near = values(c)
            moved = weights[0] * (u - near[0])
            for w, n in zip(weights[1:], near[1:]):
                moved = moved + w * (u - n)
            cells.append(u)
            flux.append(moved)
        v = pore[z].astype(F32)
        residual = [
            right[i, z]
            - v * (m[i][0] * cells[0] + m[i][1] * cells[1] + m[i][2] * cells[2])
            - (k[i][0] * flux[0] + k[i][1] * flux[1] + k[i][2] * flux[2])
            for i in range(3)
        ]
        entries = [[v * m[i][j] + total * k[i][j] for j in range(3)] for i in range(3)]

        def cofactor(r, c):
            r1, r2, c1, c2 = (r + 1) % 3, (r + 2) % 3, (c + 1) % 3, (c + 2) % 3
            return entries[r1][c1] * entries[r2][c2] - entries[r1][c2] * entries[r2][c1]

        factors = [[cofactor(r, c) for c in range(3)] for r in range(3)]
        determinant = (
            entries[0][0] * factors[0][0] + entries[0][1] * factors[0][1] + entries[0][2] * factors[0][2]
        )
        scale = inverse(determinant)
        for i in range(3):
            base[i, z] = cells[i] + scale * (
                factors[0][i] * residual[0] + factors[1][i] * residual[1] + factors[2][i] * residual[2]
            )
            gain[i, z] = scale * (factors[0][i] * k[0][0] + factors[1][i] * k[1][0] + factors[2][i] * k[2][0])
        face[0, z] = weights[0] + weights[1]
        for d in range(2, 6):
            face[d - 1, z] = weights[d]
        areal = weights[2] + weights[3] + weights[4] + weights[5]
        sums[0] += residual[0]
        sums[1] += v * m[0][0] + areal * k[0][0]
        sums[2] += weights[2] * k[0][0]
        sums[3] += weights[4] * k[0][0]
        return carry

    lax.fori_loop(0, depth, layer, 0)

    lane = lane_index((8, 128))
    last = tiles - 1

    def tile(p, t):
        return sums[p, 8 * t : 8 * t + 8, :]

    for p in range(4):
        message[0, 8 * p : 8 * p + 8, :] = tile(p, 0)
        message[1, 8 * p : 8 * p + 8, :] = tile(p, last)
        left = jnp.zeros((8, 128), F32)
        right_side = jnp.zeros((8, 128), F32)
        for t in range(tiles):
            here = (lane >= 8 * t) & (lane < 8 * t + 8)
            left = jnp.where(here, pltpu.roll(tile(p, t), 8 * t, 1) if t else tile(p, t), left)
            right_side = jnp.where(here, pltpu.roll(tile(p, t), 8 * t + 8, 1), right_side)
        message[2, 8 * p : 8 * p + 8, :] = left
        message[3, 8 * p : 8 * p + 8, :] = right_side
    for k, (t, at_end) in enumerate(((0, 0), (last, 1), (0, 1), (last, 0))):
        corner = jnp.zeros((8, 128), F32)
        for p in range(4):
            here = (lane >= 8 * p) & (lane < 8 * p + 8)
            turn = (8 * p + 8 * at_end) % 128
            corner = jnp.where(here, pltpu.roll(tile(p, t), turn, 1) if turn else tile(p, t), corner)
        message[4 + k, 0:8, :] = corner
        for t in range(4):
            message[4 + k, 8 + 8 * t : 16 + 8 * t, :] = tile(k, t)
        message[k, 32:40, :] = tile(k, last)


def sum_kernel(parts, total):
    result = parts[0]
    for i in range(1, parts.shape[0]):
        result = result + parts[i]
    total[...] = result


def sweep_kernel(shares, base, gain, face, new_state, correction):
    depth, height, width = base.shape[1:]
    tiles = height // 8
    lane = lane_index((8, 128))

    def tile(k, t):
        return shares[k, 8 * t : 8 * t + 8, :]

    def side(right, right_at, left, left_at):
        turn_right, turn_left = (128 - right_at) % 128, (width - 8 - left_at) % 128
        right = pltpu.roll(right, turn_right, 1) if turn_right else right
        left = pltpu.roll(left, turn_left, 1) if turn_left else left
        return jnp.where(lane < 8, right, jnp.where(lane >= width - 8, left, 0.0))

    planes = []
    for p in range(4):
        main = [tile(1, p)] + [tile(4 + p, 1 + t) for t in range(tiles - 1)] + [tile(p, 4), tile(0, p)]
        edge = [side(tile(7, 0), 8 * p, tile(5, 0), 8 * p)]
        for t in range(tiles):
            edge.append(side(tile(2, p), 8 * t, tile(3, p), 8 * t))
        edge.append(side(tile(4, 0), 8 * p, tile(6, 0), 8 * p))
        planes.append(
            jnp.concatenate([jnp.concatenate(main, axis=0), jnp.concatenate(edge, axis=0)], axis=1)
        )
    wide_rows, wide_columns = planes[0].shape
    filled = planes[1] > 0.0
    scale = jnp.where(filled, RELAX / jnp.where(filled, planes[1], 1.0), 0.0)
    source = scale * planes[0]
    south = scale * planes[2]
    north = scale * pltpu.roll(planes[2], 1, 0)
    east = scale * planes[3]
    west = scale * pltpu.roll(planes[3], 1, 1)

    def around(field):
        return (
            pltpu.roll(field, wide_rows - 1, 0),
            pltpu.roll(field, 1, 0),
            pltpu.roll(field, wide_columns - 1, 1),
            pltpu.roll(field, 1, 1),
        )

    field = source
    for _ in range(SWEEPS - 1):
        s, n, e, w = around(field)
        field = (1.0 - RELAX) * field + source + south * s + north * n + east * e + west * w
    near = around(field)
    own = field[8 : 8 + height, 0:width]
    near = [n[8 : 8 + height, 0:width] for n in near]
    correction[...] = own

    def layer(z, carry):
        push = face[0, z] * own
        for d in range(4):
            push = push + face[1 + d, z] * near[d]
        for i in range(3):
            new_state[i, z] = base[i, z] + gain[i, z] * push
        return carry

    lax.fori_loop(0, depth, layer, 0)


def shape_of(*dims):
    return jax.ShapeDtypeStruct(dims, F32)


def per_device(state, right_side, permeability, pore_volume, facies, storage_table, coupling_table):
    _, depth, height, width = state.shape
    layers = lax.axis_size("gz")
    row_of, rows, columns = lax.axis_size("gx"), lax.axis_size("gy"), lax.axis_size("gz")

    faces = pl.pallas_call(
        faces_kernel,
        out_shape=[shape_of(4, height, width)] * 2 + [shape_of(4, depth, width)] * 2 + [shape_of(4, 8, 128)] * 2,
        in_specs=vmem(2),
        out_specs=vmem(6),
        compiler_params=PARAMS,
    )(state, permeability)

    def from_next(first, axis):
        n = lax.axis_size(axis)
        return lax.ppermute(first, axis, [(i + 1, i) for i in range(n - 1)])

    def from_previous(last, axis):
        n = lax.axis_size(axis)
        return lax.ppermute(last, axis, [(i, i + 1) for i in range(n - 1)])

    around = []
    for axis, first, last in (("gz", 0, 1), ("gy", 2, 3), ("gx", 4, 5)):
        around += [from_previous(faces[last], axis), from_next(faces[first], axis)]

    base, gain, face, message = pl.pallas_call(
        cells_kernel,
        out_shape=[
            shape_of(3, depth, height, width),
            shape_of(3, depth, height, width),
            shape_of(5, depth, height, width),
            shape_of(layers, 40, 128),
        ],
        in_specs=smem(3) + vmem(10),
        out_specs=vmem(4),
        scratch_shapes=[pltpu.VMEM((4, height, width), F32)],
        compiler_params=PARAMS,
    )(
        facies,
        storage_table.reshape(-1, 9),
        coupling_table.reshape(-1, 9),
        state,
        right_side,
        permeability,
        pore_volume,
        *around,
    )

    parts = lax.all_to_all(message, "gz", 0, 0)
    share = pl.pallas_call(
        sum_kernel,
        out_shape=shape_of(40, 128),
        in_specs=vmem(1),
        out_specs=pl.BlockSpec(memory_space=pltpu.VMEM),
        compiler_params=PARAMS,
    )(parts)
    pairs = []
    for x in range(row_of):
        for y in range(rows):
            for k, (dy, dx) in enumerate(DIRECTIONS):
                if 0 <= x + dx < row_of and 0 <= y + dy < rows:
                    pairs.append(
                        ((x * rows + y) * columns + k, ((x + dx) * rows + y + dy) * columns + k)
                    )
    strip = lax.ppermute(share[:32], ("gx", "gy", "gz"), pairs)
    corner = lax.axis_index("gz") >= 4
    tile_row = lax.broadcasted_iota(jnp.int32, (40, 128), 0)
    take_strip = (tile_row < 8) | ((tile_row < 32) & jnp.logical_not(corner))
    padded = jnp.concatenate([strip, share[32:]], axis=0)
    merged = jnp.where(take_strip, padded, share)
    shares = lax.all_to_all(jnp.broadcast_to(merged[None], (layers, 40, 128)), "gz", 0, 0)

    new_state, correction = pl.pallas_call(
        sweep_kernel,
        out_shape=[shape_of(3, depth, height, width), shape_of(height, width)],
        in_specs=vmem(4),
        out_specs=vmem(2),
        compiler_params=PARAMS,
    )(shares, base, gain, face)
    return (new_state, correction)


def solution(mesh):
    return jax.shard_map(
        per_device,
        mesh=mesh,
        in_specs=(
            P(None, "gz", "gy", "gx"),
            P(None, "gz", "gy", "gx"),
            P("gz", "gy", "gx"),
            P("gz", "gy", "gx"),
            P("gz"),
            P(),
            P(),
        ),
        out_specs=(P(None, "gz", "gy", "gx"), P("gy", "gx")),
        check_vma=False,
    )
```

time: 309 us -> 69.2 us (0.22)
  the two profiles are of different devices: /device:TPU:154 before, /device:TPU:232 now
where the time goes in v1:
time: 69.2 us; the launch traced here: 68.5 us
  starting transfers between devices  24.7 us (36%)
  waiting for transfers between devices  13.1 us (19%)
  local copies, waits for them, and re-layouts  10.5 us (15%)
  Pallas kernels  9.71 us (14%)
  blocking collectives  9.63 us (14%)
  between operations  0.78 us (1%)
    unnamed x24, local copies, waits for them, and re-layouts  10.3 us
    ppermute x3, starting transfers between devices, from_previous(): return lax.ppermute(last, axis, [(i, i + 1) for i in range(n - 1)])  10.3 us
    all_to_all x1, blocking collectives, per_device(): lax.all_to_all(jnp.broadcast_to(merged[None], (layers, 40, 128)), 'gz', 0...  9.63 us
    all_to_all x1, starting transfers between devices, per_device(): parts = lax.all_to_all(message, 'gz', 0, 0)  6.96 us
    all_to_all x1, waiting for transfers between devices, per_device(): parts = lax.all_to_all(message, 'gz', 0, 0)  6.49 us
    pallas_call x1, Pallas kernels, per_device(): pl.pallas_call(cells_kernel, out_shape=[shape_of(3, depth, height, width)...  5.97 us
    ppermute x3, starting transfers between devices, from_next(): return lax.ppermute(first, axis, [(i + 1, i) for i in range(n - 1)])  5.57 us
    ppermute x1, waiting for transfers between devices, per_device(): strip = lax.ppermute(share[:32], ('gx', 'gy', 'gz'), pairs)  4.89 us
  transfers between devices with their start and end apart: 8, of which 3 were waited for; matrix products, arithmetic and copies ran while one was open for 2% of the time, Pallas kernels for 0%

profile of v1, /device:TPU:232, one launch (start us, length us, event | category | flops | bytes accessed | tf_op | source)
XLA Modules:
  0.0 68.5 jit_solution(10471159912385444233)
XLA Ops:
  0.6 1.2 %copy-done = f32[3,16,40,128]{3,2,1,0:T(8,128)S(1)} copy-done((f32[3,16,40,128]{3,2,1,0:T(8,128)S(1)}, f32[3,16,40,128]{3,2,1,0:T(8,128)}, u32[]{:S(2)}) %copy-start) | copy-done | bytes 983064
  1.8 0.9 %copy-done.7 = bf16[16,40,128]{2,1,0:T(8,128)(2,1)S(1)} copy-done((bf16[16,40,128]{2,1,0:T(8,128)(2,1)S(1)}, bf16[16,40,128]{2,1,0:T(8,128)(2,1)}, u32[]{:S(2)}) %copy-start.7) | copy-done | bytes 163864
  2.8 1.8 %shard_map.86 = (f32[4,40,128]{2,1,0:T(8,128)S(1)}, f32[4,40,128]{2,1,0:T(8,128)S(1)}, f32[4,16,128]{2,1,0:T(8,128)S(1)}, f32[4,16,128]{2,1,0:T(8,128)S(1)}, f32...) custom-call(f32[3,16,40,128]{3,2,1,0:T(8,128)S(1)} %copy-done, bf16[16,40,128]{2,1,0:T(8,128)(2,1)S(1)} %copy-done.7), custom_call_target="tpu_custom_call" | custom-call | tf_op jit(solution)/shard_map/pallas_call | solution.py:261
  4.5 1.7 %collective-permute-start = (f32[4,40,128]{2,1,0:T(8,128)S(1)}, f32[4,40,128]{2,1,0:T(8,128)S(1)}, u32[]{:S(2)}, u32[]{:S(2)}) collective-permute-start(f32[4,40,128]{2,1,0:T(8,128)S(1)} %get-tuple-element.12), channel_id=1, source_target_pairs={{0,1},{1,2},{2,3},{3,4},{4,5},{5,6},{6,7},{8,9},{9,10},{10,11},{11... | collective-permute-start | bytes 245768 | tf_op jit(solution)/shard_map/ppermute | solution.py:275
  6.3 1.3 %collective-permute-start.1 = (f32[4,40,128]{2,1,0:T(8,128)S(1)}, f32[4,40,128]{2,1,0:T(8,128)S(1)}, u32[]{:S(2)}, u32[]{:S(2)}) collective-permute-start(f32[4,40,128]{2,1,0:T(8,128)S(1)} %get-tuple-element.13), channel_id=1, source_target_pairs={{1,0},{2,1},{3,2},{4,3},{5,4},{6,5},{7,6},{9,8},{10,9},{11,10},{12... | collective-permute-start | bytes 245768 | tf_op jit(solution)/shard_map/ppermute | solution.py:271
  7.6 3.5 %collective-permute-start.4 = (f32[4,8,128]{2,1,0:T(8,128)S(1)}, f32[4,8,128]{2,1,0:T(8,128)S(1)}, u32[]{:S(2)}, u32[]{:S(2)}) collective-permute-start(f32[4,8,128]{2,1,0:T(8,128)S(1)} %get-tuple-element.16), channel_id=1, source_target_pairs={{0,128},{128,256},{256,384},{1,129},{129,257},{257,385},{2,130},{1... | collective-permute-start | bytes 49160 | tf_op jit(solution)/shard_map/ppermute | solution.py:275
  11.1 5.0 %collective-permute-start.2 = (f32[4,16,128]{2,1,0:T(8,128)S(1)}, f32[4,16,128]{2,1,0:T(8,128)S(1)}, u32[]{:S(2)}, u32[]{:S(2)}) collective-permute-start(f32[4,16,128]{2,1,0:T(8,128)S(1)} %get-tuple-element.14), channel_id=1, source_target_pairs={{0,8},{8,16},{16,24},{24,32},{32,40},{40,48},{48,56},{56,64},{64,7... | collective-permute-start | bytes 98312 | tf_op jit(solution)/shard_map/ppermute | solution.py:275
  16.1 1.9 %collective-permute-start.3 = (f32[4,16,128]{2,1,0:T(8,128)S(1)}, f32[4,16,128]{2,1,0:T(8,128)S(1)}, u32[]{:S(2)}, u32[]{:S(2)}) collective-permute-start(f32[4,16,128]{2,1,0:T(8,128)S(1)} %get-tuple-element.15), channel_id=1, source_target_pairs={{8,0},{16,8},{24,16},{32,24},{40,32},{48,40},{56,48},{64,56},{72,6... | collective-permute-start | bytes 98312 | tf_op jit(solution)/shard_map/ppermute | solution.py:271
  18.0 0.0 collective-permute-done.4.xlo
  18.0 2.4 %collective-permute-start.5 = (f32[4,8,128]{2,1,0:T(8,128)S(1)}, f32[4,8,128]{2,1,0:T(8,128)S(1)}, u32[]{:S(2)}, u32[]{:S(2)}) collective-permute-start(f32[4,8,128]{2,1,0:T(8,128)S(1)} %get-tuple-element.17), channel_id=1, source_target_pairs={{128,0},{256,128},{384,256},{129,1},{257,129},{385,257},{130,2},{2... | collective-permute-start | bytes 49160 | tf_op jit(solution)/shard_map/ppermute | solution.py:271
  20.4 0.7 %copy.11 = f32[4,3,3]{2,1,0:T(4,128)S(1)} copy(f32[4,3,3]{2,0,1:T(4,128)} %param.12) | data formatting | bytes 288 | tf_op args[5]
  21.1 0.1 reshape.11.storage_table
  21.2 0.7 %copy.12 = f32[4,3,3]{2,1,0:T(4,128)S(1)} copy(f32[4,3,3]{2,0,1:T(4,128)} %param.13) | data formatting | bytes 288 | tf_op args[6]
  21.9 0.1 reshape.12.coupling_table
  22.0 1.7 %collective-permute-done.5.xhi = f32[4,8,128]{2,1,0:T(8,128)S(1)} collective-permute-done((f32[4,8,128]{2,1,0:T(8,128)S(1)}, f32[4,8,128]{2,1,0:T(8,128)S(1)}, u32[]{:S(2)}, u32[]{:S(2)}) %collective-permute-start.5) | collective-permute-done | bytes 16416 | tf_op jit(solution)/shard_map/ppermute | solution.py:271
  23.7 0.0 collective-permute-done.2.ylo
  23.7 0.0 copy-start.6
  23.7 1.2 %copy-done.6 = f32[3,16,40,128]{3,2,1,0:T(8,128)S(1)} copy-done((f32[3,16,40,128]{3,2,1,0:T(8,128)S(1)}, f32[3,16,40,128]{3,2,1,0:T(8,128)}, u32[]{:S(2)}) %copy-start.6) | copy-done | bytes 983064
  24.9 0.9 %copy-done.8 = bf16[16,40,128]{2,1,0:T(8,128)(2,1)S(1)} copy-done((bf16[16,40,128]{2,1,0:T(8,128)(2,1)S(1)}, bf16[16,40,128]{2,1,0:T(8,128)(2,1)}, u32[]{:S(2)}) %copy-start.8) | copy-done | bytes 163864
  25.8 0.9 %copy-done.9 = bf16[16,40,128]{2,1,0:T(8,128)(2,1)S(1)} copy-done((bf16[16,40,128]{2,1,0:T(8,128)(2,1)S(1)}, bf16[16,40,128]{2,1,0:T(8,128)(2,1)}, u32[]{:S(2)}) %copy-start.9) | copy-done | bytes 163864
  26.8 0.7 copy-done.10
  27.4 6.0 %shard_map.87 = (f32[3,16,40,128]{3,2,1,0:T(8,128)S(1)}, f32[3,16,40,128]{3,2,1,0:T(8,128)S(1)}, f32[5,16,40,128]{3,2,1,0:T(8,128)S(1)}, f32[8,40,128]{2,1,0:T(8,128)}) custom-call(s32[16]{0:T(128)S(1)} %copy-done.10, f32[4,9]{1,0:T(4,128)S(1)} %reshape.11.storage_table, f32[4,9]{1,0:T(4,128)S(1)} %reshape.12.coupling_table, ...), custom_call_target="tpu_custom_call" | custom-call | tf_op jit(solution)/shard_map/pallas_call | solution.py:281
  33.4 0.9 %copy-done.2 = f32[3,16,40,128]{3,2,1,0:T(8,128)} copy-done((f32[3,16,40,128]{3,2,1,0:T(8,128)}, f32[3,16,40,128]{3,2,1,0:T(8,128)S(1)}, u32[]{:S(2)}) %copy-start.2) | copy-done | bytes 983064
  34.3 1.0 %copy-done.4 = f32[3,16,40,128]{3,2,1,0:T(8,128)} copy-done((f32[3,16,40,128]{3,2,1,0:T(8,128)}, f32[3,16,40,128]{3,2,1,0:T(8,128)S(1)}, u32[]{:S(2)}) %copy-start.4) | copy-done | bytes 983064
  35.3 7.0 %all-to-all-start = ((f32[8,40,128]{2,1,0:T(8,128)}), f32[8,40,128]{2,1,0:T(8,128)S(1)}, u32[]{:S(2)}, u32[]{:S(2)}) async-start(f32[8,40,128]{2,1,0:T(8,128)} %get-tuple-element.18), calls=%async_computation | async-start | bytes 327680 | tf_op jit(solution)/shard_map/all_to_all | solution.py:304
  42.3 6.5 %all-to-all-done.parts = f32[8,40,128]{2,1,0:T(8,128)S(1)} async-done(((f32[8,40,128]{2,1,0:T(8,128)}), f32[8,40,128]{2,1,0:T(8,128)S(1)}, u32[]{:S(2)}, u32[]{:S(2)}) %all-to-all-start) | async-done | bytes 163872 | tf_op jit(solution)/shard_map/all_to_all | solution.py:304
  48.8 1.9 %collective-permute-start.6 = (f32[32,128]{1,0:T(8,128)S(1)}, f32[32,128]{1,0:T(8,128)S(1)}, u32[]{:S(2)}, u32[]{:S(2)}) collective-permute-start(f32[32,128]{1,0:T(8,128)S(1)} %slice.8), channel_id=1, source_target_pairs={{1,9},{3,131},{5,141},{8,0},{9,17},{11,139},{13,149},{14,134},{16,... | collective-permute-start | bytes 49160 | tf_op jit(solution)/shard_map/ppermute | solution.py:320
  50.7 4.9 %collective-permute-done.6 = f32[32,128]{1,0:T(8,128)S(1)} collective-permute-done((f32[32,128]{1,0:T(8,128)S(1)}, f32[32,128]{1,0:T(8,128)S(1)}, u32[]{:S(2)}, u32[]{:S(2)}) %collective-permute-start.6) | collective-permute-done | bytes 16416 | tf_op jit(solution)/shard_map/ppermute | solution.py:320
  55.6 0.1 maximum_select_fusion
  55.7 9.6 %all_to_all.10.shares = f32[8,40,128]{2,1,0:T(8,128)S(1)} all-to-all(f32[8,40,128]{2,1,0:T(8,128)S(1)} %broadcast_in_dim.2), channel_id=1, replica_groups=mesh['gx'=4,'gy'=16,'gz'=8] {'gz'}, dimensions={0} | all-to-all | bytes 327680 | tf_op jit(solution)/shard_map/all_to_all | solution.py:326
  65.3 1.2 %copy-done.5 = f32[3,16,40,128]{3,2,1,0:T(8,128)S(1)} copy-done((f32[3,16,40,128]{3,2,1,0:T(8,128)S(1)}, f32[3,16,40,128]{3,2,1,0:T(8,128)}, u32[]{:S(2)}) %copy-start.5) | copy-done | bytes 983064
  66.5 2.0 %shard_map.89 = (f32[3,16,40,128]{3,2,1,0:T(8,128)}, f32[40,128]{1,0:T(8,128)}) custom-call(f32[8,40,128]{2,1,0:T(8,128)S(1)} %all_to_all.10.shares, f32[3,16,40,128]{3,2,1,0:T(8,128)S(1)} %copy-done.3, f32[3,16,40,128]{3,2,1,0:T(8,128)S(1)} %copy-done.5, f32[5,16,40,128]{3,2,1,0:T(8,128)S(1)} %get-tuple-element.21.face), custom_call_target="tpu_custom_call" | custom-call | tf_op jit(solution)/shard_map/pallas_call | solution.py:328
  (20 shorter events, 0.1 us)
Async XLA Ops:
  0.6 1.2 %copy-start = (f32[3,16,40,128]{3,2,1,0:T(8,128)S(1)}, f32[3,16,40,128]{3,2,1,0:T(8,128)}, u32[]{:S(2)}) copy-start(f32[3,16,40,128]{3,2,1,0:T(8,128)} %state.3) | copy-start | bytes 2949124
  1.8 0.9 %copy-start.7 = (bf16[16,40,128]{2,1,0:T(8,128)(2,1)S(1)}, bf16[16,40,128]{2,1,0:T(8,128)(2,1)}, u32[]{:S(2)}) copy-start(bf16[16,40,128]{2,1,0:T(8,128)(2,1)} %perm.3) | copy-start | bytes 491524
  2.7 21.0 %copy-start.1 = (f32[3,16,40,128]{3,2,1,0:T(8,128)S(1)}, f32[3,16,40,128]{3,2,1,0:T(8,128)}, u32[]{:S(2)}) copy-start(f32[3,16,40,128]{3,2,1,0:T(8,128)} %state.3) | copy-start | bytes 2949124
  4.5 19.2 %collective-permute-start = (f32[4,40,128]{2,1,0:T(8,128)S(1)}, f32[4,40,128]{2,1,0:T(8,128)S(1)}, u32[]{:S(2)}, u32[]{:S(2)}) collective-permute-start(f32[4,40,128]{2,1,0:T(8,128)S(1)} %get-tuple-element.12), channel_id=1, source_target_pairs={{0,1},{1,2},{2,3},{3,4},{4,5},{5,6},{6,7},{8,9},{9,10},{10,11},{11... | collective-permute-start | bytes 245768 | tf_op jit(solution)/shard_map/ppermute | solution.py:275
  6.3 17.4 %collective-permute-start.1 = (f32[4,40,128]{2,1,0:T(8,128)S(1)}, f32[4,40,128]{2,1,0:T(8,128)S(1)}, u32[]{:S(2)}, u32[]{:S(2)}) collective-permute-start(f32[4,40,128]{2,1,0:T(8,128)S(1)} %get-tuple-element.13), channel_id=1, source_target_pairs={{1,0},{2,1},{3,2},{4,3},{5,4},{6,5},{7,6},{9,8},{10,9},{11,10},{12... | collective-permute-start | bytes 245768 | tf_op jit(solution)/shard_map/ppermute | solution.py:271
  7.6 10.5 %collective-permute-start.4 = (f32[4,8,128]{2,1,0:T(8,128)S(1)}, f32[4,8,128]{2,1,0:T(8,128)S(1)}, u32[]{:S(2)}, u32[]{:S(2)}) collective-permute-start(f32[4,8,128]{2,1,0:T(8,128)S(1)} %get-tuple-element.16), channel_id=1, source_target_pairs={{0,128},{128,256},{256,384},{1,129},{129,257},{257,385},{2,130},{1... | collective-permute-start | bytes 49160 | tf_op jit(solution)/shard_map/ppermute | solution.py:275
  11.1 12.6 %collective-permute-start.2 = (f32[4,16,128]{2,1,0:T(8,128)S(1)}, f32[4,16,128]{2,1,0:T(8,128)S(1)}, u32[]{:S(2)}, u32[]{:S(2)}) collective-permute-start(f32[4,16,128]{2,1,0:T(8,128)S(1)} %get-tuple-element.14), channel_id=1, source_target_pairs={{0,8},{8,16},{16,24},{24,32},{32,40},{40,48},{48,56},{56,64},{64,7... | collective-permute-start | bytes 98312 | tf_op jit(solution)/shard_map/ppermute | solution.py:275
  16.1 7.6 %collective-permute-start.3 = (f32[4,16,128]{2,1,0:T(8,128)S(1)}, f32[4,16,128]{2,1,0:T(8,128)S(1)}, u32[]{:S(2)}, u32[]{:S(2)}) collective-permute-start(f32[4,16,128]{2,1,0:T(8,128)S(1)} %get-tuple-element.15), channel_id=1, source_target_pairs={{8,0},{16,8},{24,16},{32,24},{40,32},{48,40},{56,48},{64,56},{72,6... | collective-permute-start | bytes 98312 | tf_op jit(solution)/shard_map/ppermute | solution.py:271
  18.0 5.6 %collective-permute-start.5 = (f32[4,8,128]{2,1,0:T(8,128)S(1)}, f32[4,8,128]{2,1,0:T(8,128)S(1)}, u32[]{:S(2)}, u32[]{:S(2)}) collective-permute-start(f32[4,8,128]{2,1,0:T(8,128)S(1)} %get-tuple-element.17), channel_id=1, source_target_pairs={{128,0},{256,128},{384,256},{129,1},{257,129},{385,257},{130,2},{2... | collective-permute-start | bytes 49160 | tf_op jit(solution)/shard_map/ppermute | solution.py:271
  23.7 1.2 %copy-start.6 = (f32[3,16,40,128]{3,2,1,0:T(8,128)S(1)}, f32[3,16,40,128]{3,2,1,0:T(8,128)}, u32[]{:S(2)}) copy-start(f32[3,16,40,128]{3,2,1,0:T(8,128)} %right.1) | copy-start | bytes 2949124
  24.9 0.9 %copy-start.8 = (bf16[16,40,128]{2,1,0:T(8,128)(2,1)S(1)}, bf16[16,40,128]{2,1,0:T(8,128)(2,1)}, u32[]{:S(2)}) copy-start(bf16[16,40,128]{2,1,0:T(8,128)(2,1)} %perm.3) | copy-start | bytes 491524
  25.8 0.9 %copy-start.9 = (bf16[16,40,128]{2,1,0:T(8,128)(2,1)S(1)}, bf16[16,40,128]{2,1,0:T(8,128)(2,1)}, u32[]{:S(2)}) copy-start(bf16[16,40,128]{2,1,0:T(8,128)(2,1)} %pore.1) | copy-start | bytes 491524
  26.8 0.7 copy-start.10
  33.4 0.9 %copy-start.2 = (f32[3,16,40,128]{3,2,1,0:T(8,128)}, f32[3,16,40,128]{3,2,1,0:T(8,128)S(1)}, u32[]{:S(2)}) copy-start(f32[3,16,40,128]{3,2,1,0:T(8,128)S(1)} %get-tuple-element.19.base) | copy-start | bytes 2949124
  34.3 1.0 %copy-start.4 = (f32[3,16,40,128]{3,2,1,0:T(8,128)}, f32[3,16,40,128]{3,2,1,0:T(8,128)S(1)}, u32[]{:S(2)}) copy-start(f32[3,16,40,128]{3,2,1,0:T(8,128)S(1)} %get-tuple-element.20.gain) | copy-start | bytes 2949124
  35.3 30.0 %copy-start.3 = (f32[3,16,40,128]{3,2,1,0:T(8,128)S(1)}, f32[3,16,40,128]{3,2,1,0:T(8,128)}, u32[]{:S(2)}) copy-start(f32[3,16,40,128]{3,2,1,0:T(8,128)} %copy-done.2) | copy-start | bytes 2949124
  35.3 13.4 %all-to-all-start = ((f32[8,40,128]{2,1,0:T(8,128)}), f32[8,40,128]{2,1,0:T(8,128)S(1)}, u32[]{:S(2)}, u32[]{:S(2)}) async-start(f32[8,40,128]{2,1,0:T(8,128)} %get-tuple-element.18), calls=%async_computation | async-start | bytes 327680 | tf_op jit(solution)/shard_map/all_to_all | solution.py:304
  48.8 6.8 %collective-permute-start.6 = (f32[32,128]{1,0:T(8,128)S(1)}, f32[32,128]{1,0:T(8,128)S(1)}, u32[]{:S(2)}, u32[]{:S(2)}) collective-permute-start(f32[32,128]{1,0:T(8,128)S(1)} %slice.8), channel_id=1, source_target_pairs={{1,9},{3,131},{5,141},{8,0},{9,17},{11,139},{13,149},{14,134},{16,... | collective-permute-start | bytes 49160 | tf_op jit(solution)/shard_map/ppermute | solution.py:320
  65.3 1.2 %copy-start.5 = (f32[3,16,40,128]{3,2,1,0:T(8,128)S(1)}, f32[3,16,40,128]{3,2,1,0:T(8,128)}, u32[]{:S(2)}) copy-start(f32[3,16,40,128]{3,2,1,0:T(8,128)} %copy-done.4) | copy-start | bytes 2949124

commit v2 on v1

v2 whole, which is shorter than its diff:
```python
import jax
import jax.numpy as jnp
from jax import lax
from jax.experimental import pallas as pl
from jax.experimental.pallas import tpu as pltpu
from jax.sharding import PartitionSpec as P

SWEEPS = 8
RELAX = 0.8
DIRECTIONS = ((-1, 0), (1, 0), (0, -1), (0, 1), (-1, -1), (1, 1), (-1, 1), (1, -1))
F32 = jnp.float32
PARAMS = pltpu.CompilerParams(vmem_limit_bytes=16 * 2**20)
CHUNK = 4


def vmem(count):
    return [pl.BlockSpec(memory_space=pltpu.VMEM)] * count


def hbm(count):
    return [pl.BlockSpec(memory_space=pltpu.HBM)] * count


def shape_of(*dims):
    return jax.ShapeDtypeStruct(dims, F32)


def in_hbm(*arrays):
    return [pltpu.with_memory_space_constraint(a, pltpu.HBM) for a in arrays]


def lane_index(shape):
    return lax.broadcasted_iota(jnp.int32, shape, len(shape) - 1)


def row_index(shape):
    return lax.broadcasted_iota(jnp.int32, shape, len(shape) - 2)


def turn(block, shift, axis):
    shift = shift % block.shape[axis]
    return pltpu.roll(block, shift, axis) if shift else block


def inverse(value):
    guess = pl.reciprocal(value, approx=True)
    return guess * (2.0 - value * guess)


def mean_weight(a, b):
    return (a + a) * b * inverse(a + b)


def faces_kernel(
    state, right, perm, pore, facies, storage_table, coupling_table,
    state_v, right_v, perm_v, pore_v, coef, coef_lane, zlo, zhi, ylo, yhi, xpack,
    perm_half, pore_half, facies_s, storage_s, coupling_s, sems,
):
    depth, height, width = perm.shape
    tiles, half = height // 8, depth // 2
    copies = [
        pltpu.make_async_copy(perm, perm_half, sems.at[0]),
        pltpu.make_async_copy(pore, pore_half, sems.at[1]),
        pltpu.make_async_copy(facies, facies_s, sems.at[2]),
        pltpu.make_async_copy(storage_table, storage_s, sems.at[3]),
        pltpu.make_async_copy(coupling_table, coupling_s, sems.at[4]),
        pltpu.make_async_copy(right.at[0], right_v, sems.at[5]),
    ]
    pieces = [
        pltpu.make_async_copy(state.at[:, pl.ds(z, CHUNK)], state_v.at[:, pl.ds(z, CHUNK)], sems.at[6 + z // CHUNK])
        for z in range(0, depth, CHUNK)
    ]
    copies[0].start()
    for piece in pieces:
        piece.start()
    for copy in copies[1:]:
        copy.start()
    lanes = lane_index((8, 128))
    pairs = lanes // 2
    packed = [[jnp.full((8, 128), 1.0 if c == 3 else 0.0, F32) for _ in range(2)] for c in range(4)]
    copies[0].wait()
    for z in range(depth):
        if z % CHUNK == 0:
            pieces[z // CHUNK].wait()
        for c in range(4):
            if c < 3:
                cells = state_v[c, z]
            else:
                cells = perm_half[z].astype(F32)
                perm_v[z] = cells
            ylo[c, z : z + 1, :] = cells[0:1]
            yhi[c, z : z + 1, :] = cells[height - 1 : height]
            if z == 0:
                zlo[c] = cells
            if z == depth - 1:
                zhi[c] = cells
            for t in range(tiles):
                i = (z % half) * tiles + t
                turned = turn(cells[8 * t : 8 * t + 8], 2 * i + 1, 1)
                packed[c][z // half] = jnp.where(pairs == i, turned, packed[c][z // half])
    for c in range(4):
        for h in range(2):
            xpack[c, h] = packed[c][h]
    for copy in copies[1:5]:
        copy.wait()
    for z in range(depth):
        pore_v[z] = pore_half[z].astype(F32)
    rows = row_index((depth, 128))
    fids = jnp.zeros((depth, 128), jnp.int32)
    fids_lane = [jnp.zeros((8, 128), jnp.int32) for _ in range(2)]
    for z in range(depth):
        fid = facies_s[z]
        fids = jnp.where(rows == z, fid, fids)
        fids_lane[z // half] = jnp.where(lanes >= 2 * tiles * (z % half), fid, fids_lane[z // half])
    kinds = storage_table.shape[1]
    for which, table in enumerate((storage_s, coupling_s)):
        for k in range(9):
            rows_of = jnp.zeros((depth, 128), F32)
            for f in range(kinds):
                rows_of = jnp.where(fids == f, table[k // 3, f, k % 3], rows_of)
            coef[9 * which + k] = rows_of
    for k in range(3):
        for h in range(2):
            lane_of = jnp.zeros((8, 128), F32)
            for f in range(kinds):
                lane_of = jnp.where(fids_lane[h] == f, coupling_s[0, f, k], lane_of)
            coef_lane[k, h] = lane_of
    copies[5].wait()


def sums_kernel(
    coef, coef_lane, state, right, perm, pore, ylo_own, yhi_own, xpack, zlo, zhi, ylo, yhi, xlo, xhi,
    layer_out, areal_out, xnear, message,
    acc, layer_face, areal_face, sems,
):
    depth, height, width = perm.shape
    tiles, half = height // 8, depth // 2
    rows = row_index((height, width))
    lanes = lane_index((height, width))
    lane = lane_index((8, 128))

    def flat(own, near, k0):
        weight = mean_weight(own[3], near[3])
        jump = k0[0] * (own[0] - near[0]) + k0[1] * (own[1] - near[1]) + k0[2] * (own[2] - near[2])
        return weight, weight * jump

    def down_rows(block):
        return jnp.sum(block, axis=0, keepdims=True)

    k_rows = [coef[9 + k] for k in range(3)]
    south, south_flux = flat([yhi_own[c] for c in range(4)], [yhi[c] for c in range(4)], k_rows)
    north, north_flux = flat([ylo_own[c] for c in range(4)], [ylo[c] for c in range(4)], k_rows)
    south_sum, north_sum = down_rows(k_rows[0] * south), down_rows(k_rows[0] * north)
    south_flux, north_flux = down_rows(south_flux), down_rows(north_flux)
    side, side_sum, side_flux = [], 0.0, 0.0
    for h in range(2):
        near = [jnp.where(lane % 2 == 0, turn(xhi[c, h], -1, 1), turn(xlo[c, h], 1, 1)) for c in range(4)]
        for c in range(3):
            xnear[c, h] = near[c]
        weight, flux = flat([xpack[c, h] for c in range(4)], near, [coef_lane[k, h] for k in range(3)])
        used = lane < 2 * tiles * half
        side.append(weight)
        side_sum += jnp.where(used, coef_lane[0, h] * weight, 0.0)
        side_flux += jnp.where(used, flux, 0.0)
    gap = tiles * half
    while gap >= 2 * tiles:
        side_sum = side_sum + turn(side_sum, -gap, 1)
        side_flux = side_flux + turn(side_flux, -gap, 1)
        gap //= 2

    def row_of(k, z):
        return coef[k, pl.ds(z, 1), :]

    weight = mean_weight(zlo[3], perm[0])
    layer_face[0] = weight
    for a in range(1, 6):
        acc[a] = jnp.zeros((height, width), F32)
    acc[0] = -weight * (
        row_of(9, 0) * (state[0, 0] - zlo[0])
        + row_of(10, 0) * (state[1, 0] - zlo[1])
        + row_of(11, 0) * (state[2, 0] - zlo[2])
    )

    def layer(z, below, step, side_here, shift):
        q = perm[z]
        u = [state[c, z] for c in range(3)]
        k0 = [row_of(9 + c, z) for c in range(3)]
        down = mean_weight(q, below[3])
        layer_face[z + 1] = down
        jump = step[0] * (u[0] - below[0]) + step[1] * (u[1] - below[1]) + step[2] * (u[2] - below[2])
        v = pore[z]
        acc[0] += (
            right[z]
            - v * (row_of(0, z) * u[0] + row_of(1, z) * u[1] + row_of(2, z) * u[2])
            - down * jump
        )
        acc[1] += row_of(0, z) * v
        w = k0[0] * u[0] + k0[1] * u[1] + k0[2] * u[2]
        ty = jnp.where(rows == height - 1, 0.0, mean_weight(q, turn(q, -1, 0)))
        tx = jnp.where(lanes == width - 1, 0.0, mean_weight(q, turn(q, -1, 1)))
        acc[2] += k0[0] * ty
        acc[3] += k0[0] * tx
        acc[4] += ty * (w - turn(w, -1, 0))
        acc[5] += tx * (w - turn(w, -1, 1))
        edges = jnp.concatenate(
            [pltpu.roll(side_here, shift - 2 * t, 1) for t in range(tiles)], axis=0
        )
        areal_face[0, z] = jnp.where(rows == height - 1, areal_face[0, z, 0:1, :], ty)
        areal_face[1, z] = jnp.where(rows == 0, areal_face[1, z, 0:1, :], turn(ty, 1, 0))
        areal_face[2, z] = jnp.where(lanes == width - 1, edges, tx)
        areal_face[3, z] = jnp.where(lanes == 0, edges, turn(tx, 1, 1))

    for z in range(depth):
        areal_face[0, z, 0:1, :] = south[z : z + 1]
        areal_face[1, z, 0:1, :] = north[z : z + 1]

    def keep(h):
        tops, all_areal = pl.ds(h * (half + 1), half + 1 - h), pl.ds(h * half, half)
        copies = [
            pltpu.make_async_copy(layer_face.at[tops], layer_out.at[tops], sems.at[2 * h]),
            pltpu.make_async_copy(areal_face.at[:, all_areal], areal_out.at[:, all_areal], sems.at[2 * h + 1]),
        ]
        for copy in copies:
            copy.start()
        return copies

    for h in range(2):

        def body(z, carry, h=h):
            below = [state[c, z + 1] for c in range(3)] + [perm[z + 1]]
            step = [row_of(9 + c, z) - row_of(9 + c, z + 1) for c in range(3)]
            layer(z, below, step, side[h], 127 - 2 * tiles * (z - h * half))
            return carry

        lax.fori_loop(h * half, half if h == 0 else depth - 1, body, 0)
        if h == 0:
            copies = keep(0)
    z = depth - 1
    layer(z, [zhi[c] for c in range(4)], [row_of(9 + c, z) for c in range(3)], side[1], 127 - 2 * tiles * (half - 1))

    copies += keep(1)
    rhs, diag, ty, tx = acc[0], acc[1], acc[2], acc[3]
    fy, fx = acc[4], acc[5]
    edge_sum = jnp.concatenate([turn(side_sum, 127 - 2 * t, 1) for t in range(tiles)], axis=0)
    edge_flux = jnp.concatenate([turn(side_flux, 127 - 2 * t, 1) for t in range(tiles)], axis=0)
    last_row, first_row, last_lane, first_lane = rows == height - 1, rows == 0, lanes == width - 1, lanes == 0
    ty_plus, ty_minus = jnp.where(last_row, south_sum, ty), jnp.where(first_row, north_sum, turn(ty, 1, 0))
    tx_plus, tx_minus = jnp.where(last_lane, edge_sum, tx), jnp.where(first_lane, edge_sum, turn(tx, 1, 1))
    fy_plus, fy_minus = jnp.where(last_row, south_flux, fy), jnp.where(first_row, north_flux, -turn(fy, 1, 0))
    fx_plus, fx_minus = jnp.where(last_lane, edge_flux, fx), jnp.where(first_lane, edge_flux, -turn(fx, 1, 1))
    planes = [
        rhs - (fy_plus + fy_minus) - (fx_plus + fx_minus),
        diag + (ty_plus + ty_minus) + (tx_plus + tx_minus),
        ty_plus,
        tx_plus,
    ]

    last = tiles - 1

    def tile(p, t):
        return planes[p][8 * t : 8 * t + 8]

    for p in range(4):
        message[0, 8 * p : 8 * p + 8, :] = tile(p, 0)
        message[1, 8 * p : 8 * p + 8, :] = tile(p, last)
        left = jnp.zeros((8, 128), F32)
        right_side = jnp.zeros((8, 128), F32)
        for t in range(tiles):
            here = lane // 8 == t
            left = jnp.where(here, turn(tile(p, t), 8 * t, 1), left)
            right_side = jnp.where(here, turn(tile(p, t), 8 * t + 8, 1), right_side)
        message[2, 8 * p : 8 * p + 8, :] = left
        message[3, 8 * p : 8 * p + 8, :] = right_side
    for k, (t, at_end) in enumerate(((0, 0), (last, 1), (0, 1), (last, 0))):
        corner = jnp.zeros((8, 128), F32)
        for p in range(4):
            corner = jnp.where(lane // 8 == p, turn(tile(p, t), 8 * p + 8 * at_end, 1), corner)
        message[4 + k, 0:8, :] = corner
        for t in range(4):
            message[4 + k, 8 + 8 * t : 16 + 8 * t, :] = tile(k, t)
        message[k, 32:40, :] = tile(k, last)
    for copy in copies:
        copy.wait()


def cells_kernel(
    h, coef, z_face, ylo, yhi, xnear, order, state_in, right_in, pore_in, layer_in, areal_in,
    base_out, gain_out,
    state, right, pore, layer_face, areal_face, base, gain, sems,
):
    del order
    half, height, width = pore.shape
    tiles, first, pieces = height // 8, h * half, half // CHUNK
    rows = row_index((height, width))
    lanes = lane_index((height, width))
    arrivals = []
    for p in range(pieces):
        here, there = pl.ds(p * CHUNK, CHUNK), pl.ds(first + p * CHUNK, CHUNK)
        low, high = (0 if p == 0 else p * CHUNK + 1), (p + 1) * CHUNK + 1
        state_low = 1 if p == 0 and h == 0 else (0 if p == 0 else p * CHUNK + 2)
        state_high = (p + 1) * CHUNK + (1 if p == pieces - 1 and h == 1 else 2)
        z_low = first - 1 + state_low
        arrivals.append([
            pltpu.make_async_copy(
                state_in.at[:, pl.ds(z_low, state_high - state_low)],
                state.at[:, pl.ds(state_low, state_high - state_low)],
                sems.at[0, p],
            ),
            pltpu.make_async_copy(
                layer_in.at[pl.ds(first + low, high - low)], layer_face.at[pl.ds(low, high - low)], sems.at[1, p]
            ),
            pltpu.make_async_copy(areal_in.at[:, there], areal_face.at[:, here], sems.at[2, p]),
            pltpu.make_async_copy(right_in.at[:, there], right.at[:, here], sems.at[3, p]),
            pltpu.make_async_copy(pore_in.at[there], pore.at[here], sems.at[4, p]),
        ])
    for group in arrivals:
        for copy in group:
            copy.start()
    for c in range(3):
        state[c, 0 if h == 0 else half + 1] = z_face[c]

    def layer(i, carry):
        z = first + i
        m = [[coef[3 * r + c, pl.ds(z, 1), :] for c in range(3)] for r in range(3)]
        k = [[coef[9 + 3 * r + c, pl.ds(z, 1), :] for c in range(3)] for r in range(3)]
        weights = [layer_face[i + 1], layer_face[i]] + [areal_face[d, i] for d in range(4)]
        total = weights[0] + weights[1] + weights[2] + weights[3] + weights[4] + weights[5]
        cells, flux = [], []
        for c in range(3):
            u = state[c, i + 1]
            edges = jnp.concatenate(
                [pltpu.roll(xnear[c, h], 127 - 2 * tiles * i - 2 * t, 1) for t in range(tiles)], axis=0
            )
            near = (
                state[c, i + 2],
                state[c, i],
                jnp.where(rows == height - 1, yhi[c, pl.ds(z, 1), :], turn(u, -1, 0)),
                jnp.where(rows == 0, ylo[c, pl.ds(z, 1), :], turn(u, 1, 0)),
                jnp.where(lanes == width - 1, edges, turn(u, -1, 1)),
                jnp.where(lanes == 0, edges, turn(u, 1, 1)),
            )
            moved = weights[0] * (u - near[0])
            for w, n in zip(weights[1:], near[1:]):
                moved = moved + w * (u - n)
            cells.append(u)
            flux.append(moved)
        v = pore[i].astype(F32)
        residual = [
            right[r, i]
            - v * (m[r][0] * cells[0] + m[r][1] * cells[1] + m[r][2] * cells[2])
            - (k[r][0] * flux[0] + k[r][1] * flux[1] + k[r][2] * flux[2])
            for r in range(3)
        ]
        entries = [[v * m[r][c] + total * k[r][c] for c in range(3)] for r in range(3)]

        def cofactor(r, c):
            r1, r2, c1, c2 = (r + 1) % 3, (r + 2) % 3, (c + 1) % 3, (c + 2) % 3
            return entries[r1][c1] * entries[r2][c2] - entries[r1][c2] * entries[r2][c1]

        factors = [[cofactor(r, c) for c in range(3)] for r in range(3)]
        determinant = (
            entries[0][0] * factors[0][0] + entries[0][1] * factors[0][1] + entries[0][2] * factors[0][2]
        )
        scale = inverse(determinant)
        for r in range(3):
            base[r, i] = cells[r] + scale * (
                factors[0][r] * residual[0] + factors[1][r] * residual[1] + factors[2][r] * residual[2]
            )
            gain[r, i] = scale * (factors[0][r] * k[0][0] + factors[1][r] * k[1][0] + factors[2][r] * k[2][0])
        return carry

    departures = []
    for p in range(pieces):
        for copy in arrivals[p]:
            copy.wait()
        lax.fori_loop(p * CHUNK, (p + 1) * CHUNK, layer, 0)
        here = pl.ds(p * CHUNK, CHUNK)
        for n, (source, target) in enumerate(((base, base_out), (gain, gain_out))):
            copy = pltpu.make_async_copy(source.at[:, here], target.at[:, here], sems.at[5 + n, p])
            copy.start()
            departures.append(copy)
    for copy in departures:
        copy.wait()


def total_kernel(parts, total, strip):
    result = parts[0]
    for i in range(1, parts.shape[0]):
        result = result + parts[i]
    total[...] = result
    strip[...] = result[: strip.shape[0]]


def sweep_kernel(
    shares, base0, gain0, base1, gain1, layer_in, areal_in, new_state, correction,
    base, gain, layer_face, areal_face, result, plane, sems,
):
    _, depth, height, width = areal_face.shape
    tiles, half = height // 8, depth // 2
    lane = lane_index((8, 128))
    arrivals = []
    for p in range(depth // CHUNK):
        first = p * CHUNK
        here, there = pl.ds(first, CHUNK), pl.ds(first % half, CHUNK)
        low = 0 if p == 0 else first + 1
        layers = pl.ds(low, first + CHUNK + 1 - low)
        arrivals.append([
            pltpu.make_async_copy((base0 if first < half else base1).at[:, there], base.at[:, here], sems.at[1, p]),
            pltpu.make_async_copy((gain0 if first < half else gain1).at[:, there], gain.at[:, here], sems.at[2, p]),
            pltpu.make_async_copy(layer_in.at[layers], layer_face.at[layers], sems.at[3, p]),
            pltpu.make_async_copy(areal_in.at[:, here], areal_face.at[:, here], sems.at[4, p]),
        ])
    for group in arrivals:
        for copy in group:
            copy.start()

    def tile(k, t):
        return shares[k, 8 * t : 8 * t + 8, :]

    def side(right, right_at, left, left_at):
        right, left = turn(right, -right_at, 1), turn(left, width - 8 - left_at, 1)
        return jnp.where(lane < 8, right, jnp.where(lane >= width - 8, left, 0.0))

    planes = []
    for p in range(4):
        main = [tile(1, p)] + [tile(4 + p, 1 + t) for t in range(tiles - 1)] + [tile(p, 4), tile(0, p)]
        edge = [side(tile(7, 0), 8 * p, tile(5, 0), 8 * p)]
        for t in range(tiles):
            edge.append(side(tile(2, p), 8 * t, tile(3, p), 8 * t))
        edge.append(side(tile(4, 0), 8 * p, tile(6, 0), 8 * p))
        planes.append(
            jnp.concatenate([jnp.concatenate(main, axis=0), jnp.concatenate(edge, axis=0)], axis=1)
        )
    filled = planes[1] > 0.0
    scale = jnp.where(filled, RELAX / jnp.where(filled, planes[1], 1.0), 0.0)
    source = scale * planes[0]
    south = scale * planes[2]
    north = scale * turn(planes[2], 1, 0)
    east = scale * planes[3]
    west = scale * turn(planes[3], 1, 1)

    def around(field):
        return turn(field, -1, 0), turn(field, 1, 0), turn(field, -1, 1), turn(field, 1, 1)

    field = source
    for _ in range(SWEEPS - 1):
        s, n, e, w = around(field)
        field = ((1.0 - RELAX) * field + source) + (south * s + north * n) + (east * e + west * w)
    near = around(field)
    own = field[8 : 8 + height, 0:width]
    near = [n[8 : 8 + height, 0:width] for n in near]
    plane[...] = own
    copies = [pltpu.make_async_copy(plane, correction, sems.at[0, depth // CHUNK])]
    copies[0].start()

    for first in range(0, depth, CHUNK):
        for copy in arrivals[first // CHUNK]:
            copy.wait()

        def layer(z, carry):
            push = (layer_face[z] + layer_face[z + 1]) * own
            for d in range(4):
                push = push + areal_face[d, z] * near[d]
            for r in range(3):
                result[r, z] = base[r, z] + gain[r, z] * push
            return carry

        lax.fori_loop(first, first + CHUNK, layer, 0)
        copy = pltpu.make_async_copy(
            result.at[:, pl.ds(first, CHUNK)], new_state.at[:, pl.ds(first, CHUNK)], sems.at[0, first // CHUNK]
        )
        copy.start()
        copies.append(copy)
    for copy in copies:
        copy.wait()


def call(kernel, out_shape, in_specs, out_specs, scratch=(), flops=0, moved=0):
    return pl.pallas_call(
        kernel,
        out_shape=out_shape,
        in_specs=in_specs,
        out_specs=out_specs,
        scratch_shapes=list(scratch),
        compiler_params=PARAMS,
        cost_estimate=pl.CostEstimate(flops=flops, bytes_accessed=moved, transcendentals=0) if flops else None,
    )


def per_device(state, right_side, permeability, pore_volume, facies, storage_table, coupling_table):
    _, depth, height, width = state.shape
    columns = lax.axis_size("gz")
    row_of, rows = lax.axis_size("gx"), lax.axis_size("gy")
    block = (depth, height, width)
    bf16 = jnp.bfloat16
    storage_table, coupling_table = storage_table.transpose(1, 0, 2), coupling_table.transpose(1, 0, 2)

    state_v, right_v, perm_v, pore_v, coef, coef_lane, zlo, zhi, ylo, yhi, xpack = call(
        faces_kernel,
        [shape_of(3, *block), shape_of(*block), shape_of(*block), shape_of(*block)]
        + [shape_of(18, depth, 128), shape_of(3, 2, 8, 128)]
        + [shape_of(4, height, width)] * 2 + [shape_of(4, depth, width)] * 2 + [shape_of(4, 2, 8, 128)],
        hbm(7),
        vmem(11),
        [
            pltpu.VMEM(block, bf16),
            pltpu.VMEM(block, bf16),
            pltpu.SMEM(facies.shape, jnp.int32),
            pltpu.SMEM(storage_table.shape, F32),
            pltpu.SMEM(coupling_table.shape, F32),
            pltpu.SemaphoreType.DMA((6 + depth // CHUNK,)),
        ],
    )(*in_hbm(state, right_side, permeability, pore_volume, facies, storage_table, coupling_table))

    def from_next(first, axis):
        n = lax.axis_size(axis)
        return lax.ppermute(first, axis, [(i + 1, i) for i in range(n - 1)])

    def from_previous(last, axis):
        n = lax.axis_size(axis)
        return lax.ppermute(last, axis, [(i, i + 1) for i in range(n - 1)])

    around = []
    for axis, first, last in (("gz", zlo, zhi), ("gy", ylo, yhi), ("gx", xpack, xpack)):
        around += [from_previous(last, axis), from_next(first, axis)]
    zlo_near, zhi_near, ylo_near, yhi_near, xlo_near, xhi_near = around

    layer_face, areal_face, xnear, message = call(
        sums_kernel,
        [
            pltpu.HBM((depth + 1, height, width), F32),
            pltpu.HBM((4, *block), F32),
            shape_of(3, 2, 8, 128),
            shape_of(columns, 40, 128),
        ],
        vmem(15),
        hbm(2) + vmem(2),
        [
            pltpu.VMEM((6, height, width), F32),
            pltpu.VMEM((depth + 1, height, width), F32),
            pltpu.VMEM((4, *block), F32),
            pltpu.SemaphoreType.DMA((4,)),
        ],
    )(coef, coef_lane, state_v, right_v, perm_v, pore_v, ylo, yhi, xpack, *around)

    def cells(h, z_near, order):
        def kernel(*refs):
            cells_kernel(h, *refs)

        layers = depth // 2
        half = (layers, height, width)
        return call(
            kernel,
            [pltpu.HBM((3, *half), F32)] * 2,
            vmem(6) + hbm(5),
            hbm(2),
            [
                pltpu.VMEM((3, layers + 2, height, width), F32),
                pltpu.VMEM((3, *half), F32),
                pltpu.VMEM(half, bf16),
                pltpu.VMEM((layers + 1, height, width), F32),
                pltpu.VMEM((4, *half), F32),
                pltpu.VMEM((3, *half), F32),
                pltpu.VMEM((3, *half), F32),
                pltpu.SemaphoreType.DMA((7, layers // CHUNK)),
            ],
            flops=3 * 10**9,
            moved=3 * 10**6,
        )(coef, z_near, ylo_near, yhi_near, xnear, order, *in_hbm(state, right_side, pore_volume, layer_face, areal_face))

    parts = lax.all_to_all(message, "gz", 0, 0)
    base0, gain0 = cells(0, zlo_near, xnear)
    share, strip = call(total_kernel, [shape_of(40, 128), shape_of(32, 128)], vmem(1), vmem(2))(parts)
    pairs = []
    for x in range(row_of):
        for y in range(rows):
            for k, (dy, dx) in enumerate(DIRECTIONS):
                if 0 <= x + dx < row_of and 0 <= y + dy < rows:
                    pairs.append(
                        ((x * rows + y) * columns + k, ((x + dx) * rows + y + dy) * columns + k)
                    )
    strip = lax.ppermute(strip, ("gx", "gy", "gz"), pairs)
    base1, gain1 = cells(1, zhi_near, share)
    corner = lax.axis_index("gz") >= 4
    tile_row = lax.broadcasted_iota(jnp.int32, (40, 128), 0)
    take_strip = (tile_row < 8) | ((tile_row < 32) & jnp.logical_not(corner))
    padded = jnp.concatenate([strip, share[32:]], axis=0)
    merged = jnp.where(take_strip, padded, share)
    shares = lax.all_to_all(jnp.broadcast_to(merged[None], (columns, 40, 128)), "gz", 0, 0)

    new_state, correction = call(
        sweep_kernel,
        [pltpu.HBM((3, *block), F32), pltpu.HBM((height, width), F32)],
        vmem(1) + hbm(6),
        hbm(2),
        [
            pltpu.VMEM((3, *block), F32),
            pltpu.VMEM((3, *block), F32),
            pltpu.VMEM((depth + 1, height, width), F32),
            pltpu.VMEM((4, *block), F32),
            pltpu.VMEM((3, *block), F32),
            pltpu.VMEM((height, width), F32),
            pltpu.SemaphoreType.DMA((5, depth // CHUNK + 1)),
        ],
    )(shares, *in_hbm(base0, gain0, base1, gain1, layer_face, areal_face))
    return (new_state, correction)


def solution(mesh):
    return jax.shard_map(
        per_device,
        mesh=mesh,
        in_specs=(
            P(None, "gz", "gy", "gx"),
            P(None, "gz", "gy", "gx"),
            P("gz", "gy", "gx"),
            P("gz", "gy", "gx"),
            P("gz"),
            P(),
            P(),
        ),
        out_specs=(P(None, "gz", "gy", "gx"), P("gy", "gx")),
        check_vma=False,
    )
```

time: 69.2 us -> 61.3 us (0.89)
  the two profiles are of different devices: /device:TPU:232 before, /device:TPU:408 now
where the time goes in v2:
time: 61.3 us; the launch traced here: 60.7 us
  starting transfers between devices  28.4 us (46%)
  Pallas kernels  17 us (28%)
  waiting for transfers between devices  13.8 us (23%)
  between operations  0.76 us (1%)
  local copies, waits for them, and re-layouts  0.69 us (1%)
    ppermute x3, starting transfers between devices, from_next(): return lax.ppermute(first, axis, [(i + 1, i) for i in range(n - 1)])  8.07 us
    pallas_call x2, Pallas kernels, cells(): call(kernel, [pltpu.HBM((3, *half), F32)] * 2, vmem(6) + hbm(5), hbm(2),...  7.06 us
    all_to_all x1, starting transfers between devices, per_device(): parts = lax.all_to_all(message, 'gz', 0, 0)  6.84 us
    all_to_all x1, waiting for transfers between devices, per_device(): parts = lax.all_to_all(message, 'gz', 0, 0)  6.48 us
    ppermute x1, starting transfers between devices, per_device(): strip = lax.ppermute(strip, ('gx', 'gy', 'gz'), pairs)  5.13 us
    ppermute x3, starting transfers between devices, from_previous(): return lax.ppermute(last, axis, [(i, i + 1) for i in range(n - 1)])  4.96 us
    ppermute x3, waiting for transfers between devices, from_previous(): return lax.ppermute(last, axis, [(i, i + 1) for i in range(n - 1)])  4.51 us
    pallas_call x1, Pallas kernels, per_device(): call(sums_kernel, [pltpu.HBM((depth + 1, height, width), F32), pltpu.HBM(...  4.32 us
  transfers between devices with their start and end apart: 9, of which 4 were waited for; matrix products, arithmetic and copies ran while one was open for 0% of the time, Pallas kernels for 12%

profile of v2, /device:TPU:408, one launch (start us, length us, event | category | flops | bytes accessed | tf_op | source)
XLA Modules:
  0.0 60.7 jit_solution(14882069115621616470)
XLA Ops:
  0.6 1.8 %shard_map.86 = (f32[3,16,40,128]{3,2,1,0:T(8,128)S(1)}, f32[16,40,128]{2,1,0:T(8,128)S(1)}, f32[16,40,128]{2,1,0:T(8,128)S(1)}, f32[16,40,128]{2,1,0:T(8,128)S(...) custom-call(f32[3,16,40,128]{3,2,1,0:T(8,128)} %refs_6_.3, ...), custom_call_target="tpu_custom_call" | custom-call | tf_op jit(solution)/shard_map/pallas_call | solution.py:498
  2.5 1.7 %collective-permute-start = (f32[4,40,128]{2,1,0:T(8,128)S(1)}, f32[4,40,128]{2,1,0:T(8,128)S(1)}, u32[]{:S(2)}, u32[]{:S(2)}) collective-permute-start(f32[4,40,128]{2,1,0:T(8,128)S(1)} %get-tuple-element.32), channel_id=1, source_target_pairs={{0,1},{1,2},{2,3},{3,4},{4,5},{5,6},{6,7},{8,9},{9,10},{10,11},{11... | collective-permute-start | bytes 245768 | tf_op jit(solution)/shard_map/ppermute | solution.py:521
  4.2 1.3 %collective-permute-start.1 = (f32[4,40,128]{2,1,0:T(8,128)S(1)}, f32[4,40,128]{2,1,0:T(8,128)S(1)}, u32[]{:S(2)}, u32[]{:S(2)}) collective-permute-start(f32[4,40,128]{2,1,0:T(8,128)S(1)} %get-tuple-element.33), channel_id=1, source_target_pairs={{1,0},{2,1},{3,2},{4,3},{5,4},{6,5},{7,6},{9,8},{10,9},{11,10},{12... | collective-permute-start | bytes 245768 | tf_op jit(solution)/shard_map/ppermute | solution.py:517
  5.5 4.1 %collective-permute-start.3 = (f32[4,16,128]{2,1,0:T(8,128)S(1)}, f32[4,16,128]{2,1,0:T(8,128)S(1)}, u32[]{:S(2)}, u32[]{:S(2)}) collective-permute-start(f32[4,16,128]{2,1,0:T(8,128)S(1)} %get-tuple-element.29.ylo_own), channel_id=1, source_target_pairs={{8,0},{16,8},{24,16},{32,24},{40,32},{48,40},{56,48},{64,56},{72,6... | collective-permute-start | bytes 98312 | tf_op jit(solution)/shard_map/ppermute | solution.py:517
  9.6 1.9 %collective-permute-start.2 = (f32[4,16,128]{2,1,0:T(8,128)S(1)}, f32[4,16,128]{2,1,0:T(8,128)S(1)}, u32[]{:S(2)}, u32[]{:S(2)}) collective-permute-start(f32[4,16,128]{2,1,0:T(8,128)S(1)} %get-tuple-element.30.yhi_own), channel_id=1, source_target_pairs={{0,8},{8,16},{16,24},{24,32},{32,40},{40,48},{48,56},{56,64},{64,7... | collective-permute-start | bytes 98312 | tf_op jit(solution)/shard_map/ppermute | solution.py:521
  11.6 2.6 %collective-permute-start.5 = (f32[4,2,8,128]{3,2,1,0:T(8,128)S(1)}, f32[4,2,8,128]{3,2,1,0:T(8,128)S(1)}, u32[]{:S(2)}, u32[]{:S(2)}) collective-permute-start(f32[4,2,8,128]{3,2,1,0:T(8,128)S(1)} %get-tuple-element.31.xpack), channel_id=1, source_target_pairs={{128,0},{256,128},{384,256},{129,1},{257,129},{385,257},{130,2},{2... | collective-permute-start | bytes 98312 | tf_op jit(solution)/shard_map/ppermute | solution.py:517
  14.2 0.0 collective-permute-done.3.yhi.refs_3_
  14.2 1.3 %collective-permute-start.4 = (f32[4,2,8,128]{3,2,1,0:T(8,128)S(1)}, f32[4,2,8,128]{3,2,1,0:T(8,128)S(1)}, u32[]{:S(2)}, u32[]{:S(2)}) collective-permute-start(f32[4,2,8,128]{3,2,1,0:T(8,128)S(1)} %get-tuple-element.31.xpack), channel_id=1, source_target_pairs={{0,128},{128,256},{256,384},{1,129},{129,257},{257,385},{2,130},{1... | collective-permute-start | bytes 98312 | tf_op jit(solution)/shard_map/ppermute | solution.py:521
  15.5 1.1 %collective-permute-done.2.ylo.refs_2_ = f32[4,16,128]{2,1,0:T(8,128)S(1)} collective-permute-done((f32[4,16,128]{2,1,0:T(8,128)S(1)}, f32[4,16,128]{2,1,0:T(8,128)S(1)}, u32[]{:S(2)}, u32[]{:S(2)}) %collective-permute-start.2) | collective-permute-done | bytes 32800 | tf_op jit(solution)/shard_map/ppermute | solution.py:521
  16.7 0.0 collective-permute-done.5.xhi
  16.7 3.4 %collective-permute-done.4.xlo = f32[4,2,8,128]{3,2,1,0:T(8,128)S(1)} collective-permute-done((f32[4,2,8,128]{3,2,1,0:T(8,128)S(1)}, f32[4,2,8,128]{3,2,1,0:T(8,128)S(1)}, u32[]{:S(2)}, u32[]{:S(2)}) %collective-permute-start.4) | collective-permute-done | bytes 32800 | tf_op jit(solution)/shard_map/ppermute | solution.py:521
  20.0 0.0 collective-permute-done.zlo.refs_1_
  20.1 0.0 collective-permute-done.1.zhi.refs_1_
  20.1 4.3 %shard_map.87 = (f32[17,40,128]{2,1,0:T(8,128)}, f32[4,16,40,128]{3,2,1,0:T(8,128)}, f32[3,2,8,128]{3,2,1,0:T(8,128)S(1)}, f32[8,40,128]{2,1,0:T(8,128)}) custom-call(f32[18,16,128]{2,1,0:T(8,128)S(1)} %get-tuple-element.23.coef.refs_0_, f32[3,2,8,128]{3,2,1,0:T(8,128)S(1)} %get-tuple-element.24.coef_lane, f32[3,16,40,128]{3,2,1,0:T(8,128)S(1)} %get-tuple-element.25.state, ...), custom_call_target="tpu_custom_call" | custom-call | tf_op jit(solution)/shard_map/pallas_call | solution.py:528
  24.4 6.8 %all-to-all-start = ((f32[8,40,128]{2,1,0:T(8,128)}), f32[8,40,128]{2,1,0:T(8,128)S(1)}, u32[]{:S(2)}, u32[]{:S(2)}) async-start(f32[8,40,128]{2,1,0:T(8,128)} %get-tuple-element.34), calls=%async_computation | async-start | bytes 327680 | tf_op jit(solution)/shard_map/all_to_all | solution.py:571
  31.2 6.5 %all-to-all-done.parts = f32[8,40,128]{2,1,0:T(8,128)S(1)} async-done(((f32[8,40,128]{2,1,0:T(8,128)}), f32[8,40,128]{2,1,0:T(8,128)S(1)}, u32[]{:S(2)}, u32[]{:S(2)}) %all-to-all-start) | async-done | bytes 163872 | tf_op jit(solution)/shard_map/all_to_all | solution.py:571
  37.7 5.1 %collective-permute-start.6 = (f32[32,128]{1,0:T(8,128)S(1)}, f32[32,128]{1,0:T(8,128)S(1)}, u32[]{:S(2)}, u32[]{:S(2)}) collective-permute-start(f32[32,128]{1,0:T(8,128)S(1)} %get-tuple-element.35), channel_id=1, source_target_pairs={{1,9},{3,131},{5,141},{8,0},{9,17},{11,139},{13,149},{14,134},{16,... | collective-permute-start | bytes 49160 | tf_op jit(solution)/shard_map/ppermute | solution.py:582
  42.9 3.5 %shard_map.89 = (f32[3,8,40,128]{3,2,1,0:T(8,128)}, f32[3,8,40,128]{3,2,1,0:T(8,128)}) custom-call(f32[18,16,128]{2,1,0:T(8,128)S(1)} %get-tuple-element.23.coef.refs_0_, f32[4,40,128]{2,1,0:T(8,128)S(1)} %collective-permute-done.zlo.refs_1_, f32[4,16,128]{2,1,0:T(8,128)S(1)} %collective-permute-done.2.ylo.refs_2_, ...), custom_call_target="tpu_custom_call" | custom-call | flops 3000000000 | bytes 3000000 | tf_op jit(solution)/shard_map/pallas_call | solution.py:552
  46.4 0.0 collective-permute-done.6
  46.4 0.1 maximum_select_fusion
  46.5 0.7 %broadcast_in_dim.2 = f32[8,40,128]{2,1,0:T(8,128)} broadcast(f32[40,128]{1,0:T(8,128)S(1)} %maximum_select_fusion), dimensions={1,2} | broadcast | bytes 184320 | tf_op jit(solution)/shard_map/broadcast_in_dim | solution.py:589
  47.1 3.4 %all-to-all-start.1 = ((f32[8,40,128]{2,1,0:T(8,128)}), f32[8,40,128]{2,1,0:T(8,128)S(1)}, u32[]{:S(2)}, u32[]{:S(2)}) async-start(f32[8,40,128]{2,1,0:T(8,128)} %broadcast_in_dim.2), calls=%async_computation.1 | async-start | bytes 327680 | tf_op jit(solution)/shard_map/all_to_all | solution.py:589
  50.5 3.6 %shard_map.90 = (f32[3,8,40,128]{3,2,1,0:T(8,128)}, f32[3,8,40,128]{3,2,1,0:T(8,128)}) custom-call(f32[18,16,128]{2,1,0:T(8,128)S(1)} %get-tuple-element.23.coef.refs_0_, f32[4,40,128]{2,1,0:T(8,128)S(1)} %collective-permute-done.1.zhi.refs_1_, f32[4,16,128]{2,1,0:T(8,128)S(1)} %collective-permute-done.2.ylo.refs_2_, ...), custom_call_target="tpu_custom_call" | custom-call | flops 3000000000 | bytes 3000000 | tf_op jit(solution)/shard_map/pallas_call | solution.py:552
  54.1 2.8 %all-to-all-done.1.shares = f32[8,40,128]{2,1,0:T(8,128)S(1)} async-done(((f32[8,40,128]{2,1,0:T(8,128)}), f32[8,40,128]{2,1,0:T(8,128)S(1)}, u32[]{:S(2)}, u32[]{:S(2)}) %all-to-all-start.1) | async-done | bytes 163872 | tf_op jit(solution)/shard_map/all_to_all | solution.py:589
  56.9 3.8 %shard_map.91 = (f32[3,16,40,128]{3,2,1,0:T(8,128)}, f32[40,128]{1,0:T(8,128)}) custom-call(f32[8,40,128]{2,1,0:T(8,128)S(1)} %all-to-all-done.1.shares, f32[3,8,40,128]{3,2,1,0:T(8,128)} %get-tuple-element.40.base0, f32[3,8,40,128]{3,2,1,0:T(8,128)} %get-tuple-element.41.gain0, f32[3,8,40,128]{3,2,1,0:T(8,128)} %get-tuple-element.42.base1, ...), custom_call_target="tpu_custom_call" | custom-call | tf_op jit(solution)/shard_map/pallas_call | solution.py:591
  (3 shorter events, 0.0 us)
Async XLA Ops:
  2.5 17.6 %collective-permute-start = (f32[4,40,128]{2,1,0:T(8,128)S(1)}, f32[4,40,128]{2,1,0:T(8,128)S(1)}, u32[]{:S(2)}, u32[]{:S(2)}) collective-permute-start(f32[4,40,128]{2,1,0:T(8,128)S(1)} %get-tuple-element.32), channel_id=1, source_target_pairs={{0,1},{1,2},{2,3},{3,4},{4,5},{5,6},{6,7},{8,9},{9,10},{10,11},{11... | collective-permute-start | bytes 245768 | tf_op jit(solution)/shard_map/ppermute | solution.py:521
  4.2 15.8 %collective-permute-start.1 = (f32[4,40,128]{2,1,0:T(8,128)S(1)}, f32[4,40,128]{2,1,0:T(8,128)S(1)}, u32[]{:S(2)}, u32[]{:S(2)}) collective-permute-start(f32[4,40,128]{2,1,0:T(8,128)S(1)} %get-tuple-element.33), channel_id=1, source_target_pairs={{1,0},{2,1},{3,2},{4,3},{5,4},{6,5},{7,6},{9,8},{10,9},{11,10},{12... | collective-permute-start | bytes 245768 | tf_op jit(solution)/shard_map/ppermute | solution.py:517
  5.5 8.7 %collective-permute-start.3 = (f32[4,16,128]{2,1,0:T(8,128)S(1)}, f32[4,16,128]{2,1,0:T(8,128)S(1)}, u32[]{:S(2)}, u32[]{:S(2)}) collective-permute-start(f32[4,16,128]{2,1,0:T(8,128)S(1)} %get-tuple-element.29.ylo_own), channel_id=1, source_target_pairs={{8,0},{16,8},{24,16},{32,24},{40,32},{48,40},{56,48},{64,56},{72,6... | collective-permute-start | bytes 98312 | tf_op jit(solution)/shard_map/ppermute | solution.py:517
  9.6 7.0 %collective-permute-start.2 = (f32[4,16,128]{2,1,0:T(8,128)S(1)}, f32[4,16,128]{2,1,0:T(8,128)S(1)}, u32[]{:S(2)}, u32[]{:S(2)}) collective-permute-start(f32[4,16,128]{2,1,0:T(8,128)S(1)} %get-tuple-element.30.yhi_own), channel_id=1, source_target_pairs={{0,8},{8,16},{16,24},{24,32},{32,40},{40,48},{48,56},{56,64},{64,7... | collective-permute-start | bytes 98312 | tf_op jit(solution)/shard_map/ppermute | solution.py:521
  11.6 5.1 %collective-permute-start.5 = (f32[4,2,8,128]{3,2,1,0:T(8,128)S(1)}, f32[4,2,8,128]{3,2,1,0:T(8,128)S(1)}, u32[]{:S(2)}, u32[]{:S(2)}) collective-permute-start(f32[4,2,8,128]{3,2,1,0:T(8,128)S(1)} %get-tuple-element.31.xpack), channel_id=1, source_target_pairs={{128,0},{256,128},{384,256},{129,1},{257,129},{385,257},{130,2},{2... | collective-permute-start | bytes 98312 | tf_op jit(solution)/shard_map/ppermute | solution.py:517
  14.2 5.8 %collective-permute-start.4 = (f32[4,2,8,128]{3,2,1,0:T(8,128)S(1)}, f32[4,2,8,128]{3,2,1,0:T(8,128)S(1)}, u32[]{:S(2)}, u32[]{:S(2)}) collective-permute-start(f32[4,2,8,128]{3,2,1,0:T(8,128)S(1)} %get-tuple-element.31.xpack), channel_id=1, source_target_pairs={{0,128},{128,256},{256,384},{1,129},{129,257},{257,385},{2,130},{1... | collective-permute-start | bytes 98312 | tf_op jit(solution)/shard_map/ppermute | solution.py:521
  24.4 13.3 %all-to-all-start = ((f32[8,40,128]{2,1,0:T(8,128)}), f32[8,40,128]{2,1,0:T(8,128)S(1)}, u32[]{:S(2)}, u32[]{:S(2)}) async-start(f32[8,40,128]{2,1,0:T(8,128)} %get-tuple-element.34), calls=%async_computation | async-start | bytes 327680 | tf_op jit(solution)/shard_map/all_to_all | solution.py:571
  37.7 8.7 %collective-permute-start.6 = (f32[32,128]{1,0:T(8,128)S(1)}, f32[32,128]{1,0:T(8,128)S(1)}, u32[]{:S(2)}, u32[]{:S(2)}) collective-permute-start(f32[32,128]{1,0:T(8,128)S(1)} %get-tuple-element.35), channel_id=1, source_target_pairs={{1,9},{3,131},{5,141},{8,0},{9,17},{11,139},{13,149},{14,134},{16,... | collective-permute-start | bytes 49160 | tf_op jit(solution)/shard_map/ppermute | solution.py:582
  47.1 9.8 %all-to-all-start.1 = ((f32[8,40,128]{2,1,0:T(8,128)}), f32[8,40,128]{2,1,0:T(8,128)S(1)}, u32[]{:S(2)}, u32[]{:S(2)}) async-start(f32[8,40,128]{2,1,0:T(8,128)} %broadcast_in_dim.2), calls=%async_computation.1 | async-start | bytes 327680 | tf_op jit(solution)/shard_map/all_to_all | solution.py:589

commit v3 on v2

--- a/solution.py
+++ b/solution.py
@@ -130,8 +130,8 @@
 
 def sums_kernel(
     coef, coef_lane, state, right, perm, pore, ylo_own, yhi_own, xpack, zlo, zhi, ylo, yhi, xlo, xhi,
-    layer_out, areal_out, xnear, message,
-    acc, layer_face, areal_face, sems,
+    layer_face, areal_face, xnear, message,
+    acc,
 ):
     depth, height, width = perm.shape
     tiles, half = height // 8, depth // 2
@@ -214,16 +214,6 @@
         areal_face[0, z, 0:1, :] = south[z : z + 1]
         areal_face[1, z, 0:1, :] = north[z : z + 1]
 
-    def keep(h):
-        tops, all_areal = pl.ds(h * (half + 1), half + 1 - h), pl.ds(h * half, half)
-        copies = [
-            pltpu.make_async_copy(layer_face.at[tops], layer_out.at[tops], sems.at[2 * h]),
-            pltpu.make_async_copy(areal_face.at[:, all_areal], areal_out.at[:, all_areal], sems.at[2 * h + 1]),
-        ]
-        for copy in copies:
-            copy.start()
-        return copies
-
     for h in range(2):
 
         def body(z, carry, h=h):
@@ -232,13 +222,10 @@
             layer(z, below, step, side[h], 127 - 2 * tiles * (z - h * half))
             return carry
 
-        lax.fori_loop(h * half, half if h == 0 else depth - 1, body, 0)
-        if h == 0:
-            copies = keep(0)
+        lax.fori_loop(h * half, half if h == 0 else depth - 1, body, 0, unroll=True)
     z = depth - 1
     layer(z, [zhi[c] for c in range(4)], [row_of(9 + c, z) for c in range(3)], side[1], 127 - 2 * tiles * (half - 1))
 
-    copies += keep(1)
     rhs, diag, ty, tx = acc[0], acc[1], acc[2], acc[3]
     fy, fx = acc[4], acc[5]
     edge_sum = jnp.concatenate([turn(side_sum, 127 - 2 * t, 1) for t in range(tiles)], axis=0)
@@ -279,14 +266,12 @@
         for t in range(4):
             message[4 + k, 8 + 8 * t : 16 + 8 * t, :] = tile(k, t)
         message[k, 32:40, :] = tile(k, last)
-    for copy in copies:
-        copy.wait()
 
 
 def cells_kernel(
-    h, coef, z_face, ylo, yhi, xnear, order, state_in, right_in, pore_in, layer_in, areal_in,
+    h, coef, z_face, ylo, yhi, xnear, order, layer_face, areal_face, state_in, right_in, pore_in,
     base_out, gain_out,
-    state, right, pore, layer_face, areal_face, base, gain, sems,
+    state, right, pore, base, gain, sems,
 ):
     del order
     half, height, width = pore.shape
@@ -296,7 +281,6 @@
     arrivals = []
     for p in range(pieces):
         here, there = pl.ds(p * CHUNK, CHUNK), pl.ds(first + p * CHUNK, CHUNK)
-        low, high = (0 if p == 0 else p * CHUNK + 1), (p + 1) * CHUNK + 1
         state_low = 1 if p == 0 and h == 0 else (0 if p == 0 else p * CHUNK + 2)
         state_high = (p + 1) * CHUNK + (1 if p == pieces - 1 and h == 1 else 2)
         z_low = first - 1 + state_low
@@ -306,12 +290,8 @@
                 state.at[:, pl.ds(state_low, state_high - state_low)],
                 sems.at[0, p],
             ),
-            pltpu.make_async_copy(
-                layer_in.at[pl.ds(first + low, high - low)], layer_face.at[pl.ds(low, high - low)], sems.at[1, p]
-            ),
-            pltpu.make_async_copy(areal_in.at[:, there], areal_face.at[:, here], sems.at[2, p]),
-            pltpu.make_async_copy(right_in.at[:, there], right.at[:, here], sems.at[3, p]),
-            pltpu.make_async_copy(pore_in.at[there], pore.at[here], sems.at[4, p]),
+            pltpu.make_async_copy(right_in.at[:, there], right.at[:, here], sems.at[1, p]),
+            pltpu.make_async_copy(pore_in.at[there], pore.at[here], sems.at[2, p]),
         ])
     for group in arrivals:
         for copy in group:
@@ -323,7 +303,7 @@
         z = first + i
         m = [[coef[3 * r + c, pl.ds(z, 1), :] for c in range(3)] for r in range(3)]
         k = [[coef[9 + 3 * r + c, pl.ds(z, 1), :] for c in range(3)] for r in range(3)]
-        weights = [layer_face[i + 1], layer_face[i]] + [areal_face[d, i] for d in range(4)]
+        weights = [layer_face[z + 1], layer_face[z]] + [areal_face[d, z] for d in range(4)]
         total = weights[0] + weights[1] + weights[2] + weights[3] + weights[4] + weights[5]
         cells, flux = [], []
         for c in range(3):
@@ -373,10 +353,10 @@
     for p in range(pieces):
         for copy in arrivals[p]:
             copy.wait()
-        lax.fori_loop(p * CHUNK, (p + 1) * CHUNK, layer, 0)
+        lax.fori_loop(p * CHUNK, (p + 1) * CHUNK, layer, 0, unroll=True)
         here = pl.ds(p * CHUNK, CHUNK)
         for n, (source, target) in enumerate(((base, base_out), (gain, gain_out))):
-            copy = pltpu.make_async_copy(source.at[:, here], target.at[:, here], sems.at[5 + n, p])
+            copy = pltpu.make_async_copy(source.at[:, here], target.at[:, here], sems.at[3 + n, p])
             copy.start()
             departures.append(copy)
     for copy in departures:
@@ -391,9 +371,23 @@
     strip[...] = result[: strip.shape[0]]
 
 
+def merge_kernel(corner, strip, share, copies):
+    at_corner = corner[...] > 0
+    for t in range(5):
+        cells = slice(8 * t, 8 * t + 8)
+        if t == 0:
+            merged = strip[cells]
+        elif t == 4:
+            merged = share[cells]
+        else:
+            merged = jnp.where(at_corner, share[cells], strip[cells])
+        for k in range(copies.shape[0]):
+            copies[k, cells, :] = merged
+
+
 def sweep_kernel(
-    shares, base0, gain0, base1, gain1, layer_in, areal_in, new_state, correction,
-    base, gain, layer_face, areal_face, result, plane, sems,
+    shares, layer_face, areal_face, base0, gain0, base1, gain1, new_state, correction,
+    base, gain, result, plane, sems,
 ):
     _, depth, height, width = areal_face.shape
     tiles, half = height // 8, depth // 2
@@ -402,13 +396,9 @@
     for p in range(depth // CHUNK):
         first = p * CHUNK
         here, there = pl.ds(first, CHUNK), pl.ds(first % half, CHUNK)
-        low = 0 if p == 0 else first + 1
-        layers = pl.ds(low, first + CHUNK + 1 - low)
         arrivals.append([
             pltpu.make_async_copy((base0 if first < half else base1).at[:, there], base.at[:, here], sems.at[1, p]),
             pltpu.make_async_copy((gain0 if first < half else gain1).at[:, there], gain.at[:, here], sems.at[2, p]),
-            pltpu.make_async_copy(layer_in.at[layers], layer_face.at[layers], sems.at[3, p]),
-            pltpu.make_async_copy(areal_in.at[:, here], areal_face.at[:, here], sems.at[4, p]),
         ])
     for group in arrivals:
         for copy in group:
@@ -465,7 +455,7 @@
                 result[r, z] = base[r, z] + gain[r, z] * push
             return carry
 
-        lax.fori_loop(first, first + CHUNK, layer, 0)
+        lax.fori_loop(first, first + CHUNK, layer, 0, unroll=True)
         copy = pltpu.make_async_copy(
             result.at[:, pl.ds(first, CHUNK)], new_state.at[:, pl.ds(first, CHUNK)], sems.at[0, first // CHUNK]
         )
@@ -528,19 +518,14 @@
     layer_face, areal_face, xnear, message = call(
         sums_kernel,
         [
-            pltpu.HBM((depth + 1, height, width), F32),
-            pltpu.HBM((4, *block), F32),
+            shape_of(depth + 1, height, width),
+            shape_of(4, *block),
             shape_of(3, 2, 8, 128),
             shape_of(columns, 40, 128),
         ],
         vmem(15),
-        hbm(2) + vmem(2),
-        [
-            pltpu.VMEM((6, height, width), F32),
-            pltpu.VMEM((depth + 1, height, width), F32),
-            pltpu.VMEM((4, *block), F32),
-            pltpu.SemaphoreType.DMA((4,)),
-        ],
+        vmem(4),
+        [pltpu.VMEM((6, height, width), F32)],
     )(coef, coef_lane, state_v, right_v, perm_v, pore_v, ylo, yhi, xpack, *around)
 
     def cells(h, z_near, order):
@@ -552,21 +537,22 @@
         return call(
             kernel,
             [pltpu.HBM((3, *half), F32)] * 2,
-            vmem(6) + hbm(5),
+            vmem(8) + hbm(3),
             hbm(2),
             [
                 pltpu.VMEM((3, layers + 2, height, width), F32),
                 pltpu.VMEM((3, *half), F32),
                 pltpu.VMEM(half, bf16),
-                pltpu.VMEM((layers + 1, height, width), F32),
-                pltpu.VMEM((4, *half), F32),
                 pltpu.VMEM((3, *half), F32),
                 pltpu.VMEM((3, *half), F32),
-                pltpu.SemaphoreType.DMA((7, layers // CHUNK)),
+                pltpu.SemaphoreType.DMA((5, layers // CHUNK)),
             ],
             flops=3 * 10**9,
             moved=3 * 10**6,
-        )(coef, z_near, ylo_near, yhi_near, xnear, order, *in_hbm(state, right_side, pore_volume, layer_face, areal_face))
+        )(
+            coef, z_near, ylo_near, yhi_near, xnear, order, layer_face, areal_face,
+            *in_hbm(state, right_side, pore_volume),
+        )
 
     parts = lax.all_to_all(message, "gz", 0, 0)
     base0, gain0 = cells(0, zlo_near, xnear)
@@ -581,28 +567,23 @@
                     )
     strip = lax.ppermute(strip, ("gx", "gy", "gz"), pairs)
     base1, gain1 = cells(1, zhi_near, share)
-    corner = lax.axis_index("gz") >= 4
-    tile_row = lax.broadcasted_iota(jnp.int32, (40, 128), 0)
-    take_strip = (tile_row < 8) | ((tile_row < 32) & jnp.logical_not(corner))
-    padded = jnp.concatenate([strip, share[32:]], axis=0)
-    merged = jnp.where(take_strip, padded, share)
-    shares = lax.all_to_all(jnp.broadcast_to(merged[None], (columns, 40, 128)), "gz", 0, 0)
+    corner = jnp.broadcast_to((lax.axis_index("gz") >= 4).astype(jnp.int32), (8, 128))
+    copies = call(merge_kernel, shape_of(columns, 40, 128), vmem(3), vmem(1)[0])(corner, strip, share)
+    shares = lax.all_to_all(copies, "gz", 0, 0)
 
     new_state, correction = call(
         sweep_kernel,
         [pltpu.HBM((3, *block), F32), pltpu.HBM((height, width), F32)],
-        vmem(1) + hbm(6),
+        vmem(3) + hbm(4),
         hbm(2),
         [
             pltpu.VMEM((3, *block), F32),
             pltpu.VMEM((3, *block), F32),
-            pltpu.VMEM((depth + 1, height, width), F32),
-            pltpu.VMEM((4, *block), F32),
             pltpu.VMEM((3, *block), F32),
             pltpu.VMEM((height, width), F32),
-            pltpu.SemaphoreType.DMA((5, depth // CHUNK + 1)),
+            pltpu.SemaphoreType.DMA((3, depth // CHUNK + 1)),
         ],
-    )(shares, *in_hbm(base0, gain0, base1, gain1, layer_face, areal_face))
+    )(shares, layer_face, areal_face, *in_hbm(base0, gain0, base1, gain1))
     return (new_state, correction)
 
 

time: 61.3 us -> 58 us (0.946)
  Pallas kernels: 17 us -> 14.2 us
  local copies, waits for them, and re-layouts: 0.69 us -> 0.01 us
    pallas_call x3 -> x4, Pallas kernels: 11.4 us -> 9.18 us  [the longest x2 6.46 us: cells(): call(kernel, [pltpu.HBM((3, *half), F32)] * 2, vmem(8) + hbm(3), hbm(2),...]
    broadcast_in_dim x1, local copies, waits for them, and re-layouts: 0.68 us -> 0.01 us  [per_device(): jnp.broadcast_to((lax.axis_index('gz') >= 4).astype(jnp.int32), (8, 128))]
  transfers between devices with their start and end apart: 9 -> 9, of which waited for: 4 -> 4; matrix products, arithmetic and copies ran while one was open for 0% -> 0% of each run, Pallas kernels for 12% -> 11%
where the time goes in v3:
time: 58 us; the launch traced here: 57.5 us
  starting transfers between devices  28.4 us (49%)
  Pallas kernels  14.2 us (24%)
  waiting for transfers between devices  14.2 us (24%)
  between operations  0.75 us (1%)
    ppermute x3, starting transfers between devices, from_next(): return lax.ppermute(first, axis, [(i + 1, i) for i in range(n - 1)])  8.07 us
    all_to_all x1, starting transfers between devices, per_device(): parts = lax.all_to_all(message, 'gz', 0, 0)  6.83 us
    all_to_all x1, waiting for transfers between devices, per_device(): parts = lax.all_to_all(message, 'gz', 0, 0)  6.49 us
    pallas_call x2, Pallas kernels, cells(): call(kernel, [pltpu.HBM((3, *half), F32)] * 2, vmem(8) + hbm(3), hbm(2),...  6.46 us
    ppermute x1, starting transfers between devices, per_device(): strip = lax.ppermute(strip, ('gx', 'gy', 'gz'), pairs)  5.13 us
    ppermute x3, starting transfers between devices, from_previous(): return lax.ppermute(last, axis, [(i, i + 1) for i in range(n - 1)])  4.96 us
    ppermute x3, waiting for transfers between devices, from_previous(): return lax.ppermute(last, axis, [(i, i + 1) for i in range(n - 1)])  4.51 us
    all_to_all x1, starting transfers between devices, per_device(): shares = lax.all_to_all(copies, 'gz', 0, 0)  3.38 us
  transfers between devices with their start and end apart: 9, of which 4 were waited for; matrix products, arithmetic and copies ran while one was open for 0% of the time, Pallas kernels for 11%

profile of v3, /device:TPU:408, one launch (start us, length us, event | category | flops | bytes accessed | tf_op | source)
XLA Modules:
  0.0 57.5 jit_solution(11259338104300929181)
XLA Ops:
  0.6 1.8 %shard_map.86 = (f32[3,16,40,128]{3,2,1,0:T(8,128)S(1)}, f32[16,40,128]{2,1,0:T(8,128)S(1)}, f32[16,40,128]{2,1,0:T(8,128)S(1)}, f32[16,40,128]{2,1,0:T(8,128)S(...) custom-call(f32[3,16,40,128]{3,2,1,0:T(8,128)} %refs_8_.3, ...), custom_call_target="tpu_custom_call" | custom-call | tf_op jit(solution)/shard_map/pallas_call | solution.py:488
  2.5 1.7 %collective-permute-start = (f32[4,40,128]{2,1,0:T(8,128)S(1)}, f32[4,40,128]{2,1,0:T(8,128)S(1)}, u32[]{:S(2)}, u32[]{:S(2)}) collective-permute-start(f32[4,40,128]{2,1,0:T(8,128)S(1)} %get-tuple-element.32), channel_id=1, source_target_pairs={{0,1},{1,2},{2,3},{3,4},{4,5},{5,6},{6,7},{8,9},{9,10},{10,11},{11... | collective-permute-start | bytes 245768 | tf_op jit(solution)/shard_map/ppermute | solution.py:511
  4.2 1.3 %collective-permute-start.1 = (f32[4,40,128]{2,1,0:T(8,128)S(1)}, f32[4,40,128]{2,1,0:T(8,128)S(1)}, u32[]{:S(2)}, u32[]{:S(2)}) collective-permute-start(f32[4,40,128]{2,1,0:T(8,128)S(1)} %get-tuple-element.33), channel_id=1, source_target_pairs={{1,0},{2,1},{3,2},{4,3},{5,4},{6,5},{7,6},{9,8},{10,9},{11,10},{12... | collective-permute-start | bytes 245768 | tf_op jit(solution)/shard_map/ppermute | solution.py:507
  5.5 4.1 %collective-permute-start.3 = (f32[4,16,128]{2,1,0:T(8,128)S(1)}, f32[4,16,128]{2,1,0:T(8,128)S(1)}, u32[]{:S(2)}, u32[]{:S(2)}) collective-permute-start(f32[4,16,128]{2,1,0:T(8,128)S(1)} %get-tuple-element.29.ylo_own), channel_id=1, source_target_pairs={{8,0},{16,8},{24,16},{32,24},{40,32},{48,40},{56,48},{64,56},{72,6... | collective-permute-start | bytes 98312 | tf_op jit(solution)/shard_map/ppermute | solution.py:507
  9.6 1.9 %collective-permute-start.2 = (f32[4,16,128]{2,1,0:T(8,128)S(1)}, f32[4,16,128]{2,1,0:T(8,128)S(1)}, u32[]{:S(2)}, u32[]{:S(2)}) collective-permute-start(f32[4,16,128]{2,1,0:T(8,128)S(1)} %get-tuple-element.30.yhi_own), channel_id=1, source_target_pairs={{0,8},{8,16},{16,24},{24,32},{32,40},{40,48},{48,56},{56,64},{64,7... | collective-permute-start | bytes 98312 | tf_op jit(solution)/shard_map/ppermute | solution.py:511
  11.6 2.6 %collective-permute-start.5 = (f32[4,2,8,128]{3,2,1,0:T(8,128)S(1)}, f32[4,2,8,128]{3,2,1,0:T(8,128)S(1)}, u32[]{:S(2)}, u32[]{:S(2)}) collective-permute-start(f32[4,2,8,128]{3,2,1,0:T(8,128)S(1)} %get-tuple-element.31.xpack), channel_id=1, source_target_pairs={{128,0},{256,128},{384,256},{129,1},{257,129},{385,257},{130,2},{2... | collective-permute-start | bytes 98312 | tf_op jit(solution)/shard_map/ppermute | solution.py:507
  14.2 0.0 collective-permute-done.3.yhi.refs_3_
  14.2 1.3 %collective-permute-start.4 = (f32[4,2,8,128]{3,2,1,0:T(8,128)S(1)}, f32[4,2,8,128]{3,2,1,0:T(8,128)S(1)}, u32[]{:S(2)}, u32[]{:S(2)}) collective-permute-start(f32[4,2,8,128]{3,2,1,0:T(8,128)S(1)} %get-tuple-element.31.xpack), channel_id=1, source_target_pairs={{0,128},{128,256},{256,384},{1,129},{129,257},{257,385},{2,130},{1... | collective-permute-start | bytes 98312 | tf_op jit(solution)/shard_map/ppermute | solution.py:511
  15.5 1.1 %collective-permute-done.2.ylo.refs_2_ = f32[4,16,128]{2,1,0:T(8,128)S(1)} collective-permute-done((f32[4,16,128]{2,1,0:T(8,128)S(1)}, f32[4,16,128]{2,1,0:T(8,128)S(1)}, u32[]{:S(2)}, u32[]{:S(2)}) %collective-permute-start.2) | collective-permute-done | bytes 32800 | tf_op jit(solution)/shard_map/ppermute | solution.py:511
  16.7 0.0 collective-permute-done.5.xhi
  16.7 3.4 %collective-permute-done.4.xlo = f32[4,2,8,128]{3,2,1,0:T(8,128)S(1)} collective-permute-done((f32[4,2,8,128]{3,2,1,0:T(8,128)S(1)}, f32[4,2,8,128]{3,2,1,0:T(8,128)S(1)}, u32[]{:S(2)}, u32[]{:S(2)}) %collective-permute-start.4) | collective-permute-done | bytes 32800 | tf_op jit(solution)/shard_map/ppermute | solution.py:511
  20.0 0.0 collective-permute-done.zlo.refs_1_
  20.1 0.0 collective-permute-done.1.zhi.refs_1_
  20.1 2.0 %shard_map.87 = (f32[17,40,128]{2,1,0:T(8,128)S(1)}, f32[4,16,40,128]{3,2,1,0:T(8,128)S(1)}, f32[3,2,8,128]{3,2,1,0:T(8,128)S(1)}, f32[8,40,128]{2,1,0:T(8,128)}) custom-call(f32[18,16,128]{2,1,0:T(8,128)S(1)} %get-tuple-element.23.coef.refs_0_, f32[3,2,8,128]{3,2,1,0:T(8,128)S(1)} %get-tuple-element.24.coef_lane, ...), custom_call_target="tpu_custom_call" | custom-call | tf_op jit(solution)/shard_map/pallas_call | solution.py:518
  22.1 6.8 %all-to-all-start = ((f32[8,40,128]{2,1,0:T(8,128)}), f32[8,40,128]{2,1,0:T(8,128)S(1)}, u32[]{:S(2)}, u32[]{:S(2)}) async-start(f32[8,40,128]{2,1,0:T(8,128)} %get-tuple-element.34), calls=%async_computation | async-start | bytes 327680 | tf_op jit(solution)/shard_map/all_to_all | solution.py:557
  28.9 6.5 %all-to-all-done.parts = f32[8,40,128]{2,1,0:T(8,128)S(1)} async-done(((f32[8,40,128]{2,1,0:T(8,128)}), f32[8,40,128]{2,1,0:T(8,128)S(1)}, u32[]{:S(2)}, u32[]{:S(2)}) %all-to-all-start) | async-done | bytes 163872 | tf_op jit(solution)/shard_map/all_to_all | solution.py:557
  35.4 5.1 %collective-permute-start.6 = (f32[32,128]{1,0:T(8,128)S(1)}, f32[32,128]{1,0:T(8,128)S(1)}, u32[]{:S(2)}, u32[]{:S(2)}) collective-permute-start(f32[32,128]{1,0:T(8,128)S(1)} %get-tuple-element.35), channel_id=1, source_target_pairs={{1,9},{3,131},{5,141},{8,0},{9,17},{11,139},{13,149},{14,134},{16,... | collective-permute-start | bytes 49160 | tf_op jit(solution)/shard_map/ppermute | solution.py:568
  40.6 3.2 %shard_map.90 = (f32[3,8,40,128]{3,2,1,0:T(8,128)}, f32[3,8,40,128]{3,2,1,0:T(8,128)}) custom-call(f32[18,16,128]{2,1,0:T(8,128)S(1)} %get-tuple-element.23.coef.refs_0_, f32[4,40,128]{2,1,0:T(8,128)S(1)} %collective-permute-done.zlo.refs_1_, f32[4,16,128]{2,1,0:T(8,128)S(1)} %collective-permute-done.2.ylo.refs_2_, ...), custom_call_target="tpu_custom_call" | custom-call | flops 3000000000 | bytes 3000000 | tf_op jit(solution)/shard_map/pallas_call | solution.py:537
  43.8 0.0 collective-permute-done.6.strip
  43.8 0.7 %shard_map.89 = f32[8,40,128]{2,1,0:T(8,128)} custom-call(s32[8,128]{1,0:T(8,128)S(1)} %broadcast_in_dim.3.corner, f32[32,128]{1,0:T(8,128)S(1)} %collective-permute-done.6.strip, f32[40,128]{1,0:T(8,128)S(1)} %get-tuple-element.36.share.refs_5_), custom_call_target="tpu_custom_call" | custom-call | tf_op jit(solution)/shard_map/pallas_call | solution.py:571
  44.5 3.4 %all-to-all-start.1 = ((f32[8,40,128]{2,1,0:T(8,128)}), f32[8,40,128]{2,1,0:T(8,128)S(1)}, u32[]{:S(2)}, u32[]{:S(2)}) async-start(f32[8,40,128]{2,1,0:T(8,128)} %shard_map.89), calls=%async_computation.1 | async-start | bytes 327680 | tf_op jit(solution)/shard_map/all_to_all | solution.py:572
  47.9 3.2 %shard_map.91 = (f32[3,8,40,128]{3,2,1,0:T(8,128)}, f32[3,8,40,128]{3,2,1,0:T(8,128)}) custom-call(f32[18,16,128]{2,1,0:T(8,128)S(1)} %get-tuple-element.23.coef.refs_0_, f32[4,40,128]{2,1,0:T(8,128)S(1)} %collective-permute-done.1.zhi.refs_1_, f32[4,16,128]{2,1,0:T(8,128)S(1)} %collective-permute-done.2.ylo.refs_2_, ...), custom_call_target="tpu_custom_call" | custom-call | flops 3000000000 | bytes 3000000 | tf_op jit(solution)/shard_map/pallas_call | solution.py:537
  51.1 3.2 %all-to-all-done.1.shares = f32[8,40,128]{2,1,0:T(8,128)S(1)} async-done(((f32[8,40,128]{2,1,0:T(8,128)}), f32[8,40,128]{2,1,0:T(8,128)S(1)}, u32[]{:S(2)}, u32[]{:S(2)}) %all-to-all-start.1) | async-done | bytes 163872 | tf_op jit(solution)/shard_map/all_to_all | solution.py:572
  54.3 3.2 %shard_map.92 = (f32[3,16,40,128]{3,2,1,0:T(8,128)}, f32[40,128]{1,0:T(8,128)}) custom-call(f32[8,40,128]{2,1,0:T(8,128)S(1)} %all-to-all-done.1.shares, f32[17,40,128]{2,1,0:T(8,128)S(1)} %get-tuple-element.37.refs_6_.layer_face, f32[4,16,40,128]{3,2,1,0:T(8,128)S(1)} %get-tuple-element.38.refs_7_.areal_face, f32[3,8,40,128]{3,2,1,0:T(8,128)} %get-tuple-element.40.base0, ...), custom_call_target="tpu_custom_call" | custom-call | tf_op jit(solution)/shard_map/pallas_call | solution.py:574
  (2 shorter events, 0.0 us)
Async XLA Ops:
  2.5 17.6 %collective-permute-start = (f32[4,40,128]{2,1,0:T(8,128)S(1)}, f32[4,40,128]{2,1,0:T(8,128)S(1)}, u32[]{:S(2)}, u32[]{:S(2)}) collective-permute-start(f32[4,40,128]{2,1,0:T(8,128)S(1)} %get-tuple-element.32), channel_id=1, source_target_pairs={{0,1},{1,2},{2,3},{3,4},{4,5},{5,6},{6,7},{8,9},{9,10},{10,11},{11... | collective-permute-start | bytes 245768 | tf_op jit(solution)/shard_map/ppermute | solution.py:511
  4.2 15.8 %collective-permute-start.1 = (f32[4,40,128]{2,1,0:T(8,128)S(1)}, f32[4,40,128]{2,1,0:T(8,128)S(1)}, u32[]{:S(2)}, u32[]{:S(2)}) collective-permute-start(f32[4,40,128]{2,1,0:T(8,128)S(1)} %get-tuple-element.33), channel_id=1, source_target_pairs={{1,0},{2,1},{3,2},{4,3},{5,4},{6,5},{7,6},{9,8},{10,9},{11,10},{12... | collective-permute-start | bytes 245768 | tf_op jit(solution)/shard_map/ppermute | solution.py:507
  5.5 8.7 %collective-permute-start.3 = (f32[4,16,128]{2,1,0:T(8,128)S(1)}, f32[4,16,128]{2,1,0:T(8,128)S(1)}, u32[]{:S(2)}, u32[]{:S(2)}) collective-permute-start(f32[4,16,128]{2,1,0:T(8,128)S(1)} %get-tuple-element.29.ylo_own), channel_id=1, source_target_pairs={{8,0},{16,8},{24,16},{32,24},{40,32},{48,40},{56,48},{64,56},{72,6... | collective-permute-start | bytes 98312 | tf_op jit(solution)/shard_map/ppermute | solution.py:507
  9.6 7.0 %collective-permute-start.2 = (f32[4,16,128]{2,1,0:T(8,128)S(1)}, f32[4,16,128]{2,1,0:T(8,128)S(1)}, u32[]{:S(2)}, u32[]{:S(2)}) collective-permute-start(f32[4,16,128]{2,1,0:T(8,128)S(1)} %get-tuple-element.30.yhi_own), channel_id=1, source_target_pairs={{0,8},{8,16},{16,24},{24,32},{32,40},{40,48},{48,56},{56,64},{64,7... | collective-permute-start | bytes 98312 | tf_op jit(solution)/shard_map/ppermute | solution.py:511
  11.6 5.1 %collective-permute-start.5 = (f32[4,2,8,128]{3,2,1,0:T(8,128)S(1)}, f32[4,2,8,128]{3,2,1,0:T(8,128)S(1)}, u32[]{:S(2)}, u32[]{:S(2)}) collective-permute-start(f32[4,2,8,128]{3,2,1,0:T(8,128)S(1)} %get-tuple-element.31.xpack), channel_id=1, source_target_pairs={{128,0},{256,128},{384,256},{129,1},{257,129},{385,257},{130,2},{2... | collective-permute-start | bytes 98312 | tf_op jit(solution)/shard_map/ppermute | solution.py:507
  14.2 5.8 %collective-permute-start.4 = (f32[4,2,8,128]{3,2,1,0:T(8,128)S(1)}, f32[4,2,8,128]{3,2,1,0:T(8,128)S(1)}, u32[]{:S(2)}, u32[]{:S(2)}) collective-permute-start(f32[4,2,8,128]{3,2,1,0:T(8,128)S(1)} %get-tuple-element.31.xpack), channel_id=1, source_target_pairs={{0,128},{128,256},{256,384},{1,129},{129,257},{257,385},{2,130},{1... | collective-permute-start | bytes 98312 | tf_op jit(solution)/shard_map/ppermute | solution.py:511
  22.1 13.3 %all-to-all-start = ((f32[8,40,128]{2,1,0:T(8,128)}), f32[8,40,128]{2,1,0:T(8,128)S(1)}, u32[]{:S(2)}, u32[]{:S(2)}) async-start(f32[8,40,128]{2,1,0:T(8,128)} %get-tuple-element.34), calls=%async_computation | async-start | bytes 327680 | tf_op jit(solution)/shard_map/all_to_all | solution.py:557
  35.4 8.4 %collective-permute-start.6 = (f32[32,128]{1,0:T(8,128)S(1)}, f32[32,128]{1,0:T(8,128)S(1)}, u32[]{:S(2)}, u32[]{:S(2)}) collective-permute-start(f32[32,128]{1,0:T(8,128)S(1)} %get-tuple-element.35), channel_id=1, source_target_pairs={{1,9},{3,131},{5,141},{8,0},{9,17},{11,139},{13,149},{14,134},{16,... | collective-permute-start | bytes 49160 | tf_op jit(solution)/shard_map/ppermute | solution.py:568
  44.5 9.8 %all-to-all-start.1 = ((f32[8,40,128]{2,1,0:T(8,128)}), f32[8,40,128]{2,1,0:T(8,128)S(1)}, u32[]{:S(2)}, u32[]{:S(2)}) async-start(f32[8,40,128]{2,1,0:T(8,128)} %shard_map.89), calls=%async_computation.1 | async-start | bytes 327680 | tf_op jit(solution)/shard_map/all_to_all | solution.py:572

commit v4 on v3

v4 whole, which is shorter than its diff:
```python
import jax
import jax.numpy as jnp
from jax import lax
from jax.experimental import pallas as pl
from jax.experimental.pallas import tpu as pltpu
from jax.sharding import PartitionSpec as P

SWEEPS = 8
RELAX = 0.8
DIRECTIONS = ((-1, 0), (1, 0), (0, -1), (0, 1), (-1, -1), (1, 1), (-1, 1), (1, -1))
F32 = jnp.float32
PARAMS = pltpu.CompilerParams(vmem_limit_bytes=16 * 2**20)
CHUNK = 4


def vmem(count):
    return [pl.BlockSpec(memory_space=pltpu.VMEM)] * count


def hbm(count):
    return [pl.BlockSpec(memory_space=pltpu.HBM)] * count


def shape_of(*dims):
    return jax.ShapeDtypeStruct(dims, F32)


def in_hbm(*arrays):
    return [pltpu.with_memory_space_constraint(a, pltpu.HBM) for a in arrays]


def lane_index(shape):
    return lax.broadcasted_iota(jnp.int32, shape, len(shape) - 1)


def row_index(shape):
    return lax.broadcasted_iota(jnp.int32, shape, len(shape) - 2)


def turn(block, shift, axis):
    shift = shift % block.shape[axis]
    return pltpu.roll(block, shift, axis) if shift else block


def inverse(value):
    guess = pl.reciprocal(value, approx=True)
    return guess * (2.0 - value * guess)


def mean_weight(a, b):
    return (a + a) * b * inverse(a + b)


def parity(axis):
    return lax.rem(lax.axis_index(axis), 2)


def faces_kernel(state, perm, state_v, perm_v, zface0, zface1, yface0, yface1, xpack, perm_half, sems):
    depth, height, width = perm.shape
    tiles, half = height // 8, depth // 2
    fetch = pltpu.make_async_copy(perm, perm_half, sems.at[0])
    pieces = [
        pltpu.make_async_copy(state.at[:, pl.ds(z, CHUNK)], state_v.at[:, pl.ds(z, CHUNK)], sems.at[1 + z // CHUNK])
        for z in range(0, depth, CHUNK)
    ]
    fetch.start()
    for piece in pieces:
        piece.start()
    z_high, y_high = parity("gz"), parity("gy")
    lanes = lane_index((8, 128))
    pairs = lanes // 2
    packed = [[jnp.full((8, 128), 1.0 if c == 3 else 0.0, F32) for _ in range(2)] for c in range(4)]

    def pack(c, z, cells):
        low, high = cells[0:1], cells[height - 1 : height]
        yface0[c, z : z + 1, :] = jnp.where(y_high == 0, high, low)
        yface1[c, z : z + 1, :] = jnp.where(y_high == 0, low, high)
        for t in range(tiles):
            i = (z % half) * tiles + t
            turned = turn(cells[8 * t : 8 * t + 8], 2 * i + 1, 1)
            packed[c][z // half] = jnp.where(pairs == i, turned, packed[c][z // half])

    fetch.wait()
    for z in range(depth):
        perm_v[z] = perm_half[z].astype(F32)
        pack(3, z, perm_half[z].astype(F32))
    for z in range(depth):
        if z % CHUNK == 0:
            pieces[z // CHUNK].wait()
        for c in range(3):
            pack(c, z, state_v[c, z])
    for c in range(4):
        for h in range(2):
            xpack[c, h] = packed[c][h]
        low, high = (state_v[c, z] if c < 3 else perm_v[z] for z in (0, depth - 1))
        zface0[c] = jnp.where(z_high == 0, high, low)
        zface1[c] = jnp.where(z_high == 0, low, high)


def inner_kernel(
    state, perm, right, pore, facies, storage_table, coupling_table,
    coef, coef_lane, layer_face, areal_face, acc,
    right_v, pore_v, facies_s, storage_s, coupling_s, sems,
):
    depth, height, width = perm.shape
    tiles, half = height // 8, depth // 2
    copies = [
        pltpu.make_async_copy(source, target, sems.at[n])
        for n, (source, target) in enumerate(
            (
                (facies, facies_s),
                (storage_table, storage_s),
                (coupling_table, coupling_s),
                (pore, pore_v),
                (right.at[0], right_v),
            )
        )
    ]
    for copy in copies:
        copy.start()
    rows = row_index((height, width))
    lanes = lane_index((height, width))
    for z in range(depth):
        q = perm[z]
        if z < depth - 1:
            layer_face[z + 1] = mean_weight(q, perm[z + 1])
        ty = jnp.where(rows == height - 1, 0.0, mean_weight(q, turn(q, -1, 0)))
        tx = jnp.where(lanes == width - 1, 0.0, mean_weight(q, turn(q, -1, 1)))
        areal_face[0, z] = ty
        areal_face[1, z] = turn(ty, 1, 0)
        areal_face[2, z] = tx
        areal_face[3, z] = turn(tx, 1, 1)

    for copy in copies[:3]:
        copy.wait()
    lane, row = lane_index((8, 128)), row_index((depth, 128))
    fids = jnp.zeros((depth, 128), jnp.int32)
    fids_lane = [jnp.zeros((8, 128), jnp.int32) for _ in range(2)]
    for z in range(depth):
        fid = facies_s[z]
        fids = jnp.where(row == z, fid, fids)
        fids_lane[z // half] = jnp.where(lane >= 2 * tiles * (z % half), fid, fids_lane[z // half])
    kinds = storage_table.shape[1]
    for which, table in enumerate((storage_s, coupling_s)):
        for k in range(9):
            rows_of = jnp.zeros((depth, 128), F32)
            for f in range(kinds):
                rows_of = jnp.where(fids == f, table[k // 3, f, k % 3], rows_of)
            coef[9 * which + k] = rows_of
    for k in range(3):
        for h in range(2):
            lane_of = jnp.zeros((8, 128), F32)
            for f in range(kinds):
                lane_of = jnp.where(fids_lane[h] == f, coupling_s[0, f, k], lane_of)
            coef_lane[k, h] = lane_of
    for copy in copies[3:]:
        copy.wait()

    for a in range(6):
        acc[a] = jnp.zeros((height, width), F32)
    for z in range(depth):
        u = [state[c, z] for c in range(3)]
        m0 = [coef[c, z : z + 1, :] for c in range(3)]
        k0 = [coef[9 + c, z : z + 1, :] for c in range(3)]
        v = pore_v[z].astype(F32)
        part = right_v[z] - v * (m0[0] * u[0] + m0[1] * u[1] + m0[2] * u[2])
        if z < depth - 1:
            step = [k0[c] - coef[9 + c, z + 1 : z + 2, :] for c in range(3)]
            jump = [u[c] - state[c, z + 1] for c in range(3)]
            part = part - layer_face[z + 1] * (step[0] * jump[0] + step[1] * jump[1] + step[2] * jump[2])
        acc[0] += part
        acc[1] += m0[0] * v
        w = k0[0] * u[0] + k0[1] * u[1] + k0[2] * u[2]
        ty, tx = areal_face[0, z], areal_face[2, z]
        acc[2] += k0[0] * ty
        acc[3] += k0[0] * tx
        acc[4] += ty * (w - turn(w, -1, 0))
        acc[5] += tx * (w - turn(w, -1, 1))


def outer_kernel(
    coef, coef_lane, acc, zface0, zface1, yface0, yface1, xpack, z0, z1, y0, y1, x0, x1, layer_in,
    layer_face, znear, ynear, xnear, yweight, xweight, message,
):
    del layer_in
    _, height, width = zface0.shape
    depth = yface0.shape[1]
    tiles, half = height // 8, depth // 2
    rows = row_index((height, width))
    lanes = lane_index((height, width))
    lane = lane_index((8, 128))
    z_high, y_high, x_high = parity("gz"), parity("gy"), parity("gx")

    def received(high, first, second, c):
        a, b = first[c], second[c]
        return jnp.where(high == 0, b, a), jnp.where(high == 0, a, b)

    def flat(own, near, k0):
        weight = mean_weight(own[3], near[3])
        jump = k0[0] * (own[0] - near[0]) + k0[1] * (own[1] - near[1]) + k0[2] * (own[2] - near[2])
        return weight, weight * jump

    zown = [received(z_high, zface0, zface1, c) for c in range(4)]
    yown = [received(y_high, yface0, yface1, c) for c in range(4)]
    znears = [received(z_high, z0, z1, c) for c in range(4)]
    ynears = [received(y_high, y0, y1, c) for c in range(4)]
    for c in range(3):
        for e in range(2):
            znear[e, c] = znears[c][e]
            ynear[e, c] = ynears[c][e]
    rhs = acc[0]
    for e, z in ((0, 0), (1, depth - 1)):
        weight, flux = flat(
            [zown[c][e] for c in range(4)],
            [znears[c][e] for c in range(4)],
            [coef[9 + c, z : z + 1, :] for c in range(3)],
        )
        layer_face[z + e] = weight
        rhs = rhs - flux
    k_rows = [coef[9 + k] for k in range(3)]
    y_sum, y_flux = [], []
    for e in range(2):
        weight, flux = flat([yown[c][e] for c in range(4)], [ynears[c][e] for c in range(4)], k_rows)
        yweight[e] = weight
        y_sum.append(jnp.sum(k_rows[0] * weight, axis=0, keepdims=True))
        y_flux.append(jnp.sum(flux, axis=0, keepdims=True))
    side_sum, side_flux = 0.0, 0.0
    for h in range(2):
        near = []
        for c in range(4):
            west, east = jnp.where(x_high == 0, x1[c, h], x0[c, h]), jnp.where(x_high == 0, x0[c, h], x1[c, h])
            near.append(jnp.where(lane % 2 == 0, turn(east, -1, 1), turn(west, 1, 1)))
        for c in range(3):
            xnear[c, h] = near[c]
        weight, flux = flat([xpack[c, h] for c in range(4)], near, [coef_lane[k, h] for k in range(3)])
        used = lane < 2 * tiles * half
        xweight[h] = weight
        side_sum += jnp.where(used, coef_lane[0, h] * weight, 0.0)
        side_flux += jnp.where(used, flux, 0.0)
    gap = tiles * half
    while gap >= 2 * tiles:
        side_sum = side_sum + turn(side_sum, -gap, 1)
        side_flux = side_flux + turn(side_flux, -gap, 1)
        gap //= 2

    diag, ty, tx, fy, fx = acc[1], acc[2], acc[3], acc[4], acc[5]
    edge_sum = jnp.concatenate([turn(side_sum, 127 - 2 * t, 1) for t in range(tiles)], axis=0)
    edge_flux = jnp.concatenate([turn(side_flux, 127 - 2 * t, 1) for t in range(tiles)], axis=0)
    last_row, first_row, last_lane, first_lane = rows == height - 1, rows == 0, lanes == width - 1, lanes == 0
    ty_plus, ty_minus = jnp.where(last_row, y_sum[1], ty), jnp.where(first_row, y_sum[0], turn(ty, 1, 0))
    tx_plus, tx_minus = jnp.where(last_lane, edge_sum, tx), jnp.where(first_lane, edge_sum, turn(tx, 1, 1))
    fy_plus, fy_minus = jnp.where(last_row, y_flux[1], fy), jnp.where(first_row, y_flux[0], -turn(fy, 1, 0))
    fx_plus, fx_minus = jnp.where(last_lane, edge_flux, fx), jnp.where(first_lane, edge_flux, -turn(fx, 1, 1))
    planes = [
        rhs - (fy_plus + fy_minus) - (fx_plus + fx_minus),
        diag + (ty_plus + ty_minus) + (tx_plus + tx_minus),
        ty_plus,
        tx_plus,
    ]

    last = tiles - 1

    def tile(p, t):
        return planes[p][8 * t : 8 * t + 8]

    for p in range(4):
        message[0, 8 * p : 8 * p + 8, :] = tile(p, 0)
        message[1, 8 * p : 8 * p + 8, :] = tile(p, last)
        left = jnp.zeros((8, 128), F32)
        right_side = jnp.zeros((8, 128), F32)
        for t in range(tiles):
            here = lane // 8 == t
            left = jnp.where(here, turn(tile(p, t), 8 * t, 1), left)
            right_side = jnp.where(here, turn(tile(p, t), 8 * t + 8, 1), right_side)
        message[2, 8 * p : 8 * p + 8, :] = left
        message[3, 8 * p : 8 * p + 8, :] = right_side
    for k, (t, at_end) in enumerate(((0, 0), (last, 1), (0, 1), (last, 0))):
        corner = jnp.zeros((8, 128), F32)
        for p in range(4):
            corner = jnp.where(lane // 8 == p, turn(tile(p, t), 8 * p + 8 * at_end, 1), corner)
        message[4 + k, 0:8, :] = corner
        for t in range(4):
            message[4 + k, 8 + 8 * t : 16 + 8 * t, :] = tile(k, t)
        message[k, 32:40, :] = tile(k, last)


def cells_kernel(
    h, coef, znear, ynear, xnear, yweight, xweight, order, layer_face, areal_in, state_in, right_in, pore_in,
    base_out, gain_out, areal_face,
    state, right, pore, base, gain, sems,
):
    del order
    if h == 1:
        base, gain = base_out, gain_out
    half, height, width = pore.shape
    tiles, first, pieces = height // 8, h * half, half // CHUNK
    rows = row_index((height, width))
    lanes = lane_index((height, width))
    arrivals = []
    for p in range(pieces):
        here, there = pl.ds(p * CHUNK, CHUNK), pl.ds(first + p * CHUNK, CHUNK)
        state_low = 1 if p == 0 and h == 0 else (0 if p == 0 else p * CHUNK + 2)
        state_high = (p + 1) * CHUNK + (1 if p == pieces - 1 and h == 1 else 2)
        z_low = first - 1 + state_low
        arrivals.append([
            pltpu.make_async_copy(
                state_in.at[:, pl.ds(z_low, state_high - state_low)],
                state.at[:, pl.ds(state_low, state_high - state_low)],
                sems.at[0, p],
            ),
            pltpu.make_async_copy(right_in.at[:, there], right.at[:, here], sems.at[1, p]),
            pltpu.make_async_copy(pore_in.at[there], pore.at[here], sems.at[2, p]),
        ])
    for group in arrivals:
        for copy in group:
            copy.start()
    for c in range(3):
        state[c, 0 if h == 0 else half + 1] = znear[h, c]

    def layer(i):
        z = first + i
        m = [[coef[3 * r + c, z : z + 1, :] for c in range(3)] for r in range(3)]
        k = [[coef[9 + 3 * r + c, z : z + 1, :] for c in range(3)] for r in range(3)]

        def edges_of(packed):
            return jnp.concatenate(
                [turn(packed, 127 - 2 * tiles * i - 2 * t, 1) for t in range(tiles)], axis=0
            )

        edges = edges_of(xweight[h])
        areal = [
            jnp.where(rows == height - 1, yweight[1, z : z + 1, :], areal_in[0, z]),
            jnp.where(rows == 0, yweight[0, z : z + 1, :], areal_in[1, z]),
            jnp.where(lanes == width - 1, edges, areal_in[2, z]),
            jnp.where(lanes == 0, edges, areal_in[3, z]),
        ]
        for d in range(4):
            areal_face[d, z] = areal[d]
        weights = [layer_face[z + 1], layer_face[z]] + areal
        total = weights[0] + weights[1] + weights[2] + weights[3] + weights[4] + weights[5]
        cells, flux = [], []
        for c in range(3):
            u = state[c, i + 1]
            edges = edges_of(xnear[c, h])
            near = (
                state[c, i + 2],
                state[c, i],
                jnp.where(rows == height - 1, ynear[1, c, z : z + 1, :], turn(u, -1, 0)),
                jnp.where(rows == 0, ynear[0, c, z : z + 1, :], turn(u, 1, 0)),
                jnp.where(lanes == width - 1, edges, turn(u, -1, 1)),
                jnp.where(lanes == 0, edges, turn(u, 1, 1)),
            )
            moved = weights[0] * (u - near[0])
            for w, n in zip(weights[1:], near[1:]):
                moved = moved + w * (u - n)
            cells.append(u)
            flux.append(moved)
        v = pore[i].astype(F32)
        residual = [
            right[r, i]
            - v * (m[r][0] * cells[0] + m[r][1] * cells[1] + m[r][2] * cells[2])
            - (k[r][0] * flux[0] + k[r][1] * flux[1] + k[r][2] * flux[2])
            for r in range(3)
        ]
        entries = [[v * m[r][c] + total * k[r][c] for c in range(3)] for r in range(3)]

        def cofactor(r, c):
            r1, r2, c1, c2 = (r + 1) % 3, (r + 2) % 3, (c + 1) % 3, (c + 2) % 3
            return entries[r1][c1] * entries[r2][c2] - entries[r1][c2] * entries[r2][c1]

        factors = [[cofactor(r, c) for c in range(3)] for r in range(3)]
        determinant = (
            entries[0][0] * factors[0][0] + entries[0][1] * factors[0][1] + entries[0][2] * factors[0][2]
        )
        scale = inverse(determinant)
        for r in range(3):
            base[r, i] = cells[r] + scale * (
                factors[0][r] * residual[0] + factors[1][r] * residual[1] + factors[2][r] * residual[2]
            )
            gain[r, i] = scale * (factors[0][r] * k[0][0] + factors[1][r] * k[1][0] + factors[2][r] * k[2][0])

    departures = []
    for p in range(pieces):
        for copy in arrivals[p]:
            copy.wait()
        for i in range(p * CHUNK, (p + 1) * CHUNK):
            layer(i)
        if h == 1:
            continue
        here = pl.ds(p * CHUNK, CHUNK)
        for n, (source, target) in enumerate(((base, base_out), (gain, gain_out))):
            copy = pltpu.make_async_copy(source.at[:, here], target.at[:, here], sems.at[3 + n, p])
            copy.start()
            departures.append(copy)
    for copy in departures:
        copy.wait()


def total_kernel(parts, total, strip):
    result = parts[0]
    for i in range(1, parts.shape[0]):
        result = result + parts[i]
    total[...] = result
    strip[...] = result[: strip.shape[0]]


def merge_kernel(strip, share, copies):
    at_corner = lax.axis_index("gz") >= 4
    for t in range(5):
        cells = slice(8 * t, 8 * t + 8)
        if t == 0:
            merged = strip[cells]
        elif t == 4:
            merged = share[cells]
        else:
            merged = jnp.where(at_corner, share[cells], strip[cells])
        for k in range(copies.shape[0]):
            copies[k, cells, :] = merged


def sweep_kernel(
    shares, layer_face, areal_face, base0, gain0, base1, gain1, new_state, correction,
    base, gain, result, plane, sems,
):
    _, depth, height, width = areal_face.shape
    tiles, half = height // 8, depth // 2
    lane = lane_index((8, 128))
    arrivals = []
    for p in range(half // CHUNK):
        here = pl.ds(p * CHUNK, CHUNK)
        arrivals.append([
            pltpu.make_async_copy(base0.at[:, here], base.at[:, here], sems.at[1, p]),
            pltpu.make_async_copy(gain0.at[:, here], gain.at[:, here], sems.at[2, p]),
        ])
    for group in arrivals:
        for copy in group:
            copy.start()

    def tile(k, t):
        return shares[k, 8 * t : 8 * t + 8, :]

    def side(right, right_at, left, left_at):
        right, left = turn(right, -right_at, 1), turn(left, width - 8 - left_at, 1)
        return jnp.where(lane < 8, right, jnp.where(lane >= width - 8, left, 0.0))

    planes = []
    for p in range(4):
        main = [tile(1, p)] + [tile(4 + p, 1 + t) for t in range(tiles - 1)] + [tile(p, 4), tile(0, p)]
        edge = [side(tile(7, 0), 8 * p, tile(5, 0), 8 * p)]
        for t in range(tiles):
            edge.append(side(tile(2, p), 8 * t, tile(3, p), 8 * t))
        edge.append(side(tile(4, 0), 8 * p, tile(6, 0), 8 * p))
        planes.append(
            jnp.concatenate([jnp.concatenate(main, axis=0), jnp.concatenate(edge, axis=0)], axis=1)
        )
    filled = planes[1] > 0.0
    scale = jnp.where(filled, RELAX / jnp.where(filled, planes[1], 1.0), 0.0)
    source = scale * planes[0]
    south = scale * planes[2]
    north = scale * turn(planes[2], 1, 0)
    east = scale * planes[3]
    west = scale * turn(planes[3], 1, 1)

    def around(field):
        return turn(field, -1, 0), turn(field, 1, 0), turn(field, -1, 1), turn(field, 1, 1)

    field = source
    for _ in range(SWEEPS - 1):
        s, n, e, w = around(field)
        field = ((1.0 - RELAX) * field + source) + (south * s + north * n) + (east * e + west * w)
    near = around(field)
    own = field[8 : 8 + height, 0:width]
    near = [n[8 : 8 + height, 0:width] for n in near]
    plane[...] = own
    copies = [pltpu.make_async_copy(plane, correction, sems.at[0, depth // CHUNK])]
    copies[0].start()

    for first in [*range(half, depth, CHUNK), *range(0, half, CHUNK)]:
        for copy in arrivals[first // CHUNK] if first < half else ():
            copy.wait()

        for z in range(first, first + CHUNK):
            push = (layer_face[z] + layer_face[z + 1]) * own
            for d in range(4):
                push = push + areal_face[d, z] * near[d]
            for r in range(3):
                if first < half:
                    result[r, z] = base[r, z] + gain[r, z] * push
                else:
                    result[r, z] = base1[r, z - half] + gain1[r, z - half] * push
        copy = pltpu.make_async_copy(
            result.at[:, pl.ds(first, CHUNK)], new_state.at[:, pl.ds(first, CHUNK)], sems.at[0, first // CHUNK]
        )
        copy.start()
        copies.append(copy)
    for copy in copies:
        copy.wait()


def call(kernel, out_shape, in_specs, out_specs, scratch=(), flops=0, moved=0, aliases=None):
    return pl.pallas_call(
        kernel,
        out_shape=out_shape,
        in_specs=in_specs,
        out_specs=out_specs,
        scratch_shapes=list(scratch),
        compiler_params=PARAMS,
        input_output_aliases=aliases or {},
        cost_estimate=pl.CostEstimate(flops=flops, bytes_accessed=moved, transcendentals=0) if flops else None,
    )


def per_device(state, right_side, permeability, pore_volume, facies, storage_table, coupling_table):
    _, depth, height, width = state.shape
    columns = lax.axis_size("gz")
    row_of, rows = lax.axis_size("gx"), lax.axis_size("gy")
    block = (depth, height, width)
    bf16 = jnp.bfloat16
    storage_table, coupling_table = storage_table.transpose(1, 0, 2), coupling_table.transpose(1, 0, 2)

    state_v, perm_v, zface0, zface1, yface0, yface1, xpack = call(
        faces_kernel,
        [shape_of(3, *block), shape_of(*block)]
        + [shape_of(4, height, width)] * 2 + [shape_of(4, depth, width)] * 2 + [shape_of(4, 2, 8, 128)],
        hbm(2),
        vmem(7),
        [pltpu.VMEM(block, bf16), pltpu.SemaphoreType.DMA((1 + depth // CHUNK,))],
    )(*in_hbm(state, permeability))

    def exchange(face, axis, odd):
        pairs = []
        for i in range(odd, lax.axis_size(axis) - 1, 2):
            pairs += [(i, i + 1), (i + 1, i)]
        return lax.ppermute(face, axis, pairs)

    received = []
    for axis, first, second in (("gz", zface0, zface1), ("gy", yface0, yface1), ("gx", xpack, xpack)):
        received += [exchange(first, axis, 0), exchange(second, axis, 1)]

    coef, coef_lane, layer_face, areal_face, acc = call(
        inner_kernel,
        [
            shape_of(18, depth, 128),
            shape_of(3, 2, 8, 128),
            shape_of(depth + 1, height, width),
            shape_of(4, *block),
            shape_of(6, height, width),
        ],
        vmem(2) + hbm(5),
        vmem(5),
        [
            pltpu.VMEM(block, F32),
            pltpu.VMEM(block, bf16),
            pltpu.SMEM(facies.shape, jnp.int32),
            pltpu.SMEM(storage_table.shape, F32),
            pltpu.SMEM(coupling_table.shape, F32),
            pltpu.SemaphoreType.DMA((5,)),
        ],
        flops=2 * 10**9,
        moved=2 * 10**6,
    )(state_v, perm_v, *in_hbm(right_side, pore_volume, facies, storage_table, coupling_table))

    layer_face, znear, ynear, xnear, yweight, xweight, message = call(
        outer_kernel,
        [
            shape_of(depth + 1, height, width),
            shape_of(2, 3, height, width),
            shape_of(2, 3, depth, width),
            shape_of(3, 2, 8, 128),
            shape_of(2, depth, width),
            shape_of(2, 8, 128),
            shape_of(columns, 40, 128),
        ],
        vmem(15),
        vmem(7),
        aliases={14: 0},
    )(coef, coef_lane, acc, zface0, zface1, yface0, yface1, xpack, *received, layer_face)

    def cells(h, order, areal_face):
        def kernel(*refs):
            cells_kernel(h, *refs)

        layers = depth // 2
        half = (layers, height, width)
        kept = [shape_of(3, *half)] * 2 if h == 1 else [pltpu.HBM((3, *half), F32)] * 2
        return call(
            kernel,
            kept + [shape_of(4, *block)],
            vmem(9) + hbm(3),
            (vmem(2) if h == 1 else hbm(2)) + vmem(1),
            [
                pltpu.VMEM((3, layers + 2, height, width), F32),
                pltpu.VMEM((3, *half), F32),
                pltpu.VMEM(half, bf16),
                pltpu.VMEM((3, *half), F32),
                pltpu.VMEM((3, *half), F32),
                pltpu.SemaphoreType.DMA((5, layers // CHUNK)),
            ],
            flops=3 * 10**9,
            moved=3 * 10**6,
            aliases={8: 2},
        )(
            coef, znear, ynear, xnear, yweight, xweight, order, layer_face, areal_face,
            *in_hbm(state, right_side, pore_volume),
        )

    parts = lax.all_to_all(message, "gz", 0, 0)
    share, strip = call(total_kernel, [shape_of(40, 128), shape_of(32, 128)], vmem(1), vmem(2))(parts)
    pairs = []
    for x in range(row_of):
        for y in range(rows):
            for k, (dy, dx) in enumerate(DIRECTIONS):
                if 0 <= x + dx < row_of and 0 <= y + dy < rows:
                    pairs.append(
                        ((x * rows + y) * columns + k, ((x + dx) * rows + y + dy) * columns + k)
                    )
    strip = lax.ppermute(strip, ("gx", "gy", "gz"), pairs)
    base0, gain0, areal_face = cells(0, share, areal_face)
    copies = call(merge_kernel, shape_of(columns, 40, 128), vmem(2), vmem(1)[0])(strip, share)
    base1, gain1, areal_face = cells(1, strip, areal_face)
    shares = lax.all_to_all(copies, "gz", 0, 0)

    new_state, correction = call(
        sweep_kernel,
        [pltpu.HBM((3, *block), F32), pltpu.HBM((height, width), F32)],
        vmem(3) + hbm(2) + vmem(2),
        hbm(2),
        [
            pltpu.VMEM((3, depth // 2, height, width), F32),
            pltpu.VMEM((3, depth // 2, height, width), F32),
            pltpu.VMEM((3, *block), F32),
            pltpu.VMEM((height, width), F32),
            pltpu.SemaphoreType.DMA((3, depth // CHUNK + 1)),
        ],
    )(shares, layer_face, areal_face, *in_hbm(base0, gain0), base1, gain1)
    return (new_state, correction)


def solution(mesh):
    return jax.shard_map(
        per_device,
        mesh=mesh,
        in_specs=(
            P(None, "gz", "gy", "gx"),
            P(None, "gz", "gy", "gx"),
            P("gz", "gy", "gx"),
            P("gz", "gy", "gx"),
            P("gz"),
            P(),
            P(),
        ),
        out_specs=(P(None, "gz", "gy", "gx"), P("gy", "gx")),
        check_vma=False,
    )
```

time: 58 us -> 56.7 us (0.978)
  the two profiles are of different devices: /device:TPU:408 before, /device:TPU:96 now
where the time goes in v4:
time: 56.7 us; the launch traced here: 56.2 us
  starting transfers between devices  23.8 us (42%)
  Pallas kernels  13.4 us (24%)
  blocking collectives  12.5 us (22%)
  waiting for transfers between devices  5.72 us (10%)
  between operations  0.75 us (1%)
    ppermute x6, starting transfers between devices, exchange(): return lax.ppermute(face, axis, pairs)  15.6 us
    all_to_all x1, blocking collectives, per_device(): parts = lax.all_to_all(message, 'gz', 0, 0)  12.5 us
    all_to_all x1, starting transfers between devices, per_device(): shares = lax.all_to_all(copies, 'gz', 0, 0)  6.24 us
    pallas_call x2, Pallas kernels, cells(): call(kernel, kept + [shape_of(4, *block)], vmem(9) + hbm(3), (vmem(2) if...  5.94 us
    all_to_all x1, waiting for transfers between devices, per_device(): shares = lax.all_to_all(copies, 'gz', 0, 0)  3.91 us
    pallas_call x1, Pallas kernels, per_device(): call(sweep_kernel, [pltpu.HBM((3, *block), F32), pltpu.HBM((height, width...  3.09 us
    ppermute x1, starting transfers between devices, per_device(): strip = lax.ppermute(strip, ('gx', 'gy', 'gz'), pairs)  1.92 us
    pallas_call x1, Pallas kernels, per_device(): call(faces_kernel, [shape_of(3, *block), shape_of(*block)] + [shape_of(4,...  1.63 us
  transfers between devices with their start and end apart: 8, of which 3 were waited for; matrix products, arithmetic and copies ran while one was open for 0% of the time, Pallas kernels for 13%

profile of v4, /device:TPU:96, one launch (start us, length us, event | category | flops | bytes accessed | tf_op | source)
XLA Modules:
  0.0 56.2 jit_solution(12006888432436822539)
XLA Ops:
  0.6 1.6 %shard_map.86 = (f32[3,16,40,128]{3,2,1,0:T(8,128)S(1)}, f32[16,40,128]{2,1,0:T(8,128)S(1)}, f32[4,40,128]{2,1,0:T(8,128)S(1)}, f32[4,40,128]{2,1,0:T(8,128)S(1)...) custom-call(f32[3,16,40,128]{3,2,1,0:T(8,128)} %refs_9_.3, ...), custom_call_target="tpu_custom_call" | custom-call | tf_op jit(solution)/shard_map/pallas_call | solution.py:521
  2.3 3.5 %collective-permute-start.4 = (f32[4,2,8,128]{3,2,1,0:T(8,128)S(1)}, f32[4,2,8,128]{3,2,1,0:T(8,128)S(1)}, u32[]{:S(2)}, u32[]{:S(2)}) collective-permute-start(f32[4,2,8,128]{3,2,1,0:T(8,128)S(1)} %get-tuple-element.38.xpack), channel_id=1, source_target_pairs={{0,128},{128,0},{256,384},{384,256},{1,129},{129,1},{257,385},{385... | collective-permute-start | bytes 98312 | tf_op jit(solution)/shard_map/ppermute | solution.py:534
  5.8 0.7 %collective-permute-start.5 = (f32[4,2,8,128]{3,2,1,0:T(8,128)S(1)}, f32[4,2,8,128]{3,2,1,0:T(8,128)S(1)}, u32[]{:S(2)}, u32[]{:S(2)}) collective-permute-start(f32[4,2,8,128]{3,2,1,0:T(8,128)S(1)} %get-tuple-element.38.xpack), channel_id=1, source_target_pairs={{128,256},{256,128},{129,257},{257,129},{130,258},{258,130},{131,2... | collective-permute-start | bytes 98312 | tf_op jit(solution)/shard_map/ppermute | solution.py:534
  6.4 1.9 %collective-permute-start = (f32[4,40,128]{2,1,0:T(8,128)S(1)}, f32[4,40,128]{2,1,0:T(8,128)S(1)}, u32[]{:S(2)}, u32[]{:S(2)}) collective-permute-start(f32[4,40,128]{2,1,0:T(8,128)S(1)} %get-tuple-element.34.zface0), channel_id=1, source_target_pairs={{0,1},{1,0},{2,3},{3,2},{4,5},{5,4},{6,7},{7,6},{8,9},{9,8},{10,11... | collective-permute-start | bytes 245768 | tf_op jit(solution)/shard_map/ppermute | solution.py:534
  8.4 0.7 %collective-permute-start.1 = (f32[4,40,128]{2,1,0:T(8,128)S(1)}, f32[4,40,128]{2,1,0:T(8,128)S(1)}, u32[]{:S(2)}, u32[]{:S(2)}) collective-permute-start(f32[4,40,128]{2,1,0:T(8,128)S(1)} %get-tuple-element.35.zface1), channel_id=1, source_target_pairs={{1,2},{2,1},{3,4},{4,3},{5,6},{6,5},{9,10},{10,9},{11,12},{12,11},... | collective-permute-start | bytes 245768 | tf_op jit(solution)/shard_map/ppermute | solution.py:534
  9.0 2.0 %collective-permute-start.2 = (f32[4,16,128]{2,1,0:T(8,128)S(1)}, f32[4,16,128]{2,1,0:T(8,128)S(1)}, u32[]{:S(2)}, u32[]{:S(2)}) collective-permute-start(f32[4,16,128]{2,1,0:T(8,128)S(1)} %get-tuple-element.36.yface0), channel_id=1, source_target_pairs={{0,8},{8,0},{16,24},{24,16},{32,40},{40,32},{48,56},{56,48},{64,72... | collective-permute-start | bytes 98312 | tf_op jit(solution)/shard_map/ppermute | solution.py:534
  11.1 0.0 collective-permute-done.4.x0
  11.1 6.8 %collective-permute-start.3 = (f32[4,16,128]{2,1,0:T(8,128)S(1)}, f32[4,16,128]{2,1,0:T(8,128)S(1)}, u32[]{:S(2)}, u32[]{:S(2)}) collective-permute-start(f32[4,16,128]{2,1,0:T(8,128)S(1)} %get-tuple-element.37.yface1), channel_id=1, source_target_pairs={{8,16},{16,8},{24,32},{32,24},{40,48},{48,40},{56,64},{64,56},{72,... | collective-permute-start | bytes 98312 | tf_op jit(solution)/shard_map/ppermute | solution.py:534
  17.9 1.6 %shard_map.87 = (f32[18,16,128]{2,1,0:T(8,128)S(1)}, f32[3,2,8,128]{3,2,1,0:T(8,128)S(1)}, f32[17,40,128]{2,1,0:T(8,128)S(1)}, f32[4,16,40,128]{3,2,1,0:T(8,128)S(1)}, f32[6,40,128]{2,1,0:T(8,128)S(1)}) custom-call(f32[3,16,40,128]{3,2,1,0:T(8,128)S(1)} %get-tuple-element.29.state, f32[16,40,128]{2,1,0:T(8,128)S(1)} %get-tuple-element.30.perm, ...), custom_call_target="tpu_custom_call" | custom-call | flops 2000000000 | bytes 2000000 | tf_op jit(solution)/shard_map/pallas_call | solution.py:540
  19.5 0.0 collective-permute-done.5.x1
  19.5 0.0 collective-permute-done.2.y0
  19.5 0.3 collective-permute-done.3.y1
  19.8 0.0 collective-permute-done.z0
  19.8 0.0 collective-permute-done.1.z1
  19.8 0.5 shard_map.88
  20.3 12.5 %all_to_all.10.parts = f32[8,40,128]{2,1,0:T(8,128)S(1)} all-to-all(f32[8,40,128]{2,1,0:T(8,128)S(1)} %get-tuple-element.40), channel_id=1, replica_groups=mesh['gx'=4,'gy'=16,'gz'=8] {'gz'}, dimensions={0} | all-to-all | bytes 327680 | tf_op jit(solution)/shard_map/all_to_all | solution.py:607
  32.8 1.9 %collective-permute-start.6 = (f32[32,128]{1,0:T(8,128)S(1)}, f32[32,128]{1,0:T(8,128)S(1)}, u32[]{:S(2)}, u32[]{:S(2)}) collective-permute-start(f32[32,128]{1,0:T(8,128)S(1)} %get-tuple-element.41), channel_id=1, source_target_pairs={{1,9},{3,131},{5,141},{8,0},{9,17},{11,139},{13,149},{14,134},{16,... | collective-permute-start | bytes 49160 | tf_op jit(solution)/shard_map/ppermute | solution.py:617
  34.8 3.4 %shard_map.91 = (f32[3,8,40,128]{3,2,1,0:T(8,128)}, f32[3,8,40,128]{3,2,1,0:T(8,128)}, f32[4,16,40,128]{3,2,1,0:T(8,128)S(1)}) custom-call(f32[18,16,128]{2,1,0:T(8,128)S(1)} %get-tuple-element.31.coef.refs_0_, f32[2,3,40,128]{3,2,1,0:T(8,128)S(1)} %get-tuple-element.44.refs_1_, ...), custom_call_target="tpu_custom_call", output_to_operand_aliasing={{2}: (8, {})} | custom-call | flops 3000000000 | bytes 3000000 | tf_op jit(solution)/shard_map/pallas_call | solution.py:586
  38.1 1.5 %collective-permute-done.6.strip.refs_6_ = f32[32,128]{1,0:T(8,128)S(1)} collective-permute-done((f32[32,128]{1,0:T(8,128)S(1)}, f32[32,128]{1,0:T(8,128)S(1)}, u32[]{:S(2)}, u32[]{:S(2)}) %collective-permute-start.6) | collective-permute-done | bytes 16416 | tf_op jit(solution)/shard_map/ppermute | solution.py:617
  39.7 0.7 %shard_map.90 = f32[8,40,128]{2,1,0:T(8,128)} custom-call(f32[32,128]{1,0:T(8,128)S(1)} %collective-permute-done.6.strip.refs_6_, f32[40,128]{1,0:T(8,128)S(1)} %get-tuple-element.42.share.refs_6_), custom_call_target="tpu_custom_call" | custom-call | tf_op jit(solution)/shard_map/pallas_call | solution.py:619
  40.3 6.2 %all-to-all-start.1 = ((f32[8,40,128]{2,1,0:T(8,128)}), f32[8,40,128]{2,1,0:T(8,128)S(1)}, u32[]{:S(2)}, u32[]{:S(2)}) async-start(f32[8,40,128]{2,1,0:T(8,128)} %shard_map.90), calls=%async_computation.1 | async-start | bytes 327680 | tf_op jit(solution)/shard_map/all_to_all | solution.py:621
  46.6 2.6 %shard_map.92 = (f32[3,8,40,128]{3,2,1,0:T(8,128)S(1)}, f32[3,8,40,128]{3,2,1,0:T(8,128)S(1)}, f32[4,16,40,128]{3,2,1,0:T(8,128)S(1)}) custom-call(f32[18,16,128]{2,1,0:T(8,128)S(1)} %get-tuple-element.31.coef.refs_0_, f32[2,3,40,128]{3,2,1,0:T(8,128)S(1)} %get-tuple-element.44.refs_1_, ...), custom_call_target="tpu_custom_call", output_to_operand_aliasing={{2}: (8, {})} | custom-call | flops 3000000000 | bytes 3000000 | tf_op jit(solution)/shard_map/pallas_call | solution.py:586
  49.2 3.9 %all-to-all-done.1.shares = f32[8,40,128]{2,1,0:T(8,128)S(1)} async-done(((f32[8,40,128]{2,1,0:T(8,128)}), f32[8,40,128]{2,1,0:T(8,128)S(1)}, u32[]{:S(2)}, u32[]{:S(2)}) %all-to-all-start.1) | async-done | bytes 163872 | tf_op jit(solution)/shard_map/all_to_all | solution.py:621
  53.1 3.1 %shard_map.93 = (f32[3,16,40,128]{3,2,1,0:T(8,128)}, f32[40,128]{1,0:T(8,128)}) custom-call(f32[8,40,128]{2,1,0:T(8,128)S(1)} %all-to-all-done.1.shares, f32[17,40,128]{2,1,0:T(8,128)S(1)} %get-tuple-element.43.refs_7_.layer_face, f32[4,16,40,128]{3,2,1,0:T(8,128)S(1)} %get-tuple-element.51.areal_face, f32[3,8,40,128]{3,2,1,0:T(8,128)} %get-tuple-element.52.base0, ...), custom_call_target="tpu_custom_call" | custom-call | tf_op jit(solution)/shard_map/pallas_call | solution.py:623
  (1 shorter events, 0.0 us)
Async XLA Ops:
  2.3 8.8 %collective-permute-start.4 = (f32[4,2,8,128]{3,2,1,0:T(8,128)S(1)}, f32[4,2,8,128]{3,2,1,0:T(8,128)S(1)}, u32[]{:S(2)}, u32[]{:S(2)}) collective-permute-start(f32[4,2,8,128]{3,2,1,0:T(8,128)S(1)} %get-tuple-element.38.xpack), channel_id=1, source_target_pairs={{0,128},{128,0},{256,384},{384,256},{1,129},{129,1},{257,385},{385... | collective-permute-start | bytes 98312 | tf_op jit(solution)/shard_map/ppermute | solution.py:534
  5.8 13.8 %collective-permute-start.5 = (f32[4,2,8,128]{3,2,1,0:T(8,128)S(1)}, f32[4,2,8,128]{3,2,1,0:T(8,128)S(1)}, u32[]{:S(2)}, u32[]{:S(2)}) collective-permute-start(f32[4,2,8,128]{3,2,1,0:T(8,128)S(1)} %get-tuple-element.38.xpack), channel_id=1, source_target_pairs={{128,256},{256,128},{129,257},{257,129},{130,258},{258,130},{131,2... | collective-permute-start | bytes 98312 | tf_op jit(solution)/shard_map/ppermute | solution.py:534
  6.4 13.4 %collective-permute-start = (f32[4,40,128]{2,1,0:T(8,128)S(1)}, f32[4,40,128]{2,1,0:T(8,128)S(1)}, u32[]{:S(2)}, u32[]{:S(2)}) collective-permute-start(f32[4,40,128]{2,1,0:T(8,128)S(1)} %get-tuple-element.34.zface0), channel_id=1, source_target_pairs={{0,1},{1,0},{2,3},{3,2},{4,5},{5,4},{6,7},{7,6},{8,9},{9,8},{10,11... | collective-permute-start | bytes 245768 | tf_op jit(solution)/shard_map/ppermute | solution.py:534
  8.4 11.4 %collective-permute-start.1 = (f32[4,40,128]{2,1,0:T(8,128)S(1)}, f32[4,40,128]{2,1,0:T(8,128)S(1)}, u32[]{:S(2)}, u32[]{:S(2)}) collective-permute-start(f32[4,40,128]{2,1,0:T(8,128)S(1)} %get-tuple-element.35.zface1), channel_id=1, source_target_pairs={{1,2},{2,1},{3,4},{4,3},{5,6},{6,5},{9,10},{10,9},{11,12},{12,11},... | collective-permute-start | bytes 245768 | tf_op jit(solution)/shard_map/ppermute | solution.py:534
  9.0 10.5 %collective-permute-start.2 = (f32[4,16,128]{2,1,0:T(8,128)S(1)}, f32[4,16,128]{2,1,0:T(8,128)S(1)}, u32[]{:S(2)}, u32[]{:S(2)}) collective-permute-start(f32[4,16,128]{2,1,0:T(8,128)S(1)} %get-tuple-element.36.yface0), channel_id=1, source_target_pairs={{0,8},{8,0},{16,24},{24,16},{32,40},{40,32},{48,56},{56,48},{64,72... | collective-permute-start | bytes 98312 | tf_op jit(solution)/shard_map/ppermute | solution.py:534
  11.1 8.7 %collective-permute-start.3 = (f32[4,16,128]{2,1,0:T(8,128)S(1)}, f32[4,16,128]{2,1,0:T(8,128)S(1)}, u32[]{:S(2)}, u32[]{:S(2)}) collective-permute-start(f32[4,16,128]{2,1,0:T(8,128)S(1)} %get-tuple-element.37.yface1), channel_id=1, source_target_pairs={{8,16},{16,8},{24,32},{32,24},{40,48},{48,40},{56,64},{64,56},{72,... | collective-permute-start | bytes 98312 | tf_op jit(solution)/shard_map/ppermute | solution.py:534
  32.8 6.8 %collective-permute-start.6 = (f32[32,128]{1,0:T(8,128)S(1)}, f32[32,128]{1,0:T(8,128)S(1)}, u32[]{:S(2)}, u32[]{:S(2)}) collective-permute-start(f32[32,128]{1,0:T(8,128)S(1)} %get-tuple-element.41), channel_id=1, source_target_pairs={{1,9},{3,131},{5,141},{8,0},{9,17},{11,139},{13,149},{14,134},{16,... | collective-permute-start | bytes 49160 | tf_op jit(solution)/shard_map/ppermute | solution.py:617
  40.3 12.7 %all-to-all-start.1 = ((f32[8,40,128]{2,1,0:T(8,128)}), f32[8,40,128]{2,1,0:T(8,128)S(1)}, u32[]{:S(2)}, u32[]{:S(2)}) async-start(f32[8,40,128]{2,1,0:T(8,128)} %shard_map.90), calls=%async_computation.1 | async-start | bytes 327680 | tf_op jit(solution)/shard_map/all_to_all | solution.py:621

commit v5 on v4

--- a/solution.py
+++ b/solution.py
@@ -127,9 +127,7 @@
         ty = jnp.where(rows == height - 1, 0.0, mean_weight(q, turn(q, -1, 0)))
         tx = jnp.where(lanes == width - 1, 0.0, mean_weight(q, turn(q, -1, 1)))
         areal_face[0, z] = ty
-        areal_face[1, z] = turn(ty, 1, 0)
-        areal_face[2, z] = tx
-        areal_face[3, z] = turn(tx, 1, 1)
+        areal_face[1, z] = tx
 
     for copy in copies[:3]:
         copy.wait()
@@ -171,7 +169,7 @@
         acc[0] += part
         acc[1] += m0[0] * v
         w = k0[0] * u[0] + k0[1] * u[1] + k0[2] * u[2]
-        ty, tx = areal_face[0, z], areal_face[2, z]
+        ty, tx = areal_face[0, z], areal_face[1, z]
         acc[2] += k0[0] * ty
         acc[3] += k0[0] * tx
         acc[4] += ty * (w - turn(w, -1, 0))
@@ -284,67 +282,58 @@
         message[k, 32:40, :] = tile(k, last)
 
 
+def areal_weights(z, areal_face, yweight, xweight):
+    _, depth, height, width = areal_face.shape
+    tiles, half = height // 8, depth // 2
+    rows = row_index((height, width))
+    lanes = lane_index((height, width))
+    edges = edges_of(xweight[z // half], z % half, tiles)
+    ty, tx = areal_face[0, z], areal_face[1, z]
+    return (
+        jnp.where(rows == height - 1, yweight[1, z : z + 1, :], ty),
+        jnp.where(rows == 0, yweight[0, z : z + 1, :], turn(ty, 1, 0)),
+        jnp.where(lanes == width - 1, edges, tx),
+        jnp.where(lanes == 0, edges, turn(tx, 1, 1)),
+    )
+
+
+def edges_of(packed, i, tiles):
+    return jnp.concatenate([turn(packed, 127 - 2 * tiles * i - 2 * t, 1) for t in range(tiles)], axis=0)
+
+
 def cells_kernel(
-    h, coef, znear, ynear, xnear, yweight, xweight, order, layer_face, areal_in, state_in, right_in, pore_in,
-    base_out, gain_out, areal_face,
-    state, right, pore, base, gain, sems,
+    coef, znear, ynear, xnear, yweight, xweight, order, layer_face, areal_face, state, right_in, pore_in,
+    base, gain,
+    right, pore, sems,
 ):
     del order
-    if h == 1:
-        base, gain = base_out, gain_out
-    half, height, width = pore.shape
-    tiles, first, pieces = height // 8, h * half, half // CHUNK
+    depth, height, width = pore.shape
+    tiles, half = height // 8, depth // 2
     rows = row_index((height, width))
     lanes = lane_index((height, width))
     arrivals = []
-    for p in range(pieces):
-        here, there = pl.ds(p * CHUNK, CHUNK), pl.ds(first + p * CHUNK, CHUNK)
-        state_low = 1 if p == 0 and h == 0 else (0 if p == 0 else p * CHUNK + 2)
-        state_high = (p + 1) * CHUNK + (1 if p == pieces - 1 and h == 1 else 2)
-        z_low = first - 1 + state_low
+    for p in range(depth // CHUNK):
+        here = pl.ds(p * CHUNK, CHUNK)
         arrivals.append([
-            pltpu.make_async_copy(
-                state_in.at[:, pl.ds(z_low, state_high - state_low)],
-                state.at[:, pl.ds(state_low, state_high - state_low)],
-                sems.at[0, p],
-            ),
-            pltpu.make_async_copy(right_in.at[:, there], right.at[:, here], sems.at[1, p]),
-            pltpu.make_async_copy(pore_in.at[there], pore.at[here], sems.at[2, p]),
+            pltpu.make_async_copy(right_in.at[:, here], right.at[:, here], sems.at[0, p]),
+            pltpu.make_async_copy(pore_in.at[here], pore.at[here], sems.at[1, p]),
         ])
     for group in arrivals:
         for copy in group:
             copy.start()
-    for c in range(3):
-        state[c, 0 if h == 0 else half + 1] = znear[h, c]
-
-    def layer(i):
-        z = first + i
+
+    def layer(z):
         m = [[coef[3 * r + c, z : z + 1, :] for c in range(3)] for r in range(3)]
         k = [[coef[9 + 3 * r + c, z : z + 1, :] for c in range(3)] for r in range(3)]
-
-        def edges_of(packed):
-            return jnp.concatenate(
-                [turn(packed, 127 - 2 * tiles * i - 2 * t, 1) for t in range(tiles)], axis=0
-            )
-
-        edges = edges_of(xweight[h])
-        areal = [
-            jnp.where(rows == height - 1, yweight[1, z : z + 1, :], areal_in[0, z]),
-            jnp.where(rows == 0, yweight[0, z : z + 1, :], areal_in[1, z]),
-            jnp.where(lanes == width - 1, edges, areal_in[2, z]),
-            jnp.where(lanes == 0, edges, areal_in[3, z]),
-        ]
-        for d in range(4):
-            areal_face[d, z] = areal[d]
-        weights = [layer_face[z + 1], layer_face[z]] + areal
+        weights = [layer_face[z + 1], layer_face[z], *areal_weights(z, areal_face, yweight, xweight)]
         total = weights[0] + weights[1] + weights[2] + weights[3] + weights[4] + weights[5]
         cells, flux = [], []
         for c in range(3):
-            u = state[c, i + 1]
-            edges = edges_of(xnear[c, h])
+            u = state[c, z]
+            edges = edges_of(xnear[c, z // half], z % half, tiles)
             near = (
-                state[c, i + 2],
-                state[c, i],
+                znear[1, c] if z == depth - 1 else state[c, z + 1],
+                znear[0, c] if z == 0 else state[c, z - 1],
                 jnp.where(rows == height - 1, ynear[1, c, z : z + 1, :], turn(u, -1, 0)),
                 jnp.where(rows == 0, ynear[0, c, z : z + 1, :], turn(u, 1, 0)),
                 jnp.where(lanes == width - 1, edges, turn(u, -1, 1)),
@@ -355,9 +344,9 @@
                 moved = moved + w * (u - n)
             cells.append(u)
             flux.append(moved)
-        v = pore[i].astype(F32)
+        v = pore[z].astype(F32)
         residual = [
-            right[r, i]
+            right[r, z]
             - v * (m[r][0] * cells[0] + m[r][1] * cells[1] + m[r][2] * cells[2])
             - (k[r][0] * flux[0] + k[r][1] * flux[1] + k[r][2] * flux[2])
             for r in range(3)
@@ -374,26 +363,16 @@
         )
         scale = inverse(determinant)
         for r in range(3):
-            base[r, i] = cells[r] + scale * (
+            base[r, z] = cells[r] + scale * (
                 factors[0][r] * residual[0] + factors[1][r] * residual[1] + factors[2][r] * residual[2]
             )
-            gain[r, i] = scale * (factors[0][r] * k[0][0] + factors[1][r] * k[1][0] + factors[2][r] * k[2][0])
-
-    departures = []
-    for p in range(pieces):
-        for copy in arrivals[p]:
-            copy.wait()
-        for i in range(p * CHUNK, (p + 1) * CHUNK):
-            layer(i)
-        if h == 1:
-            continue
-        here = pl.ds(p * CHUNK, CHUNK)
-        for n, (source, target) in enumerate(((base, base_out), (gain, gain_out))):
-            copy = pltpu.make_async_copy(source.at[:, here], target.at[:, here], sems.at[3 + n, p])
-            copy.start()
-            departures.append(copy)
-    for copy in departures:
-        copy.wait()
+            gain[r, z] = scale * (factors[0][r] * k[0][0] + factors[1][r] * k[1][0] + factors[2][r] * k[2][0])
+
+    for z in range(depth):
+        if z % CHUNK == 0:
+            for copy in arrivals[z // CHUNK]:
+                copy.wait()
+        layer(z)
 
 
 def total_kernel(parts, total, strip):
@@ -404,7 +383,8 @@
     strip[...] = result[: strip.shape[0]]
 
 
-def merge_kernel(strip, share, copies):
+def merge_kernel(strip, share, order, copies):
+    del order
     at_corner = lax.axis_index("gz") >= 4
     for t in range(5):
         cells = slice(8 * t, 8 * t + 8)
@@ -419,22 +399,12 @@
 
 
 def sweep_kernel(
-    shares, layer_face, areal_face, base0, gain0, base1, gain1, new_state, correction,
-    base, gain, result, plane, sems,
+    shares, layer_face, areal_face, yweight, xweight, base, gain, new_state, correction,
+    result, plane, sems,
 ):
     _, depth, height, width = areal_face.shape
-    tiles, half = height // 8, depth // 2
+    tiles = height // 8
     lane = lane_index((8, 128))
-    arrivals = []
-    for p in range(half // CHUNK):
-        here = pl.ds(p * CHUNK, CHUNK)
-        arrivals.append([
-            pltpu.make_async_copy(base0.at[:, here], base.at[:, here], sems.at[1, p]),
-            pltpu.make_async_copy(gain0.at[:, here], gain.at[:, here], sems.at[2, p]),
-        ])
-    for group in arrivals:
-        for copy in group:
-            copy.start()
 
     def tile(k, t):
         return shares[k, 8 * t : 8 * t + 8, :]
@@ -472,24 +442,18 @@
     own = field[8 : 8 + height, 0:width]
     near = [n[8 : 8 + height, 0:width] for n in near]
     plane[...] = own
-    copies = [pltpu.make_async_copy(plane, correction, sems.at[0, depth // CHUNK])]
+    copies = [pltpu.make_async_copy(plane, correction, sems.at[depth // CHUNK])]
     copies[0].start()
 
-    for first in [*range(half, depth, CHUNK), *range(0, half, CHUNK)]:
-        for copy in arrivals[first // CHUNK] if first < half else ():
-            copy.wait()
-
+    for first in range(0, depth, CHUNK):
         for z in range(first, first + CHUNK):
             push = (layer_face[z] + layer_face[z + 1]) * own
-            for d in range(4):
-                push = push + areal_face[d, z] * near[d]
+            for weight, field in zip(areal_weights(z, areal_face, yweight, xweight), near):
+                push = push + weight * field
             for r in range(3):
-                if first < half:
-                    result[r, z] = base[r, z] + gain[r, z] * push
-                else:
-                    result[r, z] = base1[r, z - half] + gain1[r, z - half] * push
+                result[r, z] = base[r, z] + gain[r, z] * push
         copy = pltpu.make_async_copy(
-            result.at[:, pl.ds(first, CHUNK)], new_state.at[:, pl.ds(first, CHUNK)], sems.at[0, first // CHUNK]
+            result.at[:, pl.ds(first, CHUNK)], new_state.at[:, pl.ds(first, CHUNK)], sems.at[first // CHUNK]
         )
         copy.start()
         copies.append(copy)
@@ -543,7 +507,7 @@
             shape_of(18, depth, 128),
             shape_of(3, 2, 8, 128),
             shape_of(depth + 1, height, width),
-            shape_of(4, *block),
+            shape_of(2, *block),
             shape_of(6, height, width),
         ],
         vmem(2) + hbm(5),
@@ -576,34 +540,6 @@
         aliases={14: 0},
     )(coef, coef_lane, acc, zface0, zface1, yface0, yface1, xpack, *received, layer_face)
 
-    def cells(h, order, areal_face):
-        def kernel(*refs):
-            cells_kernel(h, *refs)
-
-        layers = depth // 2
-        half = (layers, height, width)
-        kept = [shape_of(3, *half)] * 2 if h == 1 else [pltpu.HBM((3, *half), F32)] * 2
-        return call(
-            kernel,
-            kept + [shape_of(4, *block)],
-            vmem(9) + hbm(3),
-            (vmem(2) if h == 1 else hbm(2)) + vmem(1),
-            [
-                pltpu.VMEM((3, layers + 2, height, width), F32),
-                pltpu.VMEM((3, *half), F32),
-                pltpu.VMEM(half, bf16),
-                pltpu.VMEM((3, *half), F32),
-                pltpu.VMEM((3, *half), F32),
-                pltpu.SemaphoreType.DMA((5, layers // CHUNK)),
-            ],
-            flops=3 * 10**9,
-            moved=3 * 10**6,
-            aliases={8: 2},
-        )(
-            coef, znear, ynear, xnear, yweight, xweight, order, layer_face, areal_face,
-            *in_hbm(state, right_side, pore_volume),
-        )
-
     parts = lax.all_to_all(message, "gz", 0, 0)
     share, strip = call(total_kernel, [shape_of(40, 128), shape_of(32, 128)], vmem(1), vmem(2))(parts)
     pairs = []
@@ -615,24 +551,36 @@
                         ((x * rows + y) * columns + k, ((x + dx) * rows + y + dy) * columns + k)
                     )
     strip = lax.ppermute(strip, ("gx", "gy", "gz"), pairs)
-    base0, gain0, areal_face = cells(0, share, areal_face)
-    copies = call(merge_kernel, shape_of(columns, 40, 128), vmem(2), vmem(1)[0])(strip, share)
-    base1, gain1, areal_face = cells(1, strip, areal_face)
+    base, gain = call(
+        cells_kernel,
+        [shape_of(3, *block)] * 2,
+        vmem(10) + hbm(2),
+        vmem(2),
+        [
+            pltpu.VMEM((3, *block), F32),
+            pltpu.VMEM(block, bf16),
+            pltpu.SemaphoreType.DMA((2, depth // CHUNK)),
+        ],
+        flops=4 * 10**9,
+        moved=4 * 10**6,
+    )(
+        coef, znear, ynear, xnear, yweight, xweight, share, layer_face, areal_face, state_v,
+        *in_hbm(right_side, pore_volume),
+    )
+    copies = call(merge_kernel, shape_of(columns, 40, 128), vmem(3), vmem(1)[0])(strip, share, base)
     shares = lax.all_to_all(copies, "gz", 0, 0)
 
     new_state, correction = call(
         sweep_kernel,
         [pltpu.HBM((3, *block), F32), pltpu.HBM((height, width), F32)],
-        vmem(3) + hbm(2) + vmem(2),
+        vmem(7),
         hbm(2),
         [
-            pltpu.VMEM((3, depth // 2, height, width), F32),
-            pltpu.VMEM((3, depth // 2, height, width), F32),
             pltpu.VMEM((3, *block), F32),
             pltpu.VMEM((height, width), F32),
-            pltpu.SemaphoreType.DMA((3, depth // CHUNK + 1)),
+            pltpu.SemaphoreType.DMA((depth // CHUNK + 1,)),
         ],
-    )(shares, layer_face, areal_face, *in_hbm(base0, gain0), base1, gain1)
+    )(shares, layer_face, areal_face, yweight, xweight, base, gain)
     return (new_state, correction)
 
 

time: 56.7 us -> 55.6 us (0.981)
  blocking collectives: 12.5 us -> 23.3 us
  waiting for transfers between devices: 5.72 us -> 1.23 us
  Pallas kernels: 13.4 us -> 9.53 us
  starting transfers between devices: 23.8 us -> 20.3 us
    all_to_all x0 -> x1, blocking collectives: none -> 9.19 us  [per_device(): shares = lax.all_to_all(copies, 'gz', 0, 0)]
    all_to_all x1 -> x0, starting transfers between devices: 6.24 us -> none  [per_device(): shares = lax.all_to_all(copies, 'gz', 0, 0)]
    all_to_all x1 -> x0, waiting for transfers between devices: 3.91 us -> none  [per_device(): shares = lax.all_to_all(copies, 'gz', 0, 0)]
    pallas_call x3 -> x2, Pallas kernels: 6.62 us -> 3.71 us  [the longest x1 3.7 us: per_device(): call(cells_kernel, [shape_of(3, *block)] * 2, vmem(10) + hbm(2), vmem(2),...]
    ppermute x6, starting transfers between devices: 15.6 us -> 18.4 us  [exchange(): return lax.ppermute(face, axis, pairs)]
    all_to_all x1, blocking collectives: 12.5 us -> 14.1 us  [per_device(): parts = lax.all_to_all(message, 'gz', 0, 0)]
    pallas_call x1, Pallas kernels: 3.09 us -> 2.1 us  [per_device(): call(sweep_kernel, [pltpu.HBM((3, *block), F32), pltpu.HBM((height, width...]
  transfers between devices with their start and end apart: 8 -> 7, of which waited for: 3 -> 1; matrix products, arithmetic and copies ran while one was open for 0% -> 0% of each run, Pallas kernels for 13% -> 10%
where the time goes in v5:
time: 55.6 us; the launch traced here: 55.2 us
  blocking collectives  23.3 us (42%)
  starting transfers between devices  20.3 us (37%)
  Pallas kernels  9.53 us (17%)
  waiting for transfers between devices  1.23 us (2%)
  between operations  0.77 us (1%)
    ppermute x6, starting transfers between devices, exchange(): return lax.ppermute(face, axis, pairs)  18.4 us
    all_to_all x1, blocking collectives, per_device(): parts = lax.all_to_all(message, 'gz', 0, 0)  14.1 us
    all_to_all x1, blocking collectives, per_device(): shares = lax.all_to_all(copies, 'gz', 0, 0)  9.19 us
    pallas_call x1, Pallas kernels, per_device(): call(cells_kernel, [shape_of(3, *block)] * 2, vmem(10) + hbm(2), vmem(2),...  3.7 us
    pallas_call x1, Pallas kernels, per_device(): call(sweep_kernel, [pltpu.HBM((3, *block), F32), pltpu.HBM((height, width...  2.1 us
    ppermute x1, starting transfers between devices, per_device(): strip = lax.ppermute(strip, ('gx', 'gy', 'gz'), pairs)  1.92 us
    pallas_call x1, Pallas kernels, per_device(): call(faces_kernel, [shape_of(3, *block), shape_of(*block)] + [shape_of(4,...  1.63 us
    pallas_call x1, Pallas kernels, per_device(): call(inner_kernel, [shape_of(18, depth, 128), shape_of(3, 2, 8, 128), sha...  1.6 us
  transfers between devices with their start and end apart: 7, of which 1 were waited for; matrix products, arithmetic and copies ran while one was open for 0% of the time, Pallas kernels for 10%

profile of v5, /device:TPU:96, one launch (start us, length us, event | category | flops | bytes accessed | tf_op | source)
XLA Modules:
  0.0 55.2 jit_solution(2892147163417339987)
XLA Ops:
  0.6 1.6 %shard_map.86 = (f32[3,16,40,128]{3,2,1,0:T(8,128)S(1)}, f32[16,40,128]{2,1,0:T(8,128)S(1)}, f32[4,40,128]{2,1,0:T(8,128)S(1)}, f32[4,40,128]{2,1,0:T(8,128)S(1)...) custom-call(f32[3,16,40,128]{3,2,1,0:T(8,128)} %state.1, ...), custom_call_target="tpu_custom_call" | custom-call | tf_op jit(solution)/shard_map/pallas_call | solution.py:485
  2.3 2.0 %collective-permute-start.2 = (f32[4,16,128]{2,1,0:T(8,128)S(1)}, f32[4,16,128]{2,1,0:T(8,128)S(1)}, u32[]{:S(2)}, u32[]{:S(2)}) collective-permute-start(f32[4,16,128]{2,1,0:T(8,128)S(1)} %get-tuple-element.32.yface0), channel_id=1, source_target_pairs={{0,8},{8,0},{16,24},{24,16},{32,40},{40,32},{48,56},{56,48},{64,72... | collective-permute-start | bytes 98312 | tf_op jit(solution)/shard_map/ppermute | solution.py:498
  4.3 0.7 %collective-permute-start.5 = (f32[4,2,8,128]{3,2,1,0:T(8,128)S(1)}, f32[4,2,8,128]{3,2,1,0:T(8,128)S(1)}, u32[]{:S(2)}, u32[]{:S(2)}) collective-permute-start(f32[4,2,8,128]{3,2,1,0:T(8,128)S(1)} %get-tuple-element.34.xpack), channel_id=1, source_target_pairs={{128,256},{256,128},{129,257},{257,129},{130,258},{258,130},{131,2... | collective-permute-start | bytes 98312 | tf_op jit(solution)/shard_map/ppermute | solution.py:498
  5.0 6.3 %collective-permute-start.4 = (f32[4,2,8,128]{3,2,1,0:T(8,128)S(1)}, f32[4,2,8,128]{3,2,1,0:T(8,128)S(1)}, u32[]{:S(2)}, u32[]{:S(2)}) collective-permute-start(f32[4,2,8,128]{3,2,1,0:T(8,128)S(1)} %get-tuple-element.34.xpack), channel_id=1, source_target_pairs={{0,128},{128,0},{256,384},{384,256},{1,129},{129,1},{257,385},{385... | collective-permute-start | bytes 98312 | tf_op jit(solution)/shard_map/ppermute | solution.py:498
  11.3 6.8 %collective-permute-start.3 = (f32[4,16,128]{2,1,0:T(8,128)S(1)}, f32[4,16,128]{2,1,0:T(8,128)S(1)}, u32[]{:S(2)}, u32[]{:S(2)}) collective-permute-start(f32[4,16,128]{2,1,0:T(8,128)S(1)} %get-tuple-element.33.yface1), channel_id=1, source_target_pairs={{8,16},{16,8},{24,32},{32,24},{40,48},{48,40},{56,64},{64,56},{72,... | collective-permute-start | bytes 98312 | tf_op jit(solution)/shard_map/ppermute | solution.py:498
  18.1 1.9 %collective-permute-start = (f32[4,40,128]{2,1,0:T(8,128)S(1)}, f32[4,40,128]{2,1,0:T(8,128)S(1)}, u32[]{:S(2)}, u32[]{:S(2)}) collective-permute-start(f32[4,40,128]{2,1,0:T(8,128)S(1)} %get-tuple-element.30.zface0), channel_id=1, source_target_pairs={{0,1},{1,0},{2,3},{3,2},{4,5},{5,4},{6,7},{7,6},{8,9},{9,8},{10,11... | collective-permute-start | bytes 245768 | tf_op jit(solution)/shard_map/ppermute | solution.py:498
  20.1 0.0 collective-permute-done.2.y0
  20.1 0.7 %collective-permute-start.1 = (f32[4,40,128]{2,1,0:T(8,128)S(1)}, f32[4,40,128]{2,1,0:T(8,128)S(1)}, u32[]{:S(2)}, u32[]{:S(2)}) collective-permute-start(f32[4,40,128]{2,1,0:T(8,128)S(1)} %get-tuple-element.31.zface1), channel_id=1, source_target_pairs={{1,2},{2,1},{3,4},{4,3},{5,6},{6,5},{9,10},{10,9},{11,12},{12,11},... | collective-permute-start | bytes 245768 | tf_op jit(solution)/shard_map/ppermute | solution.py:498
  20.7 1.6 %shard_map.87 = (f32[18,16,128]{2,1,0:T(8,128)S(1)}, f32[3,2,8,128]{3,2,1,0:T(8,128)S(1)}, f32[17,40,128]{2,1,0:T(8,128)S(1)}, f32[2,16,40,128]{3,2,1,0:T(8,128)S(1)}, f32[6,40,128]{2,1,0:T(8,128)S(1)}) custom-call(f32[3,16,40,128]{3,2,1,0:T(8,128)S(1)} %get-tuple-element.25.state, f32[16,40,128]{2,1,0:T(8,128)S(1)} %get-tuple-element.26.perm, ...), custom_call_target="tpu_custom_call" | custom-call | flops 2000000000 | bytes 2000000 | tf_op jit(solution)/shard_map/pallas_call | solution.py:504
  22.3 0.0 collective-permute-done.3.y1
  22.4 0.0 collective-permute-done.5.x1
  22.4 0.0 collective-permute-done.4.x0
  22.4 0.0 collective-permute-done.z0
  22.4 0.0 collective-permute-done.1.z1
  22.4 0.5 shard_map.88
  22.9 14.1 %all_to_all.10.parts = f32[8,40,128]{2,1,0:T(8,128)S(1)} all-to-all(f32[8,40,128]{2,1,0:T(8,128)S(1)} %get-tuple-element.36), channel_id=1, replica_groups=mesh['gx'=4,'gy'=16,'gz'=8] {'gz'}, dimensions={0} | all-to-all | bytes 327680 | tf_op jit(solution)/shard_map/all_to_all | solution.py:543
  37.0 1.9 %collective-permute-start.6 = (f32[32,128]{1,0:T(8,128)S(1)}, f32[32,128]{1,0:T(8,128)S(1)}, u32[]{:S(2)}, u32[]{:S(2)}) collective-permute-start(f32[32,128]{1,0:T(8,128)S(1)} %get-tuple-element.37), channel_id=1, source_target_pairs={{1,9},{3,131},{5,141},{8,0},{9,17},{11,139},{13,149},{14,134},{16,... | collective-permute-start | bytes 49160 | tf_op jit(solution)/shard_map/ppermute | solution.py:553
  38.9 3.7 %shard_map.90 = (f32[3,16,40,128]{3,2,1,0:T(8,128)S(1)}, f32[3,16,40,128]{3,2,1,0:T(8,128)S(1)}) custom-call(f32[18,16,128]{2,1,0:T(8,128)S(1)} %get-tuple-element.27.coef, f32[2,3,40,128]{3,2,1,0:T(8,128)S(1)} %get-tuple-element.39.znear, f32[2,3,16,128]{3,2,1,0:T(8,128)S(1)} %get-tuple-element.40.ynear, f32[3,2,8,128]{3,2,1,0:T(8,128)S(1)} %get-tuple-element.41.xnear, ...), custom_call_target="tpu_custom_call" | custom-call | flops 4000000000 | bytes 4000000 | tf_op jit(solution)/shard_map/pallas_call | solution.py:554
  42.6 1.2 %collective-permute-done.6.strip = f32[32,128]{1,0:T(8,128)S(1)} collective-permute-done((f32[32,128]{1,0:T(8,128)S(1)}, f32[32,128]{1,0:T(8,128)S(1)}, u32[]{:S(2)}, u32[]{:S(2)}) %collective-permute-start.6) | collective-permute-done | bytes 16416 | tf_op jit(solution)/shard_map/ppermute | solution.py:553
  43.9 9.2 %all_to_all.11.shares = f32[8,40,128]{2,1,0:T(8,128)S(1)} all-to-all(f32[8,40,128]{2,1,0:T(8,128)S(1)} %shard_map.91), channel_id=1, replica_groups=mesh['gx'=4,'gy'=16,'gz'=8] {'gz'}, dimensions={0} | all-to-all | bytes 327680 | tf_op jit(solution)/shard_map/all_to_all | solution.py:571
  53.1 2.1 %shard_map.92 = (f32[3,16,40,128]{3,2,1,0:T(8,128)}, f32[40,128]{1,0:T(8,128)}) custom-call(f32[8,40,128]{2,1,0:T(8,128)S(1)} %all_to_all.11.shares, f32[17,40,128]{2,1,0:T(8,128)S(1)} %get-tuple-element.44.layer_face, f32[2,16,40,128]{3,2,1,0:T(8,128)S(1)} %get-tuple-element.45.areal_face, f32[2,16,128]{2,1,0:T(8,128)S(1)} %get-tuple-element.42.yweight, ...), custom_call_target="tpu_custom_call" | custom-call | tf_op jit(solution)/shard_map/pallas_call | solution.py:573
  (2 shorter events, 0.0 us)
Async XLA Ops:
  2.3 17.8 %collective-permute-start.2 = (f32[4,16,128]{2,1,0:T(8,128)S(1)}, f32[4,16,128]{2,1,0:T(8,128)S(1)}, u32[]{:S(2)}, u32[]{:S(2)}) collective-permute-start(f32[4,16,128]{2,1,0:T(8,128)S(1)} %get-tuple-element.32.yface0), channel_id=1, source_target_pairs={{0,8},{8,0},{16,24},{24,16},{32,40},{40,32},{48,56},{56,48},{64,72... | collective-permute-start | bytes 98312 | tf_op jit(solution)/shard_map/ppermute | solution.py:498
  4.3 18.1 %collective-permute-start.5 = (f32[4,2,8,128]{3,2,1,0:T(8,128)S(1)}, f32[4,2,8,128]{3,2,1,0:T(8,128)S(1)}, u32[]{:S(2)}, u32[]{:S(2)}) collective-permute-start(f32[4,2,8,128]{3,2,1,0:T(8,128)S(1)} %get-tuple-element.34.xpack), channel_id=1, source_target_pairs={{128,256},{256,128},{129,257},{257,129},{130,258},{258,130},{131,2... | collective-permute-start | bytes 98312 | tf_op jit(solution)/shard_map/ppermute | solution.py:498
  5.0 17.4 %collective-permute-start.4 = (f32[4,2,8,128]{3,2,1,0:T(8,128)S(1)}, f32[4,2,8,128]{3,2,1,0:T(8,128)S(1)}, u32[]{:S(2)}, u32[]{:S(2)}) collective-permute-start(f32[4,2,8,128]{3,2,1,0:T(8,128)S(1)} %get-tuple-element.34.xpack), channel_id=1, source_target_pairs={{0,128},{128,0},{256,384},{384,256},{1,129},{129,1},{257,385},{385... | collective-permute-start | bytes 98312 | tf_op jit(solution)/shard_map/ppermute | solution.py:498
  11.3 11.1 %collective-permute-start.3 = (f32[4,16,128]{2,1,0:T(8,128)S(1)}, f32[4,16,128]{2,1,0:T(8,128)S(1)}, u32[]{:S(2)}, u32[]{:S(2)}) collective-permute-start(f32[4,16,128]{2,1,0:T(8,128)S(1)} %get-tuple-element.33.yface1), channel_id=1, source_target_pairs={{8,16},{16,8},{24,32},{32,24},{40,48},{48,40},{56,64},{64,56},{72,... | collective-permute-start | bytes 98312 | tf_op jit(solution)/shard_map/ppermute | solution.py:498
  18.1 4.3 %collective-permute-start = (f32[4,40,128]{2,1,0:T(8,128)S(1)}, f32[4,40,128]{2,1,0:T(8,128)S(1)}, u32[]{:S(2)}, u32[]{:S(2)}) collective-permute-start(f32[4,40,128]{2,1,0:T(8,128)S(1)} %get-tuple-element.30.zface0), channel_id=1, source_target_pairs={{0,1},{1,0},{2,3},{3,2},{4,5},{5,4},{6,7},{7,6},{8,9},{9,8},{10,11... | collective-permute-start | bytes 245768 | tf_op jit(solution)/shard_map/ppermute | solution.py:498
  20.1 2.3 %collective-permute-start.1 = (f32[4,40,128]{2,1,0:T(8,128)S(1)}, f32[4,40,128]{2,1,0:T(8,128)S(1)}, u32[]{:S(2)}, u32[]{:S(2)}) collective-permute-start(f32[4,40,128]{2,1,0:T(8,128)S(1)} %get-tuple-element.31.zface1), channel_id=1, source_target_pairs={{1,2},{2,1},{3,4},{4,3},{5,6},{6,5},{9,10},{10,9},{11,12},{12,11},... | collective-permute-start | bytes 245768 | tf_op jit(solution)/shard_map/ppermute | solution.py:498
  37.0 6.8 %collective-permute-start.6 = (f32[32,128]{1,0:T(8,128)S(1)}, f32[32,128]{1,0:T(8,128)S(1)}, u32[]{:S(2)}, u32[]{:S(2)}) collective-permute-start(f32[32,128]{1,0:T(8,128)S(1)} %get-tuple-element.37), channel_id=1, source_target_pairs={{1,9},{3,131},{5,141},{8,0},{9,17},{11,139},{13,149},{14,134},{16,... | collective-permute-start | bytes 49160 | tf_op jit(solution)/shard_map/ppermute | solution.py:553

commit v6 on v5

--- a/solution.py
+++ b/solution.py
@@ -11,6 +11,7 @@
 F32 = jnp.float32
 PARAMS = pltpu.CompilerParams(vmem_limit_bytes=16 * 2**20)
 CHUNK = 4
+PIECE = 8
 
 
 def vmem(count):
@@ -60,8 +61,8 @@
     tiles, half = height // 8, depth // 2
     fetch = pltpu.make_async_copy(perm, perm_half, sems.at[0])
     pieces = [
-        pltpu.make_async_copy(state.at[:, pl.ds(z, CHUNK)], state_v.at[:, pl.ds(z, CHUNK)], sems.at[1 + z // CHUNK])
-        for z in range(0, depth, CHUNK)
+        pltpu.make_async_copy(state.at[:, pl.ds(z, PIECE)], state_v.at[:, pl.ds(z, PIECE)], sems.at[1 + z // PIECE])
+        for z in range(0, depth, PIECE)
     ]
     fetch.start()
     for piece in pieces:
@@ -85,8 +86,8 @@
         perm_v[z] = perm_half[z].astype(F32)
         pack(3, z, perm_half[z].astype(F32))
     for z in range(depth):
-        if z % CHUNK == 0:
-            pieces[z // CHUNK].wait()
+        if z % PIECE == 0:
+            pieces[z // PIECE].wait()
         for c in range(3):
             pack(c, z, state_v[c, z])
     for c in range(4):
@@ -327,7 +328,7 @@
         k = [[coef[9 + 3 * r + c, z : z + 1, :] for c in range(3)] for r in range(3)]
         weights = [layer_face[z + 1], layer_face[z], *areal_weights(z, areal_face, yweight, xweight)]
         total = weights[0] + weights[1] + weights[2] + weights[3] + weights[4] + weights[5]
-        cells, flux = [], []
+        nearby = []
         for c in range(3):
             u = state[c, z]
             edges = edges_of(xnear[c, z // half], z % half, tiles)
@@ -339,17 +340,13 @@
                 jnp.where(lanes == width - 1, edges, turn(u, -1, 1)),
                 jnp.where(lanes == 0, edges, turn(u, 1, 1)),
             )
-            moved = weights[0] * (u - near[0])
+            moved = weights[0] * near[0]
             for w, n in zip(weights[1:], near[1:]):
-                moved = moved + w * (u - n)
-            cells.append(u)
-            flux.append(moved)
+                moved = moved + w * n
+            nearby.append(moved)
         v = pore[z].astype(F32)
-        residual = [
-            right[r, z]
-            - v * (m[r][0] * cells[0] + m[r][1] * cells[1] + m[r][2] * cells[2])
-            - (k[r][0] * flux[0] + k[r][1] * flux[1] + k[r][2] * flux[2])
-            for r in range(3)
+        source = [
+            right[r, z] + (k[r][0] * nearby[0] + k[r][1] * nearby[1] + k[r][2] * nearby[2]) for r in range(3)
         ]
         entries = [[v * m[r][c] + total * k[r][c] for c in range(3)] for r in range(3)]
 
@@ -363,8 +360,8 @@
         )
         scale = inverse(determinant)
         for r in range(3):
-            base[r, z] = cells[r] + scale * (
-                factors[0][r] * residual[0] + factors[1][r] * residual[1] + factors[2][r] * residual[2]
+            base[r, z] = scale * (
+                factors[0][r] * source[0] + factors[1][r] * source[1] + factors[2][r] * source[2]
             )
             gain[r, z] = scale * (factors[0][r] * k[0][0] + factors[1][r] * k[1][0] + factors[2][r] * k[2][0])
 
@@ -488,7 +485,7 @@
         + [shape_of(4, height, width)] * 2 + [shape_of(4, depth, width)] * 2 + [shape_of(4, 2, 8, 128)],
         hbm(2),
         vmem(7),
-        [pltpu.VMEM(block, bf16), pltpu.SemaphoreType.DMA((1 + depth // CHUNK,))],
+        [pltpu.VMEM(block, bf16), pltpu.SemaphoreType.DMA((1 + depth // PIECE,))],
     )(*in_hbm(state, permeability))
 
     def exchange(face, axis, odd):
@@ -520,7 +517,7 @@
             pltpu.SMEM(coupling_table.shape, F32),
             pltpu.SemaphoreType.DMA((5,)),
         ],
-        flops=2 * 10**9,
+        flops=10**8,
         moved=2 * 10**6,
     )(state_v, perm_v, *in_hbm(right_side, pore_volume, facies, storage_table, coupling_table))
 

time: 55.6 us -> 55 us (0.989)
  the two profiles are of different devices: /device:TPU:96 before, /device:TPU:104 now
where the time goes in v6:
time: 55 us; the launch traced here: 54.6 us
  blocking collectives  22.1 us (40%)
  starting transfers between devices  18.8 us (34%)
  Pallas kernels  9 us (16%)
  waiting for transfers between devices  3.91 us (7%)
  between operations  0.75 us (1%)
    ppermute x6, starting transfers between devices, exchange(): return lax.ppermute(face, axis, pairs)  16.9 us
    all_to_all x1, blocking collectives, per_device(): parts = lax.all_to_all(message, 'gz', 0, 0)  12.5 us
    all_to_all x1, blocking collectives, per_device(): shares = lax.all_to_all(copies, 'gz', 0, 0)  9.63 us
    pallas_call x1, Pallas kernels, per_device(): call(cells_kernel, [shape_of(3, *block)] * 2, vmem(10) + hbm(2), vmem(2),...  3.27 us
    ppermute x6, waiting for transfers between devices, exchange(): return lax.ppermute(face, axis, pairs)  2.28 us
    pallas_call x1, Pallas kernels, per_device(): call(sweep_kernel, [pltpu.HBM((3, *block), F32), pltpu.HBM((height, width...  2.1 us
    ppermute x1, starting transfers between devices, per_device(): strip = lax.ppermute(strip, ('gx', 'gy', 'gz'), pairs)  1.92 us
    ppermute x1, waiting for transfers between devices, per_device(): strip = lax.ppermute(strip, ('gx', 'gy', 'gz'), pairs)  1.64 us
  transfers between devices with their start and end apart: 7, of which 2 were waited for; matrix products, arithmetic and copies ran while one was open for 0% of the time, Pallas kernels for 9%

profile of v6, /device:TPU:104, one launch (start us, length us, event | category | flops | bytes accessed | tf_op | source)
XLA Modules:
  0.0 54.6 jit_solution(13158608117962469080)
XLA Ops:
  0.6 1.5 %shard_map.86 = (f32[3,16,40,128]{3,2,1,0:T(8,128)S(1)}, f32[16,40,128]{2,1,0:T(8,128)S(1)}, f32[4,40,128]{2,1,0:T(8,128)S(1)}, f32[4,40,128]{2,1,0:T(8,128)S(1)...) custom-call(f32[3,16,40,128]{3,2,1,0:T(8,128)} %state.1, ...), custom_call_target="tpu_custom_call" | custom-call | tf_op jit(solution)/shard_map/pallas_call | solution.py:482
  2.2 1.9 %collective-permute-start = (f32[4,40,128]{2,1,0:T(8,128)S(1)}, f32[4,40,128]{2,1,0:T(8,128)S(1)}, u32[]{:S(2)}, u32[]{:S(2)}) collective-permute-start(f32[4,40,128]{2,1,0:T(8,128)S(1)} %get-tuple-element.30.zface0), channel_id=1, source_target_pairs={{0,1},{1,0},{2,3},{3,2},{4,5},{5,4},{6,7},{7,6},{8,9},{9,8},{10,11... | collective-permute-start | bytes 245768 | tf_op jit(solution)/shard_map/ppermute | solution.py:495
  4.1 0.7 %collective-permute-start.1 = (f32[4,40,128]{2,1,0:T(8,128)S(1)}, f32[4,40,128]{2,1,0:T(8,128)S(1)}, u32[]{:S(2)}, u32[]{:S(2)}) collective-permute-start(f32[4,40,128]{2,1,0:T(8,128)S(1)} %get-tuple-element.31.zface1), channel_id=1, source_target_pairs={{1,2},{2,1},{3,4},{4,3},{5,6},{6,5},{9,10},{10,9},{11,12},{12,11},... | collective-permute-start | bytes 245768 | tf_op jit(solution)/shard_map/ppermute | solution.py:495
  4.8 2.0 %collective-permute-start.2 = (f32[4,16,128]{2,1,0:T(8,128)S(1)}, f32[4,16,128]{2,1,0:T(8,128)S(1)}, u32[]{:S(2)}, u32[]{:S(2)}) collective-permute-start(f32[4,16,128]{2,1,0:T(8,128)S(1)} %get-tuple-element.32.yface0), channel_id=1, source_target_pairs={{0,8},{8,0},{16,24},{24,16},{32,40},{40,32},{48,56},{56,48},{64,72... | collective-permute-start | bytes 98312 | tf_op jit(solution)/shard_map/ppermute | solution.py:495
  6.8 6.8 %collective-permute-start.3 = (f32[4,16,128]{2,1,0:T(8,128)S(1)}, f32[4,16,128]{2,1,0:T(8,128)S(1)}, u32[]{:S(2)}, u32[]{:S(2)}) collective-permute-start(f32[4,16,128]{2,1,0:T(8,128)S(1)} %get-tuple-element.33.yface1), channel_id=1, source_target_pairs={{8,16},{16,8},{24,32},{32,24},{40,48},{48,40},{56,64},{64,56},{72,... | collective-permute-start | bytes 98312 | tf_op jit(solution)/shard_map/ppermute | solution.py:495
  13.7 3.5 %collective-permute-start.5 = (f32[4,2,8,128]{3,2,1,0:T(8,128)S(1)}, f32[4,2,8,128]{3,2,1,0:T(8,128)S(1)}, u32[]{:S(2)}, u32[]{:S(2)}) collective-permute-start(f32[4,2,8,128]{3,2,1,0:T(8,128)S(1)} %get-tuple-element.34.xpack), channel_id=1, source_target_pairs={{128,256},{256,128},{129,257},{257,129},{130,258},{258,130},{131,2... | collective-permute-start | bytes 98312 | tf_op jit(solution)/shard_map/ppermute | solution.py:495
  17.2 0.0 collective-permute-done.2.y0
  17.2 1.9 %collective-permute-start.4 = (f32[4,2,8,128]{3,2,1,0:T(8,128)S(1)}, f32[4,2,8,128]{3,2,1,0:T(8,128)S(1)}, u32[]{:S(2)}, u32[]{:S(2)}) collective-permute-start(f32[4,2,8,128]{3,2,1,0:T(8,128)S(1)} %get-tuple-element.34.xpack), channel_id=1, source_target_pairs={{0,128},{128,0},{256,384},{384,256},{1,129},{129,1},{257,385},{385... | collective-permute-start | bytes 98312 | tf_op jit(solution)/shard_map/ppermute | solution.py:495
  19.1 1.6 %shard_map.87 = (f32[18,16,128]{2,1,0:T(8,128)S(1)}, f32[3,2,8,128]{3,2,1,0:T(8,128)S(1)}, f32[17,40,128]{2,1,0:T(8,128)S(1)}, f32[2,16,40,128]{3,2,1,0:T(8,128)S(1)}, f32[6,40,128]{2,1,0:T(8,128)S(1)}) custom-call(f32[3,16,40,128]{3,2,1,0:T(8,128)S(1)} %get-tuple-element.25.state, f32[16,40,128]{2,1,0:T(8,128)S(1)} %get-tuple-element.26.perm, ...), custom_call_target="tpu_custom_call" | custom-call | flops 100000000 | bytes 2000000 | tf_op jit(solution)/shard_map/pallas_call | solution.py:501
  20.7 0.0 collective-permute-done.3.y1
  20.7 0.0 collective-permute-done.5.x1
  20.7 2.3 %collective-permute-done.4.x0 = f32[4,2,8,128]{3,2,1,0:T(8,128)S(1)} collective-permute-done((f32[4,2,8,128]{3,2,1,0:T(8,128)S(1)}, f32[4,2,8,128]{3,2,1,0:T(8,128)S(1)}, u32[]{:S(2)}, u32[]{:S(2)}) %collective-permute-start.4) | collective-permute-done | bytes 32800 | tf_op jit(solution)/shard_map/ppermute | solution.py:495
  23.0 0.0 collective-permute-done.z0
  23.0 0.0 collective-permute-done.1.z1
  23.0 0.5 shard_map.88
  23.5 12.5 %all_to_all.10.parts = f32[8,40,128]{2,1,0:T(8,128)S(1)} all-to-all(f32[8,40,128]{2,1,0:T(8,128)S(1)} %get-tuple-element.36), channel_id=1, replica_groups=mesh['gx'=4,'gy'=16,'gz'=8] {'gz'}, dimensions={0} | all-to-all | bytes 327680 | tf_op jit(solution)/shard_map/all_to_all | solution.py:540
  36.0 1.9 %collective-permute-start.6 = (f32[32,128]{1,0:T(8,128)S(1)}, f32[32,128]{1,0:T(8,128)S(1)}, u32[]{:S(2)}, u32[]{:S(2)}) collective-permute-start(f32[32,128]{1,0:T(8,128)S(1)} %get-tuple-element.37), channel_id=1, source_target_pairs={{1,9},{3,131},{5,141},{8,0},{9,17},{11,139},{13,149},{14,134},{16,... | collective-permute-start | bytes 49160 | tf_op jit(solution)/shard_map/ppermute | solution.py:550
  37.9 3.3 %shard_map.90 = (f32[3,16,40,128]{3,2,1,0:T(8,128)S(1)}, f32[3,16,40,128]{3,2,1,0:T(8,128)S(1)}) custom-call(f32[18,16,128]{2,1,0:T(8,128)S(1)} %get-tuple-element.27.coef, f32[2,3,40,128]{3,2,1,0:T(8,128)S(1)} %get-tuple-element.39.znear, f32[2,3,16,128]{3,2,1,0:T(8,128)S(1)} %get-tuple-element.40.ynear, f32[3,2,8,128]{3,2,1,0:T(8,128)S(1)} %get-tuple-element.41.xnear, ...), custom_call_target="tpu_custom_call" | custom-call | flops 4000000000 | bytes 4000000 | tf_op jit(solution)/shard_map/pallas_call | solution.py:551
  41.2 1.6 %collective-permute-done.6.strip = f32[32,128]{1,0:T(8,128)S(1)} collective-permute-done((f32[32,128]{1,0:T(8,128)S(1)}, f32[32,128]{1,0:T(8,128)S(1)}, u32[]{:S(2)}, u32[]{:S(2)}) %collective-permute-start.6) | collective-permute-done | bytes 16416 | tf_op jit(solution)/shard_map/ppermute | solution.py:550
  42.8 9.6 %all_to_all.11.shares = f32[8,40,128]{2,1,0:T(8,128)S(1)} all-to-all(f32[8,40,128]{2,1,0:T(8,128)S(1)} %shard_map.91), channel_id=1, replica_groups=mesh['gx'=4,'gy'=16,'gz'=8] {'gz'}, dimensions={0} | all-to-all | bytes 327680 | tf_op jit(solution)/shard_map/all_to_all | solution.py:568
  52.5 2.1 %shard_map.92 = (f32[3,16,40,128]{3,2,1,0:T(8,128)}, f32[40,128]{1,0:T(8,128)}) custom-call(f32[8,40,128]{2,1,0:T(8,128)S(1)} %all_to_all.11.shares, f32[17,40,128]{2,1,0:T(8,128)S(1)} %get-tuple-element.44.layer_face, f32[2,16,40,128]{3,2,1,0:T(8,128)S(1)} %get-tuple-element.45.areal_face, f32[2,16,128]{2,1,0:T(8,128)S(1)} %get-tuple-element.42.yweight, ...), custom_call_target="tpu_custom_call" | custom-call | tf_op jit(solution)/shard_map/pallas_call | solution.py:570
  (2 shorter events, 0.0 us)
Async XLA Ops:
  2.2 20.8 %collective-permute-start = (f32[4,40,128]{2,1,0:T(8,128)S(1)}, f32[4,40,128]{2,1,0:T(8,128)S(1)}, u32[]{:S(2)}, u32[]{:S(2)}) collective-permute-start(f32[4,40,128]{2,1,0:T(8,128)S(1)} %get-tuple-element.30.zface0), channel_id=1, source_target_pairs={{0,1},{1,0},{2,3},{3,2},{4,5},{5,4},{6,7},{7,6},{8,9},{9,8},{10,11... | collective-permute-start | bytes 245768 | tf_op jit(solution)/shard_map/ppermute | solution.py:495
  4.1 18.9 %collective-permute-start.1 = (f32[4,40,128]{2,1,0:T(8,128)S(1)}, f32[4,40,128]{2,1,0:T(8,128)S(1)}, u32[]{:S(2)}, u32[]{:S(2)}) collective-permute-start(f32[4,40,128]{2,1,0:T(8,128)S(1)} %get-tuple-element.31.zface1), channel_id=1, source_target_pairs={{1,2},{2,1},{3,4},{4,3},{5,6},{6,5},{9,10},{10,9},{11,12},{12,11},... | collective-permute-start | bytes 245768 | tf_op jit(solution)/shard_map/ppermute | solution.py:495
  4.8 12.4 %collective-permute-start.2 = (f32[4,16,128]{2,1,0:T(8,128)S(1)}, f32[4,16,128]{2,1,0:T(8,128)S(1)}, u32[]{:S(2)}, u32[]{:S(2)}) collective-permute-start(f32[4,16,128]{2,1,0:T(8,128)S(1)} %get-tuple-element.32.yface0), channel_id=1, source_target_pairs={{0,8},{8,0},{16,24},{24,16},{32,40},{40,32},{48,56},{56,48},{64,72... | collective-permute-start | bytes 98312 | tf_op jit(solution)/shard_map/ppermute | solution.py:495
  6.8 13.9 %collective-permute-start.3 = (f32[4,16,128]{2,1,0:T(8,128)S(1)}, f32[4,16,128]{2,1,0:T(8,128)S(1)}, u32[]{:S(2)}, u32[]{:S(2)}) collective-permute-start(f32[4,16,128]{2,1,0:T(8,128)S(1)} %get-tuple-element.33.yface1), channel_id=1, source_target_pairs={{8,16},{16,8},{24,32},{32,24},{40,48},{48,40},{56,64},{64,56},{72,... | collective-permute-start | bytes 98312 | tf_op jit(solution)/shard_map/ppermute | solution.py:495
  13.7 7.0 %collective-permute-start.5 = (f32[4,2,8,128]{3,2,1,0:T(8,128)S(1)}, f32[4,2,8,128]{3,2,1,0:T(8,128)S(1)}, u32[]{:S(2)}, u32[]{:S(2)}) collective-permute-start(f32[4,2,8,128]{3,2,1,0:T(8,128)S(1)} %get-tuple-element.34.xpack), channel_id=1, source_target_pairs={{128,256},{256,128},{129,257},{257,129},{130,258},{258,130},{131,2... | collective-permute-start | bytes 98312 | tf_op jit(solution)/shard_map/ppermute | solution.py:495
  17.2 5.8 %collective-permute-start.4 = (f32[4,2,8,128]{3,2,1,0:T(8,128)S(1)}, f32[4,2,8,128]{3,2,1,0:T(8,128)S(1)}, u32[]{:S(2)}, u32[]{:S(2)}) collective-permute-start(f32[4,2,8,128]{3,2,1,0:T(8,128)S(1)} %get-tuple-element.34.xpack), channel_id=1, source_target_pairs={{0,128},{128,0},{256,384},{384,256},{1,129},{129,1},{257,385},{385... | collective-permute-start | bytes 98312 | tf_op jit(solution)/shard_map/ppermute | solution.py:495
  36.0 6.8 %collective-permute-start.6 = (f32[32,128]{1,0:T(8,128)S(1)}, f32[32,128]{1,0:T(8,128)S(1)}, u32[]{:S(2)}, u32[]{:S(2)}) collective-permute-start(f32[32,128]{1,0:T(8,128)S(1)} %get-tuple-element.37), channel_id=1, source_target_pairs={{1,9},{3,131},{5,141},{8,0},{9,17},{11,139},{13,149},{14,134},{16,... | collective-permute-start | bytes 49160 | tf_op jit(solution)/shard_map/ppermute | solution.py:550

commit v7 on v6

--- a/solution.py
+++ b/solution.py
@@ -517,7 +517,7 @@
             pltpu.SMEM(coupling_table.shape, F32),
             pltpu.SemaphoreType.DMA((5,)),
         ],
-        flops=10**8,
+        flops=6 * 10**8,
         moved=2 * 10**6,
     )(state_v, perm_v, *in_hbm(right_side, pore_volume, facies, storage_table, coupling_table))
 

time: 55 us -> 54.1 us (0.984)
  the two profiles are of different devices: /device:TPU:104 before, /device:TPU:96 now
where the time goes in v7:
time: 54.1 us; the launch traced here: 53.7 us
  blocking collectives  21.7 us (40%)
  starting transfers between devices  20.3 us (38%)
  Pallas kernels  9.01 us (17%)
  waiting for transfers between devices  1.93 us (4%)
  between operations  0.75 us (1%)
    ppermute x6, starting transfers between devices, exchange(): return lax.ppermute(face, axis, pairs)  18.4 us
    all_to_all x1, blocking collectives, per_device(): parts = lax.all_to_all(message, 'gz', 0, 0)  12.5 us
    all_to_all x1, blocking collectives, per_device(): shares = lax.all_to_all(copies, 'gz', 0, 0)  9.19 us
    pallas_call x1, Pallas kernels, per_device(): call(cells_kernel, [shape_of(3, *block)] * 2, vmem(10) + hbm(2), vmem(2),...  3.27 us
    pallas_call x1, Pallas kernels, per_device(): call(sweep_kernel, [pltpu.HBM((3, *block), F32), pltpu.HBM((height, width...  2.1 us
    ppermute x1, starting transfers between devices, per_device(): strip = lax.ppermute(strip, ('gx', 'gy', 'gz'), pairs)  1.92 us
    ppermute x1, waiting for transfers between devices, per_device(): strip = lax.ppermute(strip, ('gx', 'gy', 'gz'), pairs)  1.64 us
    pallas_call x1, Pallas kernels, per_device(): call(inner_kernel, [shape_of(18, depth, 128), shape_of(3, 2, 8, 128), sha...  1.59 us
  transfers between devices with their start and end apart: 7, of which 2 were waited for; matrix products, arithmetic and copies ran while one was open for 0% of the time, Pallas kernels for 9%

profile of v7, /device:TPU:96, one launch (start us, length us, event | category | flops | bytes accessed | tf_op | source)
XLA Modules:
  0.0 53.7 jit_solution(4027450553509232368)
XLA Ops:
  0.6 1.5 %shard_map.86 = (f32[3,16,40,128]{3,2,1,0:T(8,128)S(1)}, f32[16,40,128]{2,1,0:T(8,128)S(1)}, f32[4,40,128]{2,1,0:T(8,128)S(1)}, f32[4,40,128]{2,1,0:T(8,128)S(1)...) custom-call(f32[3,16,40,128]{3,2,1,0:T(8,128)} %state.1, ...), custom_call_target="tpu_custom_call" | custom-call | tf_op jit(solution)/shard_map/pallas_call | solution.py:482
  2.2 2.0 %collective-permute-start.2 = (f32[4,16,128]{2,1,0:T(8,128)S(1)}, f32[4,16,128]{2,1,0:T(8,128)S(1)}, u32[]{:S(2)}, u32[]{:S(2)}) collective-permute-start(f32[4,16,128]{2,1,0:T(8,128)S(1)} %get-tuple-element.32.yface0), channel_id=1, source_target_pairs={{0,8},{8,0},{16,24},{24,16},{32,40},{40,32},{48,56},{56,48},{64,72... | collective-permute-start | bytes 98312 | tf_op jit(solution)/shard_map/ppermute | solution.py:495
  4.2 1.9 %collective-permute-start = (f32[4,40,128]{2,1,0:T(8,128)S(1)}, f32[4,40,128]{2,1,0:T(8,128)S(1)}, u32[]{:S(2)}, u32[]{:S(2)}) collective-permute-start(f32[4,40,128]{2,1,0:T(8,128)S(1)} %get-tuple-element.30.zface0), channel_id=1, source_target_pairs={{0,1},{1,0},{2,3},{3,2},{4,5},{5,4},{6,7},{7,6},{8,9},{9,8},{10,11... | collective-permute-start | bytes 245768 | tf_op jit(solution)/shard_map/ppermute | solution.py:495
  6.1 0.7 %collective-permute-start.1 = (f32[4,40,128]{2,1,0:T(8,128)S(1)}, f32[4,40,128]{2,1,0:T(8,128)S(1)}, u32[]{:S(2)}, u32[]{:S(2)}) collective-permute-start(f32[4,40,128]{2,1,0:T(8,128)S(1)} %get-tuple-element.31.zface1), channel_id=1, source_target_pairs={{1,2},{2,1},{3,4},{4,3},{5,6},{6,5},{9,10},{10,9},{11,12},{12,11},... | collective-permute-start | bytes 245768 | tf_op jit(solution)/shard_map/ppermute | solution.py:495
  6.8 0.7 %collective-permute-start.5 = (f32[4,2,8,128]{3,2,1,0:T(8,128)S(1)}, f32[4,2,8,128]{3,2,1,0:T(8,128)S(1)}, u32[]{:S(2)}, u32[]{:S(2)}) collective-permute-start(f32[4,2,8,128]{3,2,1,0:T(8,128)S(1)} %get-tuple-element.34.xpack), channel_id=1, source_target_pairs={{128,256},{256,128},{129,257},{257,129},{130,258},{258,130},{131,2... | collective-permute-start | bytes 98312 | tf_op jit(solution)/shard_map/ppermute | solution.py:495
  7.5 6.3 %collective-permute-start.4 = (f32[4,2,8,128]{3,2,1,0:T(8,128)S(1)}, f32[4,2,8,128]{3,2,1,0:T(8,128)S(1)}, u32[]{:S(2)}, u32[]{:S(2)}) collective-permute-start(f32[4,2,8,128]{3,2,1,0:T(8,128)S(1)} %get-tuple-element.34.xpack), channel_id=1, source_target_pairs={{0,128},{128,0},{256,384},{384,256},{1,129},{129,1},{257,385},{385... | collective-permute-start | bytes 98312 | tf_op jit(solution)/shard_map/ppermute | solution.py:495
  13.8 0.0 collective-permute-done.2.y0
  13.8 6.8 %collective-permute-start.3 = (f32[4,16,128]{2,1,0:T(8,128)S(1)}, f32[4,16,128]{2,1,0:T(8,128)S(1)}, u32[]{:S(2)}, u32[]{:S(2)}) collective-permute-start(f32[4,16,128]{2,1,0:T(8,128)S(1)} %get-tuple-element.33.yface1), channel_id=1, source_target_pairs={{8,16},{16,8},{24,32},{32,24},{40,48},{48,40},{56,64},{64,56},{72,... | collective-permute-start | bytes 98312 | tf_op jit(solution)/shard_map/ppermute | solution.py:495
  20.7 1.6 %shard_map.87 = (f32[18,16,128]{2,1,0:T(8,128)S(1)}, f32[3,2,8,128]{3,2,1,0:T(8,128)S(1)}, f32[17,40,128]{2,1,0:T(8,128)S(1)}, f32[2,16,40,128]{3,2,1,0:T(8,128)S(1)}, f32[6,40,128]{2,1,0:T(8,128)S(1)}) custom-call(f32[3,16,40,128]{3,2,1,0:T(8,128)S(1)} %get-tuple-element.25.state, f32[16,40,128]{2,1,0:T(8,128)S(1)} %get-tuple-element.26.perm, ...), custom_call_target="tpu_custom_call" | custom-call | flops 600000000 | bytes 2000000 | tf_op jit(solution)/shard_map/pallas_call | solution.py:501
  22.3 0.3 collective-permute-done.3.y1
  22.5 0.0 collective-permute-done.5.x1
  22.5 0.0 collective-permute-done.4.x0
  22.5 0.0 collective-permute-done.z0
  22.5 0.0 collective-permute-done.1.z1
  22.6 0.5 shard_map.88
  23.1 12.5 %all_to_all.10.parts = f32[8,40,128]{2,1,0:T(8,128)S(1)} all-to-all(f32[8,40,128]{2,1,0:T(8,128)S(1)} %get-tuple-element.36), channel_id=1, replica_groups=mesh['gx'=4,'gy'=16,'gz'=8] {'gz'}, dimensions={0} | all-to-all | bytes 327680 | tf_op jit(solution)/shard_map/all_to_all | solution.py:540
  35.6 1.9 %collective-permute-start.6 = (f32[32,128]{1,0:T(8,128)S(1)}, f32[32,128]{1,0:T(8,128)S(1)}, u32[]{:S(2)}, u32[]{:S(2)}) collective-permute-start(f32[32,128]{1,0:T(8,128)S(1)} %get-tuple-element.37), channel_id=1, source_target_pairs={{1,9},{3,131},{5,141},{8,0},{9,17},{11,139},{13,149},{14,134},{16,... | collective-permute-start | bytes 49160 | tf_op jit(solution)/shard_map/ppermute | solution.py:550
  37.5 3.3 %shard_map.90 = (f32[3,16,40,128]{3,2,1,0:T(8,128)S(1)}, f32[3,16,40,128]{3,2,1,0:T(8,128)S(1)}) custom-call(f32[18,16,128]{2,1,0:T(8,128)S(1)} %get-tuple-element.27.coef, f32[2,3,40,128]{3,2,1,0:T(8,128)S(1)} %get-tuple-element.39.znear, f32[2,3,16,128]{3,2,1,0:T(8,128)S(1)} %get-tuple-element.40.ynear, f32[3,2,8,128]{3,2,1,0:T(8,128)S(1)} %get-tuple-element.41.xnear, ...), custom_call_target="tpu_custom_call" | custom-call | flops 4000000000 | bytes 4000000 | tf_op jit(solution)/shard_map/pallas_call | solution.py:551
  40.8 1.6 %collective-permute-done.6.strip = f32[32,128]{1,0:T(8,128)S(1)} collective-permute-done((f32[32,128]{1,0:T(8,128)S(1)}, f32[32,128]{1,0:T(8,128)S(1)}, u32[]{:S(2)}, u32[]{:S(2)}) %collective-permute-start.6) | collective-permute-done | bytes 16416 | tf_op jit(solution)/shard_map/ppermute | solution.py:550
  42.4 9.2 %all_to_all.11.shares = f32[8,40,128]{2,1,0:T(8,128)S(1)} all-to-all(f32[8,40,128]{2,1,0:T(8,128)S(1)} %shard_map.91), channel_id=1, replica_groups=mesh['gx'=4,'gy'=16,'gz'=8] {'gz'}, dimensions={0} | all-to-all | bytes 327680 | tf_op jit(solution)/shard_map/all_to_all | solution.py:568
  51.6 2.1 %shard_map.92 = (f32[3,16,40,128]{3,2,1,0:T(8,128)}, f32[40,128]{1,0:T(8,128)}) custom-call(f32[8,40,128]{2,1,0:T(8,128)S(1)} %all_to_all.11.shares, f32[17,40,128]{2,1,0:T(8,128)S(1)} %get-tuple-element.44.layer_face, f32[2,16,40,128]{3,2,1,0:T(8,128)S(1)} %get-tuple-element.45.areal_face, f32[2,16,128]{2,1,0:T(8,128)S(1)} %get-tuple-element.42.yweight, ...), custom_call_target="tpu_custom_call" | custom-call | tf_op jit(solution)/shard_map/pallas_call | solution.py:570
  (2 shorter events, 0.0 us)
Async XLA Ops:
  2.2 11.6 %collective-permute-start.2 = (f32[4,16,128]{2,1,0:T(8,128)S(1)}, f32[4,16,128]{2,1,0:T(8,128)S(1)}, u32[]{:S(2)}, u32[]{:S(2)}) collective-permute-start(f32[4,16,128]{2,1,0:T(8,128)S(1)} %get-tuple-element.32.yface0), channel_id=1, source_target_pairs={{0,8},{8,0},{16,24},{24,16},{32,40},{40,32},{48,56},{56,48},{64,72... | collective-permute-start | bytes 98312 | tf_op jit(solution)/shard_map/ppermute | solution.py:495
  4.2 18.3 %collective-permute-start = (f32[4,40,128]{2,1,0:T(8,128)S(1)}, f32[4,40,128]{2,1,0:T(8,128)S(1)}, u32[]{:S(2)}, u32[]{:S(2)}) collective-permute-start(f32[4,40,128]{2,1,0:T(8,128)S(1)} %get-tuple-element.30.zface0), channel_id=1, source_target_pairs={{0,1},{1,0},{2,3},{3,2},{4,5},{5,4},{6,7},{7,6},{8,9},{9,8},{10,11... | collective-permute-start | bytes 245768 | tf_op jit(solution)/shard_map/ppermute | solution.py:495
  6.1 16.4 %collective-permute-start.1 = (f32[4,40,128]{2,1,0:T(8,128)S(1)}, f32[4,40,128]{2,1,0:T(8,128)S(1)}, u32[]{:S(2)}, u32[]{:S(2)}) collective-permute-start(f32[4,40,128]{2,1,0:T(8,128)S(1)} %get-tuple-element.31.zface1), channel_id=1, source_target_pairs={{1,2},{2,1},{3,4},{4,3},{5,6},{6,5},{9,10},{10,9},{11,12},{12,11},... | collective-permute-start | bytes 245768 | tf_op jit(solution)/shard_map/ppermute | solution.py:495
  6.8 15.7 %collective-permute-start.5 = (f32[4,2,8,128]{3,2,1,0:T(8,128)S(1)}, f32[4,2,8,128]{3,2,1,0:T(8,128)S(1)}, u32[]{:S(2)}, u32[]{:S(2)}) collective-permute-start(f32[4,2,8,128]{3,2,1,0:T(8,128)S(1)} %get-tuple-element.34.xpack), channel_id=1, source_target_pairs={{128,256},{256,128},{129,257},{257,129},{130,258},{258,130},{131,2... | collective-permute-start | bytes 98312 | tf_op jit(solution)/shard_map/ppermute | solution.py:495
  7.5 15.1 %collective-permute-start.4 = (f32[4,2,8,128]{3,2,1,0:T(8,128)S(1)}, f32[4,2,8,128]{3,2,1,0:T(8,128)S(1)}, u32[]{:S(2)}, u32[]{:S(2)}) collective-permute-start(f32[4,2,8,128]{3,2,1,0:T(8,128)S(1)} %get-tuple-element.34.xpack), channel_id=1, source_target_pairs={{0,128},{128,0},{256,384},{384,256},{1,129},{129,1},{257,385},{385... | collective-permute-start | bytes 98312 | tf_op jit(solution)/shard_map/ppermute | solution.py:495
  13.8 8.7 %collective-permute-start.3 = (f32[4,16,128]{2,1,0:T(8,128)S(1)}, f32[4,16,128]{2,1,0:T(8,128)S(1)}, u32[]{:S(2)}, u32[]{:S(2)}) collective-permute-start(f32[4,16,128]{2,1,0:T(8,128)S(1)} %get-tuple-element.33.yface1), channel_id=1, source_target_pairs={{8,16},{16,8},{24,32},{32,24},{40,48},{48,40},{56,64},{64,56},{72,... | collective-permute-start | bytes 98312 | tf_op jit(solution)/shard_map/ppermute | solution.py:495
  35.6 6.8 %collective-permute-start.6 = (f32[32,128]{1,0:T(8,128)S(1)}, f32[32,128]{1,0:T(8,128)S(1)}, u32[]{:S(2)}, u32[]{:S(2)}) collective-permute-start(f32[32,128]{1,0:T(8,128)S(1)} %get-tuple-element.37), channel_id=1, source_target_pairs={{1,9},{3,131},{5,141},{8,0},{9,17},{11,139},{13,149},{14,134},{16,... | collective-permute-start | bytes 49160 | tf_op jit(solution)/shard_map/ppermute | solution.py:550

commit v8 on v7

--- a/solution.py
+++ b/solution.py
@@ -100,8 +100,8 @@
 
 def inner_kernel(
     state, perm, right, pore, facies, storage_table, coupling_table,
-    coef, coef_lane, layer_face, areal_face, acc,
-    right_v, pore_v, facies_s, storage_s, coupling_s, sems,
+    coef, coef_lane, layer_face, areal_face, acc, right_head, pore_v,
+    right_v, facies_s, storage_s, coupling_s, sems,
 ):
     depth, height, width = perm.shape
     tiles, half = height // 8, depth // 2
@@ -114,6 +114,7 @@
                 (coupling_table, coupling_s),
                 (pore, pore_v),
                 (right.at[0], right_v),
+                (right.at[:, pl.ds(0, CHUNK)], right_head),
             )
         )
     ]
@@ -152,7 +153,7 @@
             for f in range(kinds):
                 lane_of = jnp.where(fids_lane[h] == f, coupling_s[0, f, k], lane_of)
             coef_lane[k, h] = lane_of
-    for copy in copies[3:]:
+    for copy in copies[3:5]:
         copy.wait()
 
     for a in range(6):
@@ -175,6 +176,7 @@
         acc[3] += k0[0] * tx
         acc[4] += ty * (w - turn(w, -1, 0))
         acc[5] += tx * (w - turn(w, -1, 1))
+    copies[5].wait()
 
 
 def outer_kernel(
@@ -303,25 +305,20 @@
 
 
 def cells_kernel(
-    coef, znear, ynear, xnear, yweight, xweight, order, layer_face, areal_face, state, right_in, pore_in,
+    coef, znear, ynear, xnear, yweight, xweight, order, layer_face, areal_face, state, right_head, pore, right_in,
     base, gain,
-    right, pore, sems,
+    right, sems,
 ):
     del order
     depth, height, width = pore.shape
     tiles, half = height // 8, depth // 2
     rows = row_index((height, width))
     lanes = lane_index((height, width))
-    arrivals = []
-    for p in range(depth // CHUNK):
+    arrivals = {}
+    for p in range(1, depth // CHUNK):
         here = pl.ds(p * CHUNK, CHUNK)
-        arrivals.append([
-            pltpu.make_async_copy(right_in.at[:, here], right.at[:, here], sems.at[0, p]),
-            pltpu.make_async_copy(pore_in.at[here], pore.at[here], sems.at[1, p]),
-        ])
-    for group in arrivals:
-        for copy in group:
-            copy.start()
+        arrivals[p] = pltpu.make_async_copy(right_in.at[:, here], right.at[:, here], sems.at[p])
+        arrivals[p].start()
 
     def layer(z):
         m = [[coef[3 * r + c, z : z + 1, :] for c in range(3)] for r in range(3)]
@@ -346,7 +343,7 @@
             nearby.append(moved)
         v = pore[z].astype(F32)
         source = [
-            right[r, z] + (k[r][0] * nearby[0] + k[r][1] * nearby[1] + k[r][2] * nearby[2]) for r in range(3)
+            (right_head if z < CHUNK else right)[r, z] + (k[r][0] * nearby[0] + k[r][1] * nearby[1] + k[r][2] * nearby[2]) for r in range(3)
         ]
         entries = [[v * m[r][c] + total * k[r][c] for c in range(3)] for r in range(3)]
 
@@ -366,9 +363,8 @@
             gain[r, z] = scale * (factors[0][r] * k[0][0] + factors[1][r] * k[1][0] + factors[2][r] * k[2][0])
 
     for z in range(depth):
-        if z % CHUNK == 0:
-            for copy in arrivals[z // CHUNK]:
-                copy.wait()
+        if z and z % CHUNK == 0:
+            arrivals[z // CHUNK].wait()
         layer(z)
 
 
@@ -498,7 +494,7 @@
     for axis, first, second in (("gz", zface0, zface1), ("gy", yface0, yface1), ("gx", xpack, xpack)):
         received += [exchange(first, axis, 0), exchange(second, axis, 1)]
 
-    coef, coef_lane, layer_face, areal_face, acc = call(
+    coef, coef_lane, layer_face, areal_face, acc, right_head, pore_v = call(
         inner_kernel,
         [
             shape_of(18, depth, 128),
@@ -506,16 +502,17 @@
             shape_of(depth + 1, height, width),
             shape_of(2, *block),
             shape_of(6, height, width),
+            shape_of(3, CHUNK, height, width),
+            jax.ShapeDtypeStruct(block, bf16),
         ],
         vmem(2) + hbm(5),
-        vmem(5),
+        vmem(7),
         [
             pltpu.VMEM(block, F32),
-            pltpu.VMEM(block, bf16),
             pltpu.SMEM(facies.shape, jnp.int32),
             pltpu.SMEM(storage_table.shape, F32),
             pltpu.SMEM(coupling_table.shape, F32),
-            pltpu.SemaphoreType.DMA((5,)),
+            pltpu.SemaphoreType.DMA((6,)),
         ],
         flops=6 * 10**8,
         moved=2 * 10**6,
@@ -551,18 +548,14 @@
     base, gain = call(
         cells_kernel,
         [shape_of(3, *block)] * 2,
-        vmem(10) + hbm(2),
+        vmem(12) + hbm(1),
         vmem(2),
-        [
-            pltpu.VMEM((3, *block), F32),
-            pltpu.VMEM(block, bf16),
-            pltpu.SemaphoreType.DMA((2, depth // CHUNK)),
-        ],
+        [pltpu.VMEM((3, *block), F32), pltpu.SemaphoreType.DMA((depth // CHUNK,))],
         flops=4 * 10**9,
         moved=4 * 10**6,
     )(
         coef, znear, ynear, xnear, yweight, xweight, share, layer_face, areal_face, state_v,
-        *in_hbm(right_side, pore_volume),
+        right_head, pore_v, *in_hbm(right_side),
     )
     copies = call(merge_kernel, shape_of(columns, 40, 128), vmem(3), vmem(1)[0])(strip, share, base)
     shares = lax.all_to_all(copies, "gz", 0, 0)

time: 54.1 us -> 54 us (level)
  transfers between devices with their start and end apart: 7 -> 7, of which waited for: 2 -> 2; matrix products, arithmetic and copies ran while one was open for 0% -> 0% of each run, Pallas kernels for 9% -> 8%
where the time goes in v8:
time: 54 us; the launch traced here: 53.6 us
  blocking collectives  21.7 us (40%)
  starting transfers between devices  20.3 us (38%)
  Pallas kernels  8.59 us (16%)
  waiting for transfers between devices  2.29 us (4%)
  between operations  0.75 us (1%)
    ppermute x6, starting transfers between devices, exchange(): return lax.ppermute(face, axis, pairs)  18.4 us
    all_to_all x1, blocking collectives, per_device(): parts = lax.all_to_all(message, 'gz', 0, 0)  12.5 us
    all_to_all x1, blocking collectives, per_device(): shares = lax.all_to_all(copies, 'gz', 0, 0)  9.19 us
    pallas_call x1, Pallas kernels, per_device(): call(cells_kernel, [shape_of(3, *block)] * 2, vmem(12) + hbm(1), vmem(2),...  2.91 us
    pallas_call x1, Pallas kernels, per_device(): call(sweep_kernel, [pltpu.HBM((3, *block), F32), pltpu.HBM((height, width...  2.02 us
    ppermute x1, waiting for transfers between devices, per_device(): strip = lax.ppermute(strip, ('gx', 'gy', 'gz'), pairs)  2 us
    ppermute x1, starting transfers between devices, per_device(): strip = lax.ppermute(strip, ('gx', 'gy', 'gz'), pairs)  1.92 us
    pallas_call x1, Pallas kernels, per_device(): call(inner_kernel, [shape_of(18, depth, 128), shape_of(3, 2, 8, 128), sha...  1.59 us
  transfers between devices with their start and end apart: 7, of which 2 were waited for; matrix products, arithmetic and copies ran while one was open for 0% of the time, Pallas kernels for 8%

profile of v8, /device:TPU:96, one launch (start us, length us, event | category | flops | bytes accessed | tf_op | source)
XLA Modules:
  0.0 53.6 jit_solution(7639451336546460222)
XLA Ops:
  0.6 1.5 %shard_map.86 = (f32[3,16,40,128]{3,2,1,0:T(8,128)S(1)}, f32[16,40,128]{2,1,0:T(8,128)S(1)}, f32[4,40,128]{2,1,0:T(8,128)S(1)}, f32[4,40,128]{2,1,0:T(8,128)S(1)...) custom-call(f32[3,16,40,128]{3,2,1,0:T(8,128)} %state.1, ...), custom_call_target="tpu_custom_call" | custom-call | tf_op jit(solution)/shard_map/pallas_call | solution.py:478
  2.2 2.0 %collective-permute-start.2 = (f32[4,16,128]{2,1,0:T(8,128)S(1)}, f32[4,16,128]{2,1,0:T(8,128)S(1)}, u32[]{:S(2)}, u32[]{:S(2)}) collective-permute-start(f32[4,16,128]{2,1,0:T(8,128)S(1)} %get-tuple-element.34.yface0), channel_id=1, source_target_pairs={{0,8},{8,0},{16,24},{24,16},{32,40},{40,32},{48,56},{56,48},{64,72... | collective-permute-start | bytes 98312 | tf_op jit(solution)/shard_map/ppermute | solution.py:491
  4.2 1.9 %collective-permute-start = (f32[4,40,128]{2,1,0:T(8,128)S(1)}, f32[4,40,128]{2,1,0:T(8,128)S(1)}, u32[]{:S(2)}, u32[]{:S(2)}) collective-permute-start(f32[4,40,128]{2,1,0:T(8,128)S(1)} %get-tuple-element.32.zface0), channel_id=1, source_target_pairs={{0,1},{1,0},{2,3},{3,2},{4,5},{5,4},{6,7},{7,6},{8,9},{9,8},{10,11... | collective-permute-start | bytes 245768 | tf_op jit(solution)/shard_map/ppermute | solution.py:491
  6.1 0.7 %collective-permute-start.1 = (f32[4,40,128]{2,1,0:T(8,128)S(1)}, f32[4,40,128]{2,1,0:T(8,128)S(1)}, u32[]{:S(2)}, u32[]{:S(2)}) collective-permute-start(f32[4,40,128]{2,1,0:T(8,128)S(1)} %get-tuple-element.33.zface1), channel_id=1, source_target_pairs={{1,2},{2,1},{3,4},{4,3},{5,6},{6,5},{9,10},{10,9},{11,12},{12,11},... | collective-permute-start | bytes 245768 | tf_op jit(solution)/shard_map/ppermute | solution.py:491
  6.8 0.7 %collective-permute-start.5 = (f32[4,2,8,128]{3,2,1,0:T(8,128)S(1)}, f32[4,2,8,128]{3,2,1,0:T(8,128)S(1)}, u32[]{:S(2)}, u32[]{:S(2)}) collective-permute-start(f32[4,2,8,128]{3,2,1,0:T(8,128)S(1)} %get-tuple-element.36.xpack), channel_id=1, source_target_pairs={{128,256},{256,128},{129,257},{257,129},{130,258},{258,130},{131,2... | collective-permute-start | bytes 98312 | tf_op jit(solution)/shard_map/ppermute | solution.py:491
  7.5 6.3 %collective-permute-start.4 = (f32[4,2,8,128]{3,2,1,0:T(8,128)S(1)}, f32[4,2,8,128]{3,2,1,0:T(8,128)S(1)}, u32[]{:S(2)}, u32[]{:S(2)}) collective-permute-start(f32[4,2,8,128]{3,2,1,0:T(8,128)S(1)} %get-tuple-element.36.xpack), channel_id=1, source_target_pairs={{0,128},{128,0},{256,384},{384,256},{1,129},{129,1},{257,385},{385... | collective-permute-start | bytes 98312 | tf_op jit(solution)/shard_map/ppermute | solution.py:491
  13.8 0.0 collective-permute-done.2.y0
  13.8 6.8 %collective-permute-start.3 = (f32[4,16,128]{2,1,0:T(8,128)S(1)}, f32[4,16,128]{2,1,0:T(8,128)S(1)}, u32[]{:S(2)}, u32[]{:S(2)}) collective-permute-start(f32[4,16,128]{2,1,0:T(8,128)S(1)} %get-tuple-element.35.yface1), channel_id=1, source_target_pairs={{8,16},{16,8},{24,32},{32,24},{40,48},{48,40},{56,64},{64,56},{72,... | collective-permute-start | bytes 98312 | tf_op jit(solution)/shard_map/ppermute | solution.py:491
  20.7 1.6 %shard_map.87 = (f32[18,16,128]{2,1,0:T(8,128)S(1)}, f32[3,2,8,128]{3,2,1,0:T(8,128)S(1)}, f32[17,40,128]{2,1,0:T(8,128)S(1)}, f32[2,16,40,128]{3,2,1,0:T(8,128)...) custom-call(f32[3,16,40,128]{3,2,1,0:T(8,128)S(1)} %get-tuple-element.27.state, ...), custom_call_target="tpu_custom_call" | custom-call | flops 600000000 | bytes 2000000 | tf_op jit(solution)/shard_map/pallas_call | solution.py:497
  22.3 0.3 collective-permute-done.3.y1
  22.5 0.0 collective-permute-done.5.x1
  22.5 0.0 collective-permute-done.4.x0
  22.5 0.0 collective-permute-done.z0
  22.5 0.0 collective-permute-done.1.z1
  22.6 0.5 shard_map.88
  23.1 12.5 %all_to_all.10.parts = f32[8,40,128]{2,1,0:T(8,128)S(1)} all-to-all(f32[8,40,128]{2,1,0:T(8,128)S(1)} %get-tuple-element.38), channel_id=1, replica_groups=mesh['gx'=4,'gy'=16,'gz'=8] {'gz'}, dimensions={0} | all-to-all | bytes 327680 | tf_op jit(solution)/shard_map/all_to_all | solution.py:537
  35.6 1.9 %collective-permute-start.6 = (f32[32,128]{1,0:T(8,128)S(1)}, f32[32,128]{1,0:T(8,128)S(1)}, u32[]{:S(2)}, u32[]{:S(2)}) collective-permute-start(f32[32,128]{1,0:T(8,128)S(1)} %get-tuple-element.39), channel_id=1, source_target_pairs={{1,9},{3,131},{5,141},{8,0},{9,17},{11,139},{13,149},{14,134},{16,... | collective-permute-start | bytes 49160 | tf_op jit(solution)/shard_map/ppermute | solution.py:547
  37.5 2.9 %shard_map.90 = (f32[3,16,40,128]{3,2,1,0:T(8,128)S(1)}, f32[3,16,40,128]{3,2,1,0:T(8,128)S(1)}) custom-call(f32[18,16,128]{2,1,0:T(8,128)S(1)} %get-tuple-element.29.coef, f32[2,3,40,128]{3,2,1,0:T(8,128)S(1)} %get-tuple-element.41.znear, f32[2,3,16,128]{3,2,1,0:T(8,128)S(1)} %get-tuple-element.42.ynear, f32[3,2,8,128]{3,2,1,0:T(8,128)S(1)} %get-tuple-element.43.xnear, ...), custom_call_target="tpu_custom_call" | custom-call | flops 4000000000 | bytes 4000000 | tf_op jit(solution)/shard_map/pallas_call | solution.py:548
  40.4 2.0 %collective-permute-done.6.strip = f32[32,128]{1,0:T(8,128)S(1)} collective-permute-done((f32[32,128]{1,0:T(8,128)S(1)}, f32[32,128]{1,0:T(8,128)S(1)}, u32[]{:S(2)}, u32[]{:S(2)}) %collective-permute-start.6) | collective-permute-done | bytes 16416 | tf_op jit(solution)/shard_map/ppermute | solution.py:547
  42.4 9.2 %all_to_all.11.shares = f32[8,40,128]{2,1,0:T(8,128)S(1)} all-to-all(f32[8,40,128]{2,1,0:T(8,128)S(1)} %shard_map.91), channel_id=1, replica_groups=mesh['gx'=4,'gy'=16,'gz'=8] {'gz'}, dimensions={0} | all-to-all | bytes 327680 | tf_op jit(solution)/shard_map/all_to_all | solution.py:561
  51.6 2.0 %shard_map.92 = (f32[3,16,40,128]{3,2,1,0:T(8,128)}, f32[40,128]{1,0:T(8,128)}) custom-call(f32[8,40,128]{2,1,0:T(8,128)S(1)} %all_to_all.11.shares, f32[17,40,128]{2,1,0:T(8,128)S(1)} %get-tuple-element.46.layer_face, f32[2,16,40,128]{3,2,1,0:T(8,128)S(1)} %get-tuple-element.47.areal_face, f32[2,16,128]{2,1,0:T(8,128)S(1)} %get-tuple-element.44.yweight, ...), custom_call_target="tpu_custom_call" | custom-call | tf_op jit(solution)/shard_map/pallas_call | solution.py:563
  (2 shorter events, 0.0 us)
Async XLA Ops:
  2.2 11.6 %collective-permute-start.2 = (f32[4,16,128]{2,1,0:T(8,128)S(1)}, f32[4,16,128]{2,1,0:T(8,128)S(1)}, u32[]{:S(2)}, u32[]{:S(2)}) collective-permute-start(f32[4,16,128]{2,1,0:T(8,128)S(1)} %get-tuple-element.34.yface0), channel_id=1, source_target_pairs={{0,8},{8,0},{16,24},{24,16},{32,40},{40,32},{48,56},{56,48},{64,72... | collective-permute-start | bytes 98312 | tf_op jit(solution)/shard_map/ppermute | solution.py:491
  4.2 18.3 %collective-permute-start = (f32[4,40,128]{2,1,0:T(8,128)S(1)}, f32[4,40,128]{2,1,0:T(8,128)S(1)}, u32[]{:S(2)}, u32[]{:S(2)}) collective-permute-start(f32[4,40,128]{2,1,0:T(8,128)S(1)} %get-tuple-element.32.zface0), channel_id=1, source_target_pairs={{0,1},{1,0},{2,3},{3,2},{4,5},{5,4},{6,7},{7,6},{8,9},{9,8},{10,11... | collective-permute-start | bytes 245768 | tf_op jit(solution)/shard_map/ppermute | solution.py:491
  6.1 16.4 %collective-permute-start.1 = (f32[4,40,128]{2,1,0:T(8,128)S(1)}, f32[4,40,128]{2,1,0:T(8,128)S(1)}, u32[]{:S(2)}, u32[]{:S(2)}) collective-permute-start(f32[4,40,128]{2,1,0:T(8,128)S(1)} %get-tuple-element.33.zface1), channel_id=1, source_target_pairs={{1,2},{2,1},{3,4},{4,3},{5,6},{6,5},{9,10},{10,9},{11,12},{12,11},... | collective-permute-start | bytes 245768 | tf_op jit(solution)/shard_map/ppermute | solution.py:491
  6.8 15.7 %collective-permute-start.5 = (f32[4,2,8,128]{3,2,1,0:T(8,128)S(1)}, f32[4,2,8,128]{3,2,1,0:T(8,128)S(1)}, u32[]{:S(2)}, u32[]{:S(2)}) collective-permute-start(f32[4,2,8,128]{3,2,1,0:T(8,128)S(1)} %get-tuple-element.36.xpack), channel_id=1, source_target_pairs={{128,256},{256,128},{129,257},{257,129},{130,258},{258,130},{131,2... | collective-permute-start | bytes 98312 | tf_op jit(solution)/shard_map/ppermute | solution.py:491
  7.5 15.1 %collective-permute-start.4 = (f32[4,2,8,128]{3,2,1,0:T(8,128)S(1)}, f32[4,2,8,128]{3,2,1,0:T(8,128)S(1)}, u32[]{:S(2)}, u32[]{:S(2)}) collective-permute-start(f32[4,2,8,128]{3,2,1,0:T(8,128)S(1)} %get-tuple-element.36.xpack), channel_id=1, source_target_pairs={{0,128},{128,0},{256,384},{384,256},{1,129},{129,1},{257,385},{385... | collective-permute-start | bytes 98312 | tf_op jit(solution)/shard_map/ppermute | solution.py:491
  13.8 8.7 %collective-permute-start.3 = (f32[4,16,128]{2,1,0:T(8,128)S(1)}, f32[4,16,128]{2,1,0:T(8,128)S(1)}, u32[]{:S(2)}, u32[]{:S(2)}) collective-permute-start(f32[4,16,128]{2,1,0:T(8,128)S(1)} %get-tuple-element.35.yface1), channel_id=1, source_target_pairs={{8,16},{16,8},{24,32},{32,24},{40,48},{48,40},{56,64},{64,56},{72,... | collective-permute-start | bytes 98312 | tf_op jit(solution)/shard_map/ppermute | solution.py:491
  35.6 6.8 %collective-permute-start.6 = (f32[32,128]{1,0:T(8,128)S(1)}, f32[32,128]{1,0:T(8,128)S(1)}, u32[]{:S(2)}, u32[]{:S(2)}) collective-permute-start(f32[32,128]{1,0:T(8,128)S(1)} %get-tuple-element.39), channel_id=1, source_target_pairs={{1,9},{3,131},{5,141},{8,0},{9,17},{11,139},{13,149},{14,134},{16,... | collective-permute-start | bytes 49160 | tf_op jit(solution)/shard_map/ppermute | solution.py:547

commit v9 on v8

--- a/solution.py
+++ b/solution.py
@@ -56,7 +56,11 @@
     return lax.rem(lax.axis_index(axis), 2)
 
 
-def faces_kernel(state, perm, state_v, perm_v, zface0, zface1, yface0, yface1, xpack, perm_half, sems):
+def faces_kernel(
+    state, perm, facies, storage_table, coupling_table,
+    state_v, perm_v, coef, coef_lane, zface0, zface1, yface0, yface1, xpack,
+    perm_half, facies_s, storage_s, coupling_s, sems,
+):
     depth, height, width = perm.shape
     tiles, half = height // 8, depth // 2
     fetch = pltpu.make_async_copy(perm, perm_half, sems.at[0])
@@ -64,7 +68,15 @@
         pltpu.make_async_copy(state.at[:, pl.ds(z, PIECE)], state_v.at[:, pl.ds(z, PIECE)], sems.at[1 + z // PIECE])
         for z in range(0, depth, PIECE)
     ]
+    tables = [
+        pltpu.make_async_copy(source, target, sems.at[1 + depth // PIECE + n])
+        for n, (source, target) in enumerate(
+            ((facies, facies_s), (storage_table, storage_s), (coupling_table, coupling_s))
+        )
+    ]
     fetch.start()
+    for copy in tables:
+        copy.start()
     for piece in pieces:
         piece.start()
     z_high, y_high = parity("gz"), parity("gy")
@@ -85,6 +97,28 @@
     for z in range(depth):
         perm_v[z] = perm_half[z].astype(F32)
         pack(3, z, perm_half[z].astype(F32))
+    for copy in tables:
+        copy.wait()
+    row = row_index((depth, 128))
+    fids = jnp.zeros((depth, 128), jnp.int32)
+    fids_lane = [jnp.zeros((8, 128), jnp.int32) for _ in range(2)]
+    for z in range(depth):
+        fid = facies_s[z]
+        fids = jnp.where(row == z, fid, fids)
+        fids_lane[z // half] = jnp.where(lanes >= 2 * tiles * (z % half), fid, fids_lane[z // half])
+    kinds = storage_table.shape[1]
+    for which, table in enumerate((storage_s, coupling_s)):
+        for k in range(9):
+            rows_of = jnp.zeros((depth, 128), F32)
+            for f in range(kinds):
+                rows_of = jnp.where(fids == f, table[k // 3, f, k % 3], rows_of)
+            coef[9 * which + k] = rows_of
+    for k in range(3):
+        for h in range(2):
+            lane_of = jnp.zeros((8, 128), F32)
+            for f in range(kinds):
+                lane_of = jnp.where(fids_lane[h] == f, coupling_s[0, f, k], lane_of)
+            coef_lane[k, h] = lane_of
     for z in range(depth):
         if z % PIECE == 0:
             pieces[z // PIECE].wait()
@@ -99,9 +133,9 @@
 
 
 def inner_kernel(
-    state, perm, right, pore, facies, storage_table, coupling_table,
-    coef, coef_lane, layer_face, areal_face, acc, right_head, pore_v,
-    right_v, facies_s, storage_s, coupling_s, sems,
+    state, perm, coef, right, pore,
+    layer_face, areal_face, acc, right_v, right_head, pore_v,
+    sems,
 ):
     depth, height, width = perm.shape
     tiles, half = height // 8, depth // 2
@@ -109,12 +143,9 @@
         pltpu.make_async_copy(source, target, sems.at[n])
         for n, (source, target) in enumerate(
             (
-                (facies, facies_s),
-                (storage_table, storage_s),
-                (coupling_table, coupling_s),
                 (pore, pore_v),
                 (right.at[0], right_v),
-                (right.at[:, pl.ds(0, CHUNK)], right_head),
+                (right.at[pl.ds(1, 2), pl.ds(0, CHUNK)], right_head),
             )
         )
     ]
@@ -131,29 +162,7 @@
         areal_face[0, z] = ty
         areal_face[1, z] = tx
 
-    for copy in copies[:3]:
-        copy.wait()
-    lane, row = lane_index((8, 128)), row_index((depth, 128))
-    fids = jnp.zeros((depth, 128), jnp.int32)
-    fids_lane = [jnp.zeros((8, 128), jnp.int32) for _ in range(2)]
-    for z in range(depth):
-        fid = facies_s[z]
-        fids = jnp.where(row == z, fid, fids)
-        fids_lane[z // half] = jnp.where(lane >= 2 * tiles * (z % half), fid, fids_lane[z // half])
-    kinds = storage_table.shape[1]
-    for which, table in enumerate((storage_s, coupling_s)):
-        for k in range(9):
-            rows_of = jnp.zeros((depth, 128), F32)
-            for f in range(kinds):
-                rows_of = jnp.where(fids == f, table[k // 3, f, k % 3], rows_of)
-            coef[9 * which + k] = rows_of
-    for k in range(3):
-        for h in range(2):
-            lane_of = jnp.zeros((8, 128), F32)
-            for f in range(kinds):
-                lane_of = jnp.where(fids_lane[h] == f, coupling_s[0, f, k], lane_of)
-            coef_lane[k, h] = lane_of
-    for copy in copies[3:5]:
+    for copy in copies[:2]:
         copy.wait()
 
     for a in range(6):
@@ -176,7 +185,7 @@
         acc[3] += k0[0] * tx
         acc[4] += ty * (w - turn(w, -1, 0))
         acc[5] += tx * (w - turn(w, -1, 1))
-    copies[5].wait()
+    copies[2].wait()
 
 
 def outer_kernel(
@@ -305,7 +314,7 @@
 
 
 def cells_kernel(
-    coef, znear, ynear, xnear, yweight, xweight, order, layer_face, areal_face, state, right_head, pore, right_in,
+    coef, znear, ynear, xnear, yweight, xweight, order, layer_face, areal_face, state, right_first, right_head, pore, right_in,
     base, gain,
     right, sems,
 ):
@@ -317,7 +326,7 @@
     arrivals = {}
     for p in range(1, depth // CHUNK):
         here = pl.ds(p * CHUNK, CHUNK)
-        arrivals[p] = pltpu.make_async_copy(right_in.at[:, here], right.at[:, here], sems.at[p])
+        arrivals[p] = pltpu.make_async_copy(right_in.at[pl.ds(1, 2), here], right.at[:, here], sems.at[p])
         arrivals[p].start()
 
     def layer(z):
@@ -343,7 +352,8 @@
             nearby.append(moved)
         v = pore[z].astype(F32)
         source = [
-            (right_head if z < CHUNK else right)[r, z] + (k[r][0] * nearby[0] + k[r][1] * nearby[1] + k[r][2] * nearby[2]) for r in range(3)
+            (right_first[z] if r == 0 else (right_head if z < CHUNK else right)[r - 1, z])
+            + (k[r][0] * nearby[0] + k[r][1] * nearby[1] + k[r][2] * nearby[2]) for r in range(3)
         ]
         entries = [[v * m[r][c] + total * k[r][c] for c in range(3)] for r in range(3)]
 
@@ -475,14 +485,20 @@
     bf16 = jnp.bfloat16
     storage_table, coupling_table = storage_table.transpose(1, 0, 2), coupling_table.transpose(1, 0, 2)
 
-    state_v, perm_v, zface0, zface1, yface0, yface1, xpack = call(
+    state_v, perm_v, coef, coef_lane, zface0, zface1, yface0, yface1, xpack = call(
         faces_kernel,
-        [shape_of(3, *block), shape_of(*block)]
+        [shape_of(3, *block), shape_of(*block), shape_of(18, depth, 128), shape_of(3, 2, 8, 128)]
         + [shape_of(4, height, width)] * 2 + [shape_of(4, depth, width)] * 2 + [shape_of(4, 2, 8, 128)],
-        hbm(2),
-        vmem(7),
-        [pltpu.VMEM(block, bf16), pltpu.SemaphoreType.DMA((1 + depth // PIECE,))],
-    )(*in_hbm(state, permeability))
+        hbm(5),
+        vmem(9),
+        [
+            pltpu.VMEM(block, bf16),
+            pltpu.SMEM(facies.shape, jnp.int32),
+            pltpu.SMEM(storage_table.shape, F32),
+            pltpu.SMEM(coupling_table.shape, F32),
+            pltpu.SemaphoreType.DMA((4 + depth // PIECE,)),
+        ],
+    )(*in_hbm(state, permeability, facies, storage_table, coupling_table))
 
     def exchange(face, axis, odd):
         pairs = []
@@ -494,29 +510,22 @@
     for axis, first, second in (("gz", zface0, zface1), ("gy", yface0, yface1), ("gx", xpack, xpack)):
         received += [exchange(first, axis, 0), exchange(second, axis, 1)]
 
-    coef, coef_lane, layer_face, areal_face, acc, right_head, pore_v = call(
+    layer_face, areal_face, acc, right_first, right_head, pore_v = call(
         inner_kernel,
         [
-            shape_of(18, depth, 128),
-            shape_of(3, 2, 8, 128),
             shape_of(depth + 1, height, width),
             shape_of(2, *block),
             shape_of(6, height, width),
-            shape_of(3, CHUNK, height, width),
+            shape_of(*block),
+            shape_of(2, CHUNK, height, width),
             jax.ShapeDtypeStruct(block, bf16),
         ],
-        vmem(2) + hbm(5),
-        vmem(7),
-        [
-            pltpu.VMEM(block, F32),
-            pltpu.SMEM(facies.shape, jnp.int32),
-            pltpu.SMEM(storage_table.shape, F32),
-            pltpu.SMEM(coupling_table.shape, F32),
-            pltpu.SemaphoreType.DMA((6,)),
-        ],
+        vmem(3) + hbm(2),
+        vmem(6),
+        [pltpu.SemaphoreType.DMA((3,))],
         flops=6 * 10**8,
         moved=2 * 10**6,
-    )(state_v, perm_v, *in_hbm(right_side, pore_volume, facies, storage_table, coupling_table))
+    )(state_v, perm_v, coef, *in_hbm(right_side, pore_volume))
 
     layer_face, znear, ynear, xnear, yweight, xweight, message = call(
         outer_kernel,
@@ -548,14 +557,14 @@
     base, gain = call(
         cells_kernel,
         [shape_of(3, *block)] * 2,
-        vmem(12) + hbm(1),
+        vmem(13) + hbm(1),
         vmem(2),
-        [pltpu.VMEM((3, *block), F32), pltpu.SemaphoreType.DMA((depth // CHUNK,))],
+        [pltpu.VMEM((2, *block), F32), pltpu.SemaphoreType.DMA((depth // CHUNK,))],
         flops=4 * 10**9,
         moved=4 * 10**6,
     )(
         coef, znear, ynear, xnear, yweight, xweight, share, layer_face, areal_face, state_v,
-        right_head, pore_v, *in_hbm(right_side),
+        right_first, right_head, pore_v, *in_hbm(right_side),
     )
     copies = call(merge_kernel, shape_of(columns, 40, 128), vmem(3), vmem(1)[0])(strip, share, base)
     shares = lax.all_to_all(copies, "gz", 0, 0)

time: 54 us -> 54.2 us (level)
  the two profiles are of different devices: /device:TPU:96 before, /device:TPU:104 now
where the time goes in v9:
time: 54.2 us; the launch traced here: 53.8 us
  blocking collectives  22.1 us (41%)
  starting transfers between devices  20 us (37%)
  Pallas kernels  8.61 us (16%)
  waiting for transfers between devices  2.29 us (4%)
  between operations  0.75 us (1%)
    ppermute x6, starting transfers between devices, exchange(): return lax.ppermute(face, axis, pairs)  18.1 us
    all_to_all x1, blocking collectives, per_device(): parts = lax.all_to_all(message, 'gz', 0, 0)  12.5 us
    all_to_all x1, blocking collectives, per_device(): shares = lax.all_to_all(copies, 'gz', 0, 0)  9.63 us
    pallas_call x1, Pallas kernels, per_device(): call(cells_kernel, [shape_of(3, *block)] * 2, vmem(13) + hbm(1), vmem(2),...  2.92 us
    pallas_call x1, Pallas kernels, per_device(): call(sweep_kernel, [pltpu.HBM((3, *block), F32), pltpu.HBM((height, width...  2.02 us
    ppermute x1, waiting for transfers between devices, per_device(): strip = lax.ppermute(strip, ('gx', 'gy', 'gz'), pairs)  1.99 us
    ppermute x1, starting transfers between devices, per_device(): strip = lax.ppermute(strip, ('gx', 'gy', 'gz'), pairs)  1.92 us
    pallas_call x1, Pallas kernels, per_device(): call(inner_kernel, [shape_of(depth + 1, height, width), shape_of(2, *bloc...  1.58 us
  transfers between devices with their start and end apart: 7, of which 2 were waited for; matrix products, arithmetic and copies ran while one was open for 0% of the time, Pallas kernels for 8%

profile of v9, /device:TPU:104, one launch (start us, length us, event | category | flops | bytes accessed | tf_op | source)
XLA Modules:
  0.0 53.8 jit_solution(874118296785898841)
XLA Ops:
  0.6 1.6 %shard_map.86 = (f32[3,16,40,128]{3,2,1,0:T(8,128)S(1)}, f32[16,40,128]{2,1,0:T(8,128)S(1)}, f32[18,16,128]{2,1,0:T(8,128)S(1)}, f32[3,2,8,128]{3,2,1,0:T(8,128)...) custom-call(f32[3,16,40,128]{3,2,1,0:T(8,128)} %state.1, ...), custom_call_target="tpu_custom_call" | custom-call | tf_op jit(solution)/shard_map/pallas_call | solution.py:488
  2.2 2.0 %collective-permute-start.2 = (f32[4,16,128]{2,1,0:T(8,128)S(1)}, f32[4,16,128]{2,1,0:T(8,128)S(1)}, u32[]{:S(2)}, u32[]{:S(2)}) collective-permute-start(f32[4,16,128]{2,1,0:T(8,128)S(1)} %get-tuple-element.35.yface0), channel_id=1, source_target_pairs={{0,8},{8,0},{16,24},{24,16},{32,40},{40,32},{48,56},{56,48},{64,72... | collective-permute-start | bytes 98312 | tf_op jit(solution)/shard_map/ppermute | solution.py:507
  4.2 1.9 %collective-permute-start = (f32[4,40,128]{2,1,0:T(8,128)S(1)}, f32[4,40,128]{2,1,0:T(8,128)S(1)}, u32[]{:S(2)}, u32[]{:S(2)}) collective-permute-start(f32[4,40,128]{2,1,0:T(8,128)S(1)} %get-tuple-element.33.zface0), channel_id=1, source_target_pairs={{0,1},{1,0},{2,3},{3,2},{4,5},{5,4},{6,7},{7,6},{8,9},{9,8},{10,11... | collective-permute-start | bytes 245768 | tf_op jit(solution)/shard_map/ppermute | solution.py:507
  6.2 0.7 %collective-permute-start.1 = (f32[4,40,128]{2,1,0:T(8,128)S(1)}, f32[4,40,128]{2,1,0:T(8,128)S(1)}, u32[]{:S(2)}, u32[]{:S(2)}) collective-permute-start(f32[4,40,128]{2,1,0:T(8,128)S(1)} %get-tuple-element.34.zface1), channel_id=1, source_target_pairs={{1,2},{2,1},{3,4},{4,3},{5,6},{6,5},{9,10},{10,9},{11,12},{12,11},... | collective-permute-start | bytes 245768 | tf_op jit(solution)/shard_map/ppermute | solution.py:507
  6.8 2.4 %collective-permute-start.4 = (f32[4,2,8,128]{3,2,1,0:T(8,128)S(1)}, f32[4,2,8,128]{3,2,1,0:T(8,128)S(1)}, u32[]{:S(2)}, u32[]{:S(2)}) collective-permute-start(f32[4,2,8,128]{3,2,1,0:T(8,128)S(1)} %get-tuple-element.37.xpack), channel_id=1, source_target_pairs={{0,128},{128,0},{256,384},{384,256},{1,129},{129,1},{257,385},{385... | collective-permute-start | bytes 98312 | tf_op jit(solution)/shard_map/ppermute | solution.py:507
  9.2 4.3 %collective-permute-start.5 = (f32[4,2,8,128]{3,2,1,0:T(8,128)S(1)}, f32[4,2,8,128]{3,2,1,0:T(8,128)S(1)}, u32[]{:S(2)}, u32[]{:S(2)}) collective-permute-start(f32[4,2,8,128]{3,2,1,0:T(8,128)S(1)} %get-tuple-element.37.xpack), channel_id=1, source_target_pairs={{128,256},{256,128},{129,257},{257,129},{130,258},{258,130},{131,2... | collective-permute-start | bytes 98312 | tf_op jit(solution)/shard_map/ppermute | solution.py:507
  13.5 0.0 collective-permute-done.2.y0
  13.5 6.8 %collective-permute-start.3 = (f32[4,16,128]{2,1,0:T(8,128)S(1)}, f32[4,16,128]{2,1,0:T(8,128)S(1)}, u32[]{:S(2)}, u32[]{:S(2)}) collective-permute-start(f32[4,16,128]{2,1,0:T(8,128)S(1)} %get-tuple-element.36.yface1), channel_id=1, source_target_pairs={{8,16},{16,8},{24,32},{32,24},{40,48},{48,40},{56,64},{64,56},{72,... | collective-permute-start | bytes 98312 | tf_op jit(solution)/shard_map/ppermute | solution.py:507
  20.4 1.6 %shard_map.87 = (f32[17,40,128]{2,1,0:T(8,128)S(1)}, f32[2,16,40,128]{3,2,1,0:T(8,128)S(1)}, f32[6,40,128]{2,1,0:T(8,128)S(1)}, f32[16,40,128]{2,1,0:T(8,128)S(1...) custom-call(f32[3,16,40,128]{3,2,1,0:T(8,128)S(1)} %get-tuple-element.30.state, ...), custom_call_target="tpu_custom_call" | custom-call | flops 600000000 | bytes 2000000 | tf_op jit(solution)/shard_map/pallas_call | solution.py:513
  22.0 0.3 collective-permute-done.3.y1
  22.3 0.0 collective-permute-done.4.x0
  22.3 0.0 collective-permute-done.5.x1
  22.3 0.0 collective-permute-done.z0
  22.3 0.0 collective-permute-done.1.z1
  22.3 0.5 shard_map.88
  22.8 12.5 %all_to_all.10.parts = f32[8,40,128]{2,1,0:T(8,128)S(1)} all-to-all(f32[8,40,128]{2,1,0:T(8,128)S(1)} %get-tuple-element.39), channel_id=1, replica_groups=mesh['gx'=4,'gy'=16,'gz'=8] {'gz'}, dimensions={0} | all-to-all | bytes 327680 | tf_op jit(solution)/shard_map/all_to_all | solution.py:546
  35.3 1.9 %collective-permute-start.6 = (f32[32,128]{1,0:T(8,128)S(1)}, f32[32,128]{1,0:T(8,128)S(1)}, u32[]{:S(2)}, u32[]{:S(2)}) collective-permute-start(f32[32,128]{1,0:T(8,128)S(1)} %get-tuple-element.40), channel_id=1, source_target_pairs={{1,9},{3,131},{5,141},{8,0},{9,17},{11,139},{13,149},{14,134},{16,... | collective-permute-start | bytes 49160 | tf_op jit(solution)/shard_map/ppermute | solution.py:556
  37.2 2.9 %shard_map.90 = (f32[3,16,40,128]{3,2,1,0:T(8,128)S(1)}, f32[3,16,40,128]{3,2,1,0:T(8,128)S(1)}) custom-call(f32[18,16,128]{2,1,0:T(8,128)S(1)} %get-tuple-element.28.coef, f32[2,3,40,128]{3,2,1,0:T(8,128)S(1)} %get-tuple-element.42.znear, f32[2,3,16,128]{3,2,1,0:T(8,128)S(1)} %get-tuple-element.43.ynear, f32[3,2,8,128]{3,2,1,0:T(8,128)S(1)} %get-tuple-element.44.xnear, ...), custom_call_target="tpu_custom_call" | custom-call | flops 4000000000 | bytes 4000000 | tf_op jit(solution)/shard_map/pallas_call | solution.py:557
  40.2 2.0 %collective-permute-done.6.strip = f32[32,128]{1,0:T(8,128)S(1)} collective-permute-done((f32[32,128]{1,0:T(8,128)S(1)}, f32[32,128]{1,0:T(8,128)S(1)}, u32[]{:S(2)}, u32[]{:S(2)}) %collective-permute-start.6) | collective-permute-done | bytes 16416 | tf_op jit(solution)/shard_map/ppermute | solution.py:556
  42.2 9.6 %all_to_all.11.shares = f32[8,40,128]{2,1,0:T(8,128)S(1)} all-to-all(f32[8,40,128]{2,1,0:T(8,128)S(1)} %shard_map.91), channel_id=1, replica_groups=mesh['gx'=4,'gy'=16,'gz'=8] {'gz'}, dimensions={0} | all-to-all | bytes 327680 | tf_op jit(solution)/shard_map/all_to_all | solution.py:570
  51.8 2.0 %shard_map.92 = (f32[3,16,40,128]{3,2,1,0:T(8,128)}, f32[40,128]{1,0:T(8,128)}) custom-call(f32[8,40,128]{2,1,0:T(8,128)S(1)} %all_to_all.11.shares, f32[17,40,128]{2,1,0:T(8,128)S(1)} %get-tuple-element.47.layer_face, f32[2,16,40,128]{3,2,1,0:T(8,128)S(1)} %get-tuple-element.48.areal_face, f32[2,16,128]{2,1,0:T(8,128)S(1)} %get-tuple-element.45.yweight, ...), custom_call_target="tpu_custom_call" | custom-call | tf_op jit(solution)/shard_map/pallas_call | solution.py:572
  (2 shorter events, 0.0 us)
Async XLA Ops:
  2.2 11.3 %collective-permute-start.2 = (f32[4,16,128]{2,1,0:T(8,128)S(1)}, f32[4,16,128]{2,1,0:T(8,128)S(1)}, u32[]{:S(2)}, u32[]{:S(2)}) collective-permute-start(f32[4,16,128]{2,1,0:T(8,128)S(1)} %get-tuple-element.35.yface0), channel_id=1, source_target_pairs={{0,8},{8,0},{16,24},{24,16},{32,40},{40,32},{48,56},{56,48},{64,72... | collective-permute-start | bytes 98312 | tf_op jit(solution)/shard_map/ppermute | solution.py:507
  4.2 18.0 %collective-permute-start = (f32[4,40,128]{2,1,0:T(8,128)S(1)}, f32[4,40,128]{2,1,0:T(8,128)S(1)}, u32[]{:S(2)}, u32[]{:S(2)}) collective-permute-start(f32[4,40,128]{2,1,0:T(8,128)S(1)} %get-tuple-element.33.zface0), channel_id=1, source_target_pairs={{0,1},{1,0},{2,3},{3,2},{4,5},{5,4},{6,7},{7,6},{8,9},{9,8},{10,11... | collective-permute-start | bytes 245768 | tf_op jit(solution)/shard_map/ppermute | solution.py:507
  6.2 16.1 %collective-permute-start.1 = (f32[4,40,128]{2,1,0:T(8,128)S(1)}, f32[4,40,128]{2,1,0:T(8,128)S(1)}, u32[]{:S(2)}, u32[]{:S(2)}) collective-permute-start(f32[4,40,128]{2,1,0:T(8,128)S(1)} %get-tuple-element.34.zface1), channel_id=1, source_target_pairs={{1,2},{2,1},{3,4},{4,3},{5,6},{6,5},{9,10},{10,9},{11,12},{12,11},... | collective-permute-start | bytes 245768 | tf_op jit(solution)/shard_map/ppermute | solution.py:507
  6.8 15.4 %collective-permute-start.4 = (f32[4,2,8,128]{3,2,1,0:T(8,128)S(1)}, f32[4,2,8,128]{3,2,1,0:T(8,128)S(1)}, u32[]{:S(2)}, u32[]{:S(2)}) collective-permute-start(f32[4,2,8,128]{3,2,1,0:T(8,128)S(1)} %get-tuple-element.37.xpack), channel_id=1, source_target_pairs={{0,128},{128,0},{256,384},{384,256},{1,129},{129,1},{257,385},{385... | collective-permute-start | bytes 98312 | tf_op jit(solution)/shard_map/ppermute | solution.py:507
  9.2 13.1 %collective-permute-start.5 = (f32[4,2,8,128]{3,2,1,0:T(8,128)S(1)}, f32[4,2,8,128]{3,2,1,0:T(8,128)S(1)}, u32[]{:S(2)}, u32[]{:S(2)}) collective-permute-start(f32[4,2,8,128]{3,2,1,0:T(8,128)S(1)} %get-tuple-element.37.xpack), channel_id=1, source_target_pairs={{128,256},{256,128},{129,257},{257,129},{130,258},{258,130},{131,2... | collective-permute-start | bytes 98312 | tf_op jit(solution)/shard_map/ppermute | solution.py:507
  13.5 8.7 %collective-permute-start.3 = (f32[4,16,128]{2,1,0:T(8,128)S(1)}, f32[4,16,128]{2,1,0:T(8,128)S(1)}, u32[]{:S(2)}, u32[]{:S(2)}) collective-permute-start(f32[4,16,128]{2,1,0:T(8,128)S(1)} %get-tuple-element.36.yface1), channel_id=1, source_target_pairs={{8,16},{16,8},{24,32},{32,24},{40,48},{48,40},{56,64},{64,56},{72,... | collective-permute-start | bytes 98312 | tf_op jit(solution)/shard_map/ppermute | solution.py:507
  35.3 6.8 %collective-permute-start.6 = (f32[32,128]{1,0:T(8,128)S(1)}, f32[32,128]{1,0:T(8,128)S(1)}, u32[]{:S(2)}, u32[]{:S(2)}) collective-permute-start(f32[32,128]{1,0:T(8,128)S(1)} %get-tuple-element.40), channel_id=1, source_target_pairs={{1,9},{3,131},{5,141},{8,0},{9,17},{11,139},{13,149},{14,134},{16,... | collective-permute-start | bytes 49160 | tf_op jit(solution)/shard_map/ppermute | solution.py:556
